TPU v7x, 128 devices: a whole 4x4x4 slice. The times are simulated.
128 devices in a mesh: seq: 8 (over z_hi, y), fsdp: 16 (over z_lo, x, core).
Axes of the slice: x: 4, y: 4, z: 4 (z_hi: 2, z_lo: 2; z = z_hi * 2 + z_lo), core: 2. Of those that a mesh axis runs over, the one named last changes fastest.
Arguments:
- tokens: bfloat16 [16, 1024, 2048], P('fsdp', 'seq'), may hold values from -6 to 6
- segment_ids: int32 [16, 1024], P('fsdp'), may hold values from 0 to 1, as said below
- query_weight: bfloat16 [2048, 2048], P('fsdp'), may hold values from -0.25 to 0.25
- key_matrix: bfloat16 [2048, 512], P('fsdp'), may hold values from -0.125 to 0.125
- value_matrix: bfloat16 [2048, 512], P('fsdp'), may hold values from -0.125 to 0.125
- output_weight: bfloat16 [2048, 2048], P('fsdp'), may hold values from -0.75 to 0.75
- gate_weight: bfloat16 [2048, 8192], P('fsdp'), may hold values from -0.125 to 0.125
- up_weight: bfloat16 [2048, 8192], P('fsdp'), may hold values from -0.125 to 0.125
- down_weight: bfloat16 [8192, 2048], P('fsdp'), may hold values from -0.0625 to 0.0625
- attention_gain: bfloat16 [2048], P('fsdp'), may hold values from 0.099609375 to 1.8984375
- feed_gain: bfloat16 [2048], P('fsdp'), may hold values from 0.099609375 to 1.8984375
- cotangent: bfloat16 [16, 1024, 2048], P('fsdp', 'seq'), may hold values from -6 to 6
Outputs:
- layer_out: bfloat16 [16, 1024, 2048], P('fsdp', 'seq')
- grad_tokens: bfloat16 [16, 1024, 2048], P('fsdp', 'seq')
- grad_query: float32 [2048, 2048], P('fsdp')
- grad_key: float32 [2048, 512], P('fsdp')
- grad_value: float32 [2048, 512], P('fsdp')
- grad_output: float32 [2048, 2048], P('fsdp')
- grad_gate: float32 [2048, 8192], P('fsdp')
- grad_up: float32 [2048, 8192], P('fsdp')
- grad_down: float32 [8192, 2048], P('fsdp')
- grad_attention_gain: float32 [2048], P('fsdp')
- grad_feed_gain: float32 [2048], P('fsdp')
Inputs may be any that keep to these rules, and one draw needn't show every extreme that they name: `segment_ids`: each sequence holds two documents, 0 then 1; document 0 ends within the last 128 tokens.
All inputs are finite; a program needn't handle non-finite values.
Results may differ from a plain program's by a relative error of at most 0.025.
Values may be sent and summed in bfloat16 or wider, within the bound.
A program may use at most 448 MiB of HBM per device.

v0:
```python
import math

import jax
import jax.numpy as jnp
from jax import lax
from jax.sharding import PartitionSpec as P

QUERY_HEADS = 32
KEY_VALUE_HEADS = 8
HEAD_SIZE = 64
BLK = 512


EPS = 1e-05
ROPE_BASE = 500000.0
NEG = -1e30


def rope_freqs(head_dim):
    half_dim = head_dim // 2
    table = []
    for index in range(half_dim):
        inverse = 1.0 / ROPE_BASE ** (index * 2.0 / head_dim)
        wavelen = 2.0 * math.pi / inverse
        blend = (8192.0 / wavelen - 1.0) / 3.0
        mixed = (1.0 - blend) * inverse / 32.0 + blend * inverse
        entry = inverse if wavelen < 2048.0 else inverse / 32.0 if wavelen > 8192.0 else mixed
        table.append(entry)
    return jnp.asarray(table, dtype=jnp.float32)


def positions_of(segment_row):
    indices = jnp.arange(segment_row.shape[0], dtype=jnp.int32)
    begins = jnp.concatenate(
        [jnp.ones((1,), dtype=jnp.int32), (segment_row[1:] != segment_row[:-1]).astype(jnp.int32)]
    )
    starts_at = lax.cummax(jnp.where(begins > 0, indices, 0), axis=0)
    return indices - starts_at


def angles_of(segment_row, head_dim):
    positions = positions_of(segment_row)
    phase = positions.astype(jnp.float32)[:, None] * rope_freqs(head_dim)[None, :]
    return (jnp.cos(phase), jnp.sin(phase))


def apply_rotation(values_in, cosine_table, sine_table):
    half_dim = values_in.shape[-1] // 2
    first_half = values_in[..., :half_dim]
    second_half = values_in[..., half_dim:]
    return jnp.concatenate(
        [
            first_half * cosine_table - second_half * sine_table,
            second_half * cosine_table + first_half * sine_table,
        ],
        axis=-1,
    )


def unrotate(values_in, cosine_table, sine_table):
    half_dim = values_in.shape[-1] // 2
    first_half = values_in[..., :half_dim]
    second_half = values_in[..., half_dim:]
    return jnp.concatenate(
        [
            first_half * cosine_table + second_half * sine_table,
            second_half * cosine_table - first_half * sine_table,
        ],
        axis=-1,
    )


def norm_back(grad_in, gain, factor, normed):
    weighted = grad_in * gain
    return factor * (weighted - normed * jnp.mean(weighted * normed, axis=-1, keepdims=True))


def allowed_mask(offset, segment_row):
    token_length = segment_row.shape[0]
    key_index = jnp.arange(token_length, dtype=jnp.int32)
    query_index = offset + jnp.arange(BLK, dtype=jnp.int32)
    query_segment = lax.dynamic_slice_in_dim(segment_row, offset, BLK, 0)
    return (key_index[None, :] <= query_index[:, None]) & (
        segment_row[None, :] == query_segment[:, None]
    )


def contract_rows(left, right):
    return jnp.einsum("ta,tb->ab", left, right, preferred_element_type=jnp.float32)


def matmul(left, right):
    return jnp.dot(left, right, preferred_element_type=jnp.float32)


def shards(
    tokens,
    segment_ids,
    query_weight,
    key_matrix,
    value_matrix,
    output_weight,
    gate_weight,
    up_weight,
    down_weight,
    attention_gain,
    feed_gain,
    cotangent,
):
    inputs = tokens[0].astype(jnp.float32)
    segment_row = segment_ids[0]
    token_length = segment_row.shape[0]
    group_width = QUERY_HEADS // KEY_VALUE_HEADS
    query_all, key_all, value_all, output_all, gain_one = (
        lax.all_gather(query_weight, "fsdp", axis=0, tiled=True),
        lax.all_gather(key_matrix, "fsdp", axis=0, tiled=True),
        lax.all_gather(value_matrix, "fsdp", axis=0, tiled=True),
        lax.all_gather(output_weight, "fsdp", axis=0, tiled=True),
        lax.all_gather(attention_gain, "fsdp", axis=0, tiled=True),
    )
    factor_one = lax.rsqrt(jnp.mean(inputs * inputs, axis=-1, keepdims=True) + EPS)
    normed_one = inputs * factor_one
    hidden_one = (normed_one * gain_one.astype(jnp.float32)).astype(jnp.bfloat16)
    query_rows_in = matmul(hidden_one, query_all).astype(jnp.bfloat16)
    projected_keys = matmul(hidden_one, key_all).astype(jnp.bfloat16)
    projected_values = matmul(hidden_one, value_all).astype(jnp.bfloat16)
    query_heads, kv_heads = (
        lax.all_to_all(query_rows_in[:, None, :], "seq", split_axis=2, concat_axis=0, tiled=True),
        lax.all_to_all(
            jnp.stack([projected_keys, projected_values], axis=1),
            "seq",
            split_axis=2,
            concat_axis=0,
            tiled=True,
        ),
    )
    local_kv = kv_heads.shape[2] // HEAD_SIZE
    cosine_table, sine_table = angles_of(segment_row, HEAD_SIZE)
    cos_query, sin_query = (cosine_table[:, None, None, :], sine_table[:, None, None, :])
    cos_key, sin_key = (cosine_table[:, None, :], sine_table[:, None, :])
    rotated_queries = apply_rotation(
        query_heads[:, 0]
        .reshape(token_length, local_kv, group_width, HEAD_SIZE)
        .astype(jnp.float32),
        cos_query,
        sin_query,
    ).astype(jnp.bfloat16)
    rotated_keys = apply_rotation(
        kv_heads[:, 0].reshape(token_length, local_kv, HEAD_SIZE).astype(jnp.float32),
        cos_key,
        sin_key,
    ).astype(jnp.bfloat16)
    heads_of_values = kv_heads[:, 1].reshape(token_length, local_kv, HEAD_SIZE)
    offsets = jnp.arange(token_length // BLK, dtype=jnp.int32) * BLK

    def forward_block(offset):
        query_rows = lax.dynamic_slice_in_dim(rotated_queries, offset, BLK, 0)
        scores = (
            jnp.einsum(
                "qkgd,skd->kgqs", query_rows, rotated_keys, preferred_element_type=jnp.float32
            )
            * 0.125
        )
        masked = jnp.where(allowed_mask(offset, segment_row), scores, NEG)
        highest = jnp.max(masked, axis=-1, keepdims=True)
        weights = jnp.exp(masked - highest)
        total = jnp.sum(weights, axis=-1, keepdims=True)
        probs = (weights / total).astype(jnp.bfloat16)
        block_out = jnp.einsum(
            "kgqs,skd->qkgd", probs, heads_of_values, preferred_element_type=jnp.float32
        )
        return (block_out.astype(jnp.bfloat16), (highest + jnp.log(total))[..., 0])

    out_blocks, lse_blocks = lax.map(forward_block, offsets)
    attended_heads = out_blocks.reshape(token_length, -1)
    attended = lax.all_to_all(attended_heads, "seq", split_axis=0, concat_axis=1, tiled=True)
    middle = inputs + matmul(attended, output_all)
    gate_all, up_all, down_all, gain_two = (
        lax.all_gather(gate_weight, "fsdp", axis=0, tiled=True),
        lax.all_gather(up_weight, "fsdp", axis=0, tiled=True),
        lax.all_gather(down_weight, "fsdp", axis=0, tiled=True),
        lax.all_gather(feed_gain, "fsdp", axis=0, tiled=True),
    )
    factor_two = lax.rsqrt(jnp.mean(middle * middle, axis=-1, keepdims=True) + EPS)
    normed_two = middle * factor_two
    hidden_two = (normed_two * gain_two.astype(jnp.float32)).astype(jnp.bfloat16)
    gate = matmul(hidden_two, gate_all)
    up_proj = matmul(hidden_two, up_all)
    sig_gate = jax.nn.sigmoid(gate)
    silu_gate = gate * sig_gate
    act = (silu_gate * up_proj).astype(jnp.bfloat16)
    layer_out = (middle + matmul(act, down_all)).astype(jnp.bfloat16)
    grad_out = cotangent[0]
    grad_out_f = grad_out.astype(jnp.float32)
    gate_back, up_back, down_back, gain_two_back = (
        lax.all_gather(gate_weight, "fsdp", axis=0, tiled=True),
        lax.all_gather(up_weight, "fsdp", axis=0, tiled=True),
        lax.all_gather(down_weight, "fsdp", axis=0, tiled=True),
        lax.all_gather(feed_gain, "fsdp", axis=0, tiled=True),
    )
    down_share = lax.psum_scatter(
        contract_rows(act, grad_out).astype(jnp.bfloat16), "fsdp", scatter_dimension=0, tiled=True
    )
    grad_act = matmul(grad_out, down_back.T)
    grad_gate = (grad_act * up_proj * (sig_gate * (1.0 + gate * (1.0 - sig_gate)))).astype(
        jnp.bfloat16
    )
    grad_up = (grad_act * silu_gate).astype(jnp.bfloat16)
    gate_up_grads = jnp.concatenate([grad_gate, grad_up], axis=1)
    hidden_cols = hidden_two
    mlp_share = lax.psum_scatter(
        contract_rows(hidden_cols, gate_up_grads).astype(jnp.bfloat16),
        "fsdp",
        scatter_dimension=0,
        tiled=True,
    )
    grad_hidden_two = matmul(grad_gate, gate_back.T) + matmul(grad_up, up_back.T)
    gain_two_f = gain_two_back.astype(jnp.float32)
    grad_gain_two = jnp.sum(grad_hidden_two * normed_two, axis=0)
    grad_middle = grad_out_f + norm_back(grad_hidden_two, gain_two_f, factor_two, normed_two)
    grad_branch = grad_middle.astype(jnp.bfloat16)
    query_back, key_back, value_back, output_back, gain_one_back = (
        lax.all_gather(query_weight, "fsdp", axis=0, tiled=True),
        lax.all_gather(key_matrix, "fsdp", axis=0, tiled=True),
        lax.all_gather(value_matrix, "fsdp", axis=0, tiled=True),
        lax.all_gather(output_weight, "fsdp", axis=0, tiled=True),
        lax.all_gather(attention_gain, "fsdp", axis=0, tiled=True),
    )
    grad_attended = matmul(grad_branch, output_back.T).astype(jnp.bfloat16)
    grad_heads = lax.all_to_all(
        grad_attended, "seq", split_axis=1, concat_axis=0, tiled=True
    ).reshape(token_length, local_kv, group_width, HEAD_SIZE)

    def backward_block(carry, block_data):
        key_grad, value_grad = carry
        offset, block_lse = block_data
        query_rows = lax.dynamic_slice_in_dim(rotated_queries, offset, BLK, 0)
        grad_rows = lax.dynamic_slice_in_dim(grad_heads, offset, BLK, 0)
        scores = (
            jnp.einsum(
                "qkgd,skd->kgqs", query_rows, rotated_keys, preferred_element_type=jnp.float32
            )
            * 0.125
        )
        probs = jnp.where(
            allowed_mask(offset, segment_row), jnp.exp(scores - block_lse[..., None]), 0.0
        )
        grad_probs = jnp.einsum(
            "qkgd,skd->kgqs", grad_rows, heads_of_values, preferred_element_type=jnp.float32
        )
        row_dot = jnp.sum(probs * grad_probs, axis=-1, keepdims=True)
        grad_scores = (probs * (grad_probs - row_dot) * 0.125).astype(jnp.bfloat16)
        query_grad = jnp.einsum(
            "kgqs,skd->qkgd", grad_scores, rotated_keys, preferred_element_type=jnp.float32
        )
        key_grad = key_grad + jnp.einsum(
            "kgqs,qkgd->skd", grad_scores, query_rows, preferred_element_type=jnp.float32
        )
        value_grad = value_grad + jnp.einsum(
            "kgqs,qkgd->skd",
            probs.astype(jnp.bfloat16),
            grad_rows,
            preferred_element_type=jnp.float32,
        )
        return ((key_grad, value_grad), query_grad)

    zeros_kv = jnp.zeros((token_length, local_kv, HEAD_SIZE), jnp.float32)
    (key_grad_all, value_grad_all), query_grad_blocks = lax.scan(
        backward_block, (zeros_kv, zeros_kv), (offsets, lse_blocks)
    )
    query_send = (
        unrotate(
            query_grad_blocks.reshape(token_length, local_kv, group_width, HEAD_SIZE),
            cos_query,
            sin_query,
        )
        .astype(jnp.bfloat16)
        .reshape(token_length, 1, -1)
    )
    key_send = (
        unrotate(key_grad_all, cos_key, sin_key).astype(jnp.bfloat16).reshape(token_length, -1)
    )
    value_send = value_grad_all.astype(jnp.bfloat16).reshape(token_length, -1)
    query_return, kv_return = (
        lax.all_to_all(query_send, "seq", split_axis=0, concat_axis=2, tiled=True),
        lax.all_to_all(
            jnp.stack([key_send, value_send], axis=1),
            "seq",
            split_axis=0,
            concat_axis=2,
            tiled=True,
        ),
    )
    grad_queries = query_return[:, 0]
    grad_keys = kv_return[:, 0]
    grad_values = kv_return[:, 1]
    proj_grads = jnp.concatenate([grad_queries, grad_keys, grad_values], axis=1)
    hidden_cols = hidden_one
    attn_share = lax.psum_scatter(
        jnp.concatenate(
            [contract_rows(hidden_cols, proj_grads), contract_rows(attended, grad_branch)], axis=1
        ).astype(jnp.bfloat16),
        "fsdp",
        scatter_dimension=0,
        tiled=True,
    )
    grad_hidden_one = (
        matmul(grad_queries, query_back.T)
        + matmul(grad_keys, key_back.T)
        + matmul(grad_values, value_back.T)
    )
    gain_one_f = gain_one_back.astype(jnp.float32)
    grad_gain_one = jnp.sum(grad_hidden_one * normed_one, axis=0)
    grad_inputs = (
        grad_middle + norm_back(grad_hidden_one, gain_one_f, factor_one, normed_one)
    ).astype(jnp.bfloat16)
    attn_total, mlp_total, down_total = (
        lax.psum(attn_share, "seq").astype(jnp.float32),
        lax.psum(mlp_share, "seq").astype(jnp.float32),
        lax.psum(down_share, "seq").astype(jnp.float32),
    )
    gain_one_total, gain_two_total = lax.psum((grad_gain_one, grad_gain_two), ("seq", "fsdp"))
    query_cols = query_weight.shape[1]
    key_cols = key_matrix.shape[1]
    grad_query = attn_total[:, :query_cols]
    grad_key = attn_total[:, query_cols : query_cols + key_cols]
    grad_value = attn_total[:, query_cols + key_cols : query_cols + 2 * key_cols]
    grad_output = attn_total[:, query_cols + 2 * key_cols :]
    ff_cols = gate_weight.shape[1]
    grad_gate_w = mlp_total[:, :ff_cols]
    grad_up_w = mlp_total[:, ff_cols:]
    gain_rows = attention_gain.shape[0]
    gain_offset = lax.axis_index("fsdp") * gain_rows
    grad_attention_gain = lax.dynamic_slice_in_dim(gain_one_total, gain_offset, gain_rows, 0)
    grad_feed_gain = lax.dynamic_slice_in_dim(gain_two_total, gain_offset, gain_rows, 0)
    return (
        layer_out[None],
        grad_inputs[None],
        grad_query,
        grad_key,
        grad_value,
        grad_output,
        grad_gate_w,
        grad_up_w,
        down_total,
        grad_attention_gain,
        grad_feed_gain,
    )


def solution(mesh):
    placed = (
        P("fsdp", "seq", None),
        P("fsdp", None),
        P("fsdp", None),
        P("fsdp", None),
        P("fsdp", None),
        P("fsdp", None),
        P("fsdp", None),
        P("fsdp", None),
        P("fsdp", None),
        P("fsdp"),
        P("fsdp"),
        P("fsdp", "seq", None),
    )
    return jax.shard_map(
        shards,
        mesh=mesh,
        in_specs=placed,
        out_specs=(
            P("fsdp", "seq", None),
            P("fsdp", "seq", None),
            P("fsdp", None),
            P("fsdp", None),
            P("fsdp", None),
            P("fsdp", None),
            P("fsdp", None),
            P("fsdp", None),
            P("fsdp", None),
            P("fsdp"),
            P("fsdp"),
        ),
        check_vma=False,
    )
```

profile of v0, /device:TPU:0, one launch (start us, length us, event | category | flops | bytes accessed | tf_op | source)
XLA Modules:
  0.0 1804.9 jit_solution(10550925911419515872)
XLA Ops:
  11.9 20.2 %all-gather = bf16[16,1,128]{2,1,0:T(2,128)(2,1)S(1)} all-gather(bf16[1,1,128]{2,1,0:T(2,128)(2,1)} %bitcast.376), channel_id=1, replica_groups=mesh['seq'=8,'fsdp'=16] {'fsdp'}, dimensions={0}, use_global_device_ids=true | all-gather | bytes 4352 | tf_op jit(solution)/shard_map/all_gather | solution.py:119
  34.9 11.3 all-gather.14.cloned.1.call-done
  48.5 33.6 %all-gather.12.cloned.1.call-done = bf16[2048,512]{1,0:T(8,128)(2,1)} async-done(((bf16[128,512]{1,0:T(8,128)(2,1)}), bf16[2048,512]{1,0:T(8,128)(2,1)}) %all-gather.12.cloned.1.call-update) | async-done | bytes 2097168 | tf_op jit(solution)/shard_map/all_gather | solution.py:116
  92.1 8.7 all-to-all-done.1
  100.9 36.9 %all-gather.10.cloned.1.call-done = bf16[2048,2048]{1,0:T(8,128)(2,1)} async-done(((bf16[128,2048]{1,0:T(8,128)(2,1)}), bf16[2048,2048]{1,0:T(8,128)(2,1)}) %all-gather.10.cloned.1.call-update) | async-done | bytes 8388624 | tf_op jit(solution)/shard_map/all_gather | solution.py:115
  143.8 11.5 reduce.7
  156.3 6.9 all-to-all-start
  163.7 11.4 all-to-all-done
  180.0 23.9 %while.27 = (s32[]{:T(128)}, bf16[2,512,1,4,64]{1,4,3,2,0:T(8,128)(2,1)}, f32[2,1,4,512]{3,2,1,0:T(4,128)S(1)}, s32[2]{0:T(128)S(1)}, s32[1,1024]{1,0:T(1,128)S(...) while((s32[]{:T(128)}, ...), condition=%wide.region_6.7_spmd, body=%wide.region_3.6_spmd.sunk | while | flops 563739136 | bytes 32323832 | solution.py:174
  210.4 17.6 all-gather.1
  233.3 141.9 %all-gather.18.cloned.1.call-done = bf16[2048,8192]{1,0:T(8,128)(2,1)} async-done(((bf16[128,8192]{1,0:T(8,128)(2,1)}), bf16[2048,8192]{1,0:T(8,128)(2,1)}) %all-gather.18.cloned.1.call-update) | async-done | bytes 33554448 | tf_op jit(solution)/shard_map/all_gather | solution.py:179
  375.2 17.1 fusion.121
  392.3 155.5 %all-gather.20.cloned.1.call-done = bf16[2048,8192]{1,0:T(8,128)(2,1)} async-done(((bf16[128,8192]{1,0:T(8,128)(2,1)}), bf16[2048,8192]{1,0:T(8,128)(2,1)}) %all-gather.20.cloned.1.call-update) | async-done | bytes 33554448 | tf_op jit(solution)/shard_map/all_gather | solution.py:180
  547.8 17.1 fusion.122
  564.9 156.0 %all-gather.22.cloned.1.call-done = bf16[8192,2048]{1,0:T(8,128)(2,1)} async-done(((bf16[512,2048]{1,0:T(8,128)(2,1)}), bf16[8192,2048]{1,0:T(8,128)(2,1)}) %all-gather.22.cloned.1.call-update) | async-done | bytes 33554448 | tf_op jit(solution)/shard_map/all_gather | solution.py:181
  720.9 21.3 %multiply_convert_fusion = (bf16[128,8192]{1,0:T(8,128)(2,1)}, bf16[128,8192]{1,0:T(8,128)(2,1)}, bf16[128,8192]{1,0:T(8,128)(2,1)}) fusion(f32[128,8192]{1,0:T(8,128)} %fusion.121, f32[128,8192]{1,0:T(8,128)} %fusion.122, bf16[8192,2048]{1,0:T(8,128)(2,1)} %all-gather.22.cloned.1.call-done, bf16[1,128,2048]{2,1,0:T(8,128)(2,1)S(1)} %copy-done.15), kind=kOutput, calls=%fused_computation.72 | convolution fusion | flops 4310695936 | bytes 48758784 | tf_op jit(solution)/shard_map/dot_general | solution.py:93
  742.1 16.3 fusion.123
  758.4 17.2 multiply_reduce_fusion
  783.1 6.8 all-to-all-start.3
  789.9 12.0 all-to-all-done.3
  804.3 67.2 %while.28 = (s32[]{:T(128)}, f32[1024,1,64]{0,2,1:T(8,128)S(1)}, f32[1024,1,64]{0,2,1:T(8,128)}, f32[2,512,1,4,64]{1,0,4,3,2:T(2,128)}, s32[2]{0:T(128)S(1)}, /*...) while((s32[]{:T(128)}, f32[1024,1,64]{0,2,1:T(8,128)S(1)}, ...), condition=%wide.region_11.12_spmd.clone, body=%wide.region_9.11_spmd.clone.sunk | while | flops 1377565184 | bytes 120527152 | solution.py:268
  827.4 10.4 dynamic_update_slice.20
  861.1 10.4 dynamic_update_slice.20
  916.0 16.7 pad_maximum_fusion
  933.7 16.0 convolution_convert_fusion.1
  950.8 27.8 %convolution_convert_fusion = bf16[2048,16384]{1,0:T(8,128)(2,1)} fusion(bf16[128,2048]{1,0:T(8,128)(2,1)S(1)} %copy-done.10, bf16[128,8192]{1,0:T(8,128)(2,1)} %get-tuple-element.234, bf16[128,8192]{1,0:T(8,128)(2,1)} %get-tuple-element.235), kind=kOutput, calls=%fused_computation.64 | convolution fusion | flops 8631877632 | bytes 71827456 | tf_op jit(solution)/shard_map/ta,tb->ab/dot_general | solution.py:89
  978.6 71.4 %reduce-scatter.4.cloned.1.call-done = bf16[128,5120]{1,0:T(8,128)(2,1)} async-done(((bf16[2048,5120]{1,0:T(8,128)(2,1)}), bf16[128,5120]{1,0:T(8,128)(2,1)}) %reduce-scatter.4.cloned.1.call-update) | async-done | bytes 1310736 | tf_op jit(solution)/shard_map/reduce_scatter | solution.py:299
  1050.1 183.7 %reduce-scatter.8.cloned.1.call-done = bf16[512,2048]{1,0:T(8,128)(2,1)} async-done(((bf16[8192,2048]{1,0:T(8,128)(2,1)}), bf16[512,2048]{1,0:T(8,128)(2,1)}) %reduce-scatter.8.cloned.1.call-update) | async-done | bytes 2097168 | tf_op jit(solution)/shard_map/reduce_scatter | solution.py:201
  1233.7 352.3 %reduce-scatter.6.cloned.1.call-done = bf16[128,16384]{1,0:T(8,128)(2,1)} async-done(((bf16[2048,16384]{1,0:T(8,128)(2,1)}), bf16[128,16384]{1,0:T(8,128)(2,1)}) %reduce-scatter.6.cloned.1.call-update) | async-done | bytes 4194320 | tf_op jit(solution)/shard_map/reduce_scatter | solution.py:211
  1586.1 17.1 fusion.67
  1603.2 6.5 fusion.124
  1611.6 172.2 %all-reduce = (f32[2048]{0:T(1024)S(1)}, f32[2048]{0:T(1024)S(1)}) all-reduce(f32[2048]{0:T(1024)S(1)} %get-tuple-element.181, f32[2048]{0:T(1024)S(1)} %copy-done.30), channel_id=1, replica_groups=mesh['seq'=8,'fsdp'=16] {'seq','fsdp'}, use_global_device_ids=true, to_apply=%region_20.21 | all-reduce | flops 4096 | bytes 32768 | tf_op jit(solution)/shard_map/psum | solution.py:322
  (229 shorter events, 178.1 us)
Async XLA Ops:
  7.2 84.4 %copy-start.33 = (f32[32]{0:T(128)S(1)}, f32[32]{0:T(128)}, u32[]{:S(2)}) copy-start(f32[32]{0:T(128)} %constant.75.clone) | copy-start | bytes 388
  7.2 74.9 %copy-start.4 = (bf16[1,128,2048]{2,1,0:T(8,128)(2,1)S(1)}, bf16[1,128,2048]{2,1,0:T(8,128)(2,1)}, u32[]{:S(2)}) copy-start(bf16[1,128,2048]{2,1,0:T(8,128)(2,1)} %param.17) | copy-start | bytes 1572868
  7.2 39.1 %all-gather.14.cloned.1.call-start = ((), (), s32[]{:S(2)}) async-start(), calls=%async_computation.11 | async-start | bytes 2228224 | tf_op jit(solution)/shard_map/all_gather | solution.py:117
  7.9 74.2 %all-gather.12.cloned.1.call-start = ((), (), s32[]{:S(2)}) async-start(), calls=%async_computation.10 | async-start | bytes 2228224 | tf_op jit(solution)/shard_map/all_gather | solution.py:116
  8.7 129.1 %all-gather.10.cloned.1.call-start = ((), (), s32[]{:S(2)}) async-start(), calls=%async_computation.9 | async-start | bytes 8912896 | tf_op jit(solution)/shard_map/all_gather | solution.py:115
  9.4 218.6 %all-gather.16.cloned.1.call-start = ((), (), s32[]{:S(2)}) async-start(), calls=%async_computation.12 | async-start | bytes 8912896 | tf_op jit(solution)/shard_map/all_gather | solution.py:118
  10.0 365.2 %all-gather.18.cloned.1.call-start = ((), (), s32[]{:S(2)}) async-start(), calls=%async_computation.13 | async-start | bytes 35651584 | tf_op jit(solution)/shard_map/all_gather | solution.py:179
  10.6 537.2 %all-gather.20.cloned.1.call-start = ((), (), s32[]{:S(2)}) async-start(), calls=%async_computation.14 | async-start | bytes 35651584 | tf_op jit(solution)/shard_map/all_gather | solution.py:180
  11.2 709.7 %all-gather.22.cloned.1.call-start = ((), (), s32[]{:S(2)}) async-start(), calls=%async_computation.15 | async-start | bytes 35651584 | tf_op jit(solution)/shard_map/all_gather | solution.py:181
  32.1 105.7 %copy-start.22 = (f32[16,1,128]{2,1,0:T(1,128)}, f32[16,1,128]{2,1,0:T(1,128)S(1)}, u32[]{:S(2)}) copy-start(f32[16,1,128]{2,1,0:T(1,128)S(1)} %convert_element_type.202) | copy-start | bytes 24580
  34.8 107.7 %copy-start.31 = (f32[128]{0:T(128)}, f32[128]{0:T(128)S(1)}, u32[]{:S(2)}) copy-start(f32[128]{0:T(128)S(1)} %add_rsqrt_fusion.1) | copy-start | bytes 1540
  34.9 128.3 %copy-start.28 = (f32[1024]{0:T(1024)}, f32[1024]{0:T(1024)S(1)}, u32[]{:S(2)}) copy-start(f32[1024]{0:T(1024)S(1)} %fusion.109) | copy-start | bytes 12292
  85.1 15.7 all-to-all-start.1
  92.1 87.7 %copy-start.19 = (f32[1024,32]{0,1:T(8,128)}, f32[1024,32]{0,1:T(8,128)S(1)}, u32[]{:S(2)}) copy-start(f32[1024,32]{0,1:T(8,128)S(1)} %get-tuple-element.255) | copy-start | bytes 393220
  92.1 87.7 %copy-start.21 = (f32[1024,32]{0,1:T(8,128)}, f32[1024,32]{0,1:T(8,128)S(1)}, u32[]{:S(2)}) copy-start(f32[1024,32]{0,1:T(8,128)S(1)} %get-tuple-element.256) | copy-start | bytes 393220
  142.5 37.5 %copy-start.18 = (s32[1,1024]{1,0:T(1,128)S(1)}, s32[1,1024]{1,0:T(1,128)}, u32[]{:S(2)}) copy-start(s32[1,1024]{1,0:T(1,128)} %param.18) | copy-start | bytes 12292
  156.3 18.9 %all-to-all-start = ((bf16[8,2,16384]{2,1,0:T(2,128)(2,1)}), bf16[8,2,16384]{2,1,0:T(2,128)(2,1)S(1)}, u32[]{:S(2)}, u32[]{:S(2)}) async-start(bf16[8,2,16384]{2,1,0:T(2,128)(2,1)} %reshape.475), calls=%async_computation | async-start | bytes 1048576 | tf_op jit(solution)/shard_map/all_to_all | solution.py:128
  206.8 21.3 %all-to-all-start.2 = ((bf16[8,128,256]{1,2,0:T(8,128)(2,1)}), bf16[8,128,256]{1,2,0:T(8,128)(2,1)S(1)}, u32[]{:S(2)}, u32[]{:S(2)}) async-start(bf16[8,128,256]{1,2,0:T(8,128)(2,1)} %copy.68), calls=%async_computation.2 | async-start | bytes 1048576 | tf_op jit(solution)/shard_map/all_to_all | solution.py:176
  233.1 542.5 %copy-start.2 = (f32[128,2048]{1,0:T(8,128)}, f32[128,2048]{1,0:T(8,128)S(1)}, u32[]{:S(2)}) copy-start(f32[128,2048]{1,0:T(8,128)S(1)} %get-tuple-element.258) | copy-start | bytes 3145732
  233.3 314.5 %copy-start.9 = (bf16[128,2048]{1,0:T(8,128)(2,1)}, bf16[128,2048]{1,0:T(8,128)(2,1)S(1)}, u32[]{:S(2)}) copy-start(bf16[128,2048]{1,0:T(8,128)(2,1)S(1)} %multiply_convert_fusion.3) | copy-start | bytes 1572868
  392.3 328.5 %copy-start.15 = (bf16[1,128,2048]{2,1,0:T(8,128)(2,1)S(1)}, bf16[1,128,2048]{2,1,0:T(8,128)(2,1)}, u32[]{:S(2)}) copy-start(bf16[1,128,2048]{2,1,0:T(8,128)(2,1)} %param.28) | copy-start | bytes 1572868
  783.1 18.8 %all-to-all-start.3 = ((bf16[128,8,256]{2,0,1:T(8,128)(2,1)}), bf16[128,8,256]{2,0,1:T(8,128)(2,1)S(1)}, u32[]{:S(2)}, u32[]{:S(2)}) async-start(bf16[128,8,256]{2,0,1:T(8,128)(2,1)} %bitcast.278), calls=%async_computation.3 | async-start | bytes 1048576 | tf_op jit(solution)/shard_map/all_to_all | solution.py:230
  804.2 70.4 %copy-start.29 = (f32[1024]{0:T(1024)S(1)}, f32[1024]{0:T(1024)}, u32[]{:S(2)}) copy-start(f32[1024]{0:T(1024)} %copy-done.28) | copy-start | bytes 12292
  804.2 70.4 %copy-start.34 = (f32[32]{0:T(128)S(1)}, f32[32]{0:T(128)}, u32[]{:S(2)}) copy-start(f32[32]{0:T(128)} %constant.75.clone) | copy-start | bytes 388
  804.3 77.8 %copy-start.20 = (f32[1024,32]{0,1:T(8,128)S(1)}, f32[1024,32]{0,1:T(8,128)}, u32[]{:S(2)}) copy-start(f32[1024,32]{0,1:T(8,128)} %copy-done.19) | copy-start | bytes 393220
  878.7 12.3 all-to-all-start.5
  891.0 14.8 all-to-all-start.4
  895.2 154.9 %reduce-scatter.4.cloned.1.call-start = ((), (), s32[]{:S(2)}) async-start(), calls=%async_computation.16 | async-start | bytes 22282240 | tf_op jit(solution)/shard_map/reduce_scatter | solution.py:299
  932.7 301.1 %reduce-scatter.8.cloned.1.call-start = ((), (), s32[]{:S(2)}) async-start(), calls=%async_computation.18 | async-start | bytes 35651584 | tf_op jit(solution)/shard_map/reduce_scatter | solution.py:201
  949.7 636.3 %reduce-scatter.6.cloned.1.call-start = ((), (), s32[]{:S(2)}) async-start(), calls=%async_computation.17 | async-start | bytes 71303168 | tf_op jit(solution)/shard_map/reduce_scatter | solution.py:211
  978.5 607.6 %copy-start.3 = (f32[128,2048]{1,0:T(8,128)S(1)}, f32[128,2048]{1,0:T(8,128)}, u32[]{:S(2)}) copy-start(f32[128,2048]{1,0:T(8,128)} %copy-done.2) | copy-start | bytes 3145732
  978.6 807.6 %all-reduce.4.cloned.1.call-start = ((), (), s32[]{:S(2)}) async-start(), calls=%async_computation.19 | async-start | bytes 15204352 | tf_op jit(solution)/shard_map/psum | solution.py:318
  (25 other events, 246.1 us)
Sparse Core Ops, SparseCore 0:
  9.7 36.4 all-gather.13
  48.0 34.1 all-gather.11
  83.8 53.9 all-gather.9
  139.4 57.2 all-gather.15
  198.3 176.9 all-gather.17
  376.8 170.9 all-gather.19
  549.5 171.3 all-gather.21
  932.8 117.2 reduce-scatter.3
  1052.5 181.1 reduce-scatter.7
  1236.1 349.9 reduce-scatter.5
  1589.1 171.6 all-reduce.3
where the time goes:
time: 1820 us; the launch traced here: 1800 us
  waiting for transfers between devices  1190 us (65%)
  matrix products  229 us (13%)
  blocking collectives  210 us (12%)
  local copies, waits for them, and re-layouts  64.5 us (4%)
  other arithmetic  58.7 us (3%)
  starting transfers between devices  31.7 us (2%)
    reduce_scatter x1, waiting for transfers between devices, shards(): lax.psum_scatter(contract_rows(hidden_cols, gate_up_grads).astype(jnp.bfl...  352 us
    reduce_scatter x1, waiting for transfers between devices, shards(): lax.psum_scatter(contract_rows(act, grad_out).astype(jnp.bfloat16), 'fsdp...  184 us
    psum x1, blocking collectives, shards(): lax.psum((grad_gain_one, grad_gain_two), ('seq', 'fsdp'))  172 us
    all_gather x1, waiting for transfers between devices, shards(): lax.all_gather(down_weight, 'fsdp', axis=0, tiled=True)  156 us
    all_gather x1, waiting for transfers between devices, shards(): lax.all_gather(up_weight, 'fsdp', axis=0, tiled=True)  155 us
    all_gather x1, waiting for transfers between devices, shards(): lax.all_gather(gate_weight, 'fsdp', axis=0, tiled=True)  142 us
    dot_general x14, matrix products, matmul(): return jnp.dot(left, right, preferred_element_type=jnp.float32)  135 us
    reduce_scatter x1, waiting for transfers between devices, shards(): lax.psum_scatter(jnp.concatenate([contract_rows(hidden_cols, proj_grads),...  71.4 us
  transfers between devices with their start and end apart: 17, of which 14 were waited for; matrix products, arithmetic and copies ran while one was open for 10% of the time, Pallas kernels for 0%

commit v1 on v0

v1 whole, which is shorter than its diff:
```python
import math

import jax
import jax.numpy as jnp
from jax import lax
from jax.experimental import pallas as pl
from jax.experimental.pallas import tpu as pltpu
from jax.sharding import PartitionSpec as P

HEAD_SIZE = 64
EPS = 1e-05
ROPE_BASE = 500000.0
NEG = -1e30


def rope_freqs(head_dim):
    half_dim = head_dim // 2
    table = []
    for index in range(half_dim):
        inverse = 1.0 / ROPE_BASE ** (index * 2.0 / head_dim)
        wavelen = 2.0 * math.pi / inverse
        blend = (8192.0 / wavelen - 1.0) / 3.0
        mixed = (1.0 - blend) * inverse / 32.0 + blend * inverse
        entry = inverse if wavelen < 2048.0 else inverse / 32.0 if wavelen > 8192.0 else mixed
        table.append(entry)
    return jnp.asarray(table, dtype=jnp.float32)


def positions_of(segment_row):
    indices = jnp.arange(segment_row.shape[0], dtype=jnp.int32)
    begins = jnp.concatenate(
        [jnp.ones((1,), dtype=jnp.int32), (segment_row[1:] != segment_row[:-1]).astype(jnp.int32)]
    )
    starts_at = lax.cummax(jnp.where(begins > 0, indices, 0), axis=0)
    return indices - starts_at


def angles_of(segment_row, head_dim):
    positions = positions_of(segment_row)
    phase = positions.astype(jnp.float32)[:, None] * rope_freqs(head_dim)[None, :]
    return (jnp.cos(phase), jnp.sin(phase))


MESH = pl.DeviceIdType.MESH
CHUNKS = 4
TILE = 256


def ring():
    rank, owner = lax.axis_index("seq"), lax.axis_index("fsdp")
    side = lax.axis_size("seq") // 2
    row, col = lax.div(rank, side), lax.rem(rank, side)

    def at(which, step):
        return which * side + lax.rem(col + step, side)

    near = [at(row, step) for step in range(side)]
    far = [at(1 - row, step) for step in range(side)]
    return owner, near, far


def greet(owner, peers):
    barrier = pltpu.get_barrier_semaphore()
    for peer in peers:
        pl.semaphore_signal(barrier, inc=1, device_id=(peer, owner), device_id_type=MESH)
    pl.semaphore_wait(barrier, len(peers))


class Copies:
    def __init__(self, owner, send, recv):
        self.owner, self.send, self.recv = owner, send, recv
        self.made = []

    def start(self, source, target, peer):
        number = len(self.made)
        copy = pltpu.make_async_remote_copy(
            src_ref=source,
            dst_ref=target,
            send_sem=self.send.at[number],
            recv_sem=self.recv.at[number],
            device_id=(peer, self.owner),
            device_id_type=MESH,
        )
        copy.start()
        self.made.append(copy)
        return copy

    def finish(self):
        for copy in self.made:
            copy.wait_send()


def gather_blocks(ids, copies, own, out, rows, chunks):
    _, near, far = ids
    me, right, opposite, left = near
    partner = far[0]
    size = rows // chunks
    half = chunks // 2

    def part(index):
        return pl.ds(index * size, size)

    to_right, to_left, to_far = {}, {}, {}
    for step in range(chunks):
        back = chunks - 1 - step
        to_right[step] = copies.start(own.at[part(step)], out.at[me, part(step)], right)
        to_left[back] = copies.start(own.at[part(back)], out.at[me, part(back)], left)
        to_far[step] = copies.start(own.at[part(step)], out.at[me, part(step)], partner)
    on = {}
    for step in range(half):
        back = chunks - 1 - step
        to_right[step].wait_recv()
        on[step] = copies.start(out.at[left, part(step)], out.at[left, part(step)], right)
        to_left[back].wait_recv()
        on[back] = copies.start(out.at[right, part(back)], out.at[right, part(back)], left)
    rest = []
    for step in range(chunks):
        to_far[step].wait_recv()
        block = out.at[partner, part(step)]
        rest.append(copies.start(block, block, right))
        rest.append(copies.start(block, block, left))
    for step in range(half):
        for index in (step, chunks - 1 - step):
            on[index].wait_recv()
            block = out.at[opposite, part(index)]
            rest.append(copies.start(block, block, partner))
    for step in range(half):
        to_right[chunks - 1 - step].wait_recv()
        to_left[step].wait_recv()
    for copy in rest:
        copy.wait_recv()


def gather_copies(chunks):
    return 3 * chunks + chunks + 2 * chunks + chunks


def reduce_blocks(ids, copies, part_of, bufs, rows, chunks, done):
    _, near, far = ids
    me, right, opposite, left = near
    partner, far_right, far_opposite, far_left = far
    from_left, from_right, from_far, mid, end_left, end_right, end_far = bufs
    size = rows // chunks
    half = chunks // 2

    def part(index):
        return pl.ds(index * size, size)

    def wide(ref):
        return ref.astype(jnp.float32)

    order = [x for step in range(half) for x in (step, chunks - 1 - step)]
    one_right, one_left, one_far = {}, {}, {}
    for index in order:
        rows_of = part(index)
        one_far[index] = copies.start(
            part_of.at[far_opposite, rows_of], from_far.at[rows_of], partner
        )
        one_right[index] = copies.start(
            part_of.at[far_right, rows_of], from_left.at[rows_of], right
        )
        one_left[index] = copies.start(part_of.at[far_left, rows_of], from_right.at[rows_of], left)
    last_right, last_left, last_far = {}, {}, {}
    for index in range(half):
        rows_of = part(index)
        last_right[index] = copies.start(part_of.at[right, rows_of], end_left.at[rows_of], right)
        rows_of = part(chunks - 1 - index)
        last_left[chunks - 1 - index] = copies.start(
            part_of.at[left, rows_of], end_right.at[rows_of], left
        )
    two = {}
    for index in order:
        rows_of = part(index)
        one_far[index].wait_recv()
        from_far[rows_of] = (wide(from_far[rows_of]) + wide(part_of[opposite, rows_of])).astype(
            jnp.bfloat16
        )
        two[index] = copies.start(
            from_far.at[rows_of], mid.at[rows_of], left if index < half else right
        )
    for index in order:
        rows_of = part(index)
        one_right[index].wait_recv()
        one_left[index].wait_recv()
        from_left[rows_of] = (
            wide(from_left[rows_of]) + wide(from_right[rows_of]) + wide(part_of[partner, rows_of])
        ).astype(jnp.bfloat16)
        last_far[index] = copies.start(from_left.at[rows_of], end_far.at[rows_of], partner)
    for index in order:
        rows_of = part(index)
        two[index].wait_recv()
        if index < half:
            mid[rows_of] = (wide(mid[rows_of]) + wide(part_of[left, rows_of])).astype(jnp.bfloat16)
            last_left[index] = copies.start(mid.at[rows_of], end_right.at[rows_of], left)
        else:
            mid[rows_of] = (wide(mid[rows_of]) + wide(part_of[right, rows_of])).astype(
                jnp.bfloat16
            )
            last_right[index] = copies.start(mid.at[rows_of], end_left.at[rows_of], right)
    for index in order:
        rows_of = part(index)
        last_far[index].wait_recv()
        last_left[index].wait_recv()
        last_right[index].wait_recv()
        done(
            rows_of,
            wide(part_of[me, rows_of])
            + wide(end_left[rows_of])
            + wide(end_right[rows_of])
            + wide(end_far[rows_of]),
        )


def reduce_copies(chunks):
    return 3 * chunks + 2 * chunks + chunks + chunks


def reduce_scratch(rows, width):
    return [pltpu.VMEM((rows, width), jnp.bfloat16) for _ in range(7)]


def semaphores(count):
    return [pltpu.SemaphoreType.DMA((count,)), pltpu.SemaphoreType.DMA((count,))]


def params(number, limit):
    return pltpu.CompilerParams(
        collective_id=number, has_side_effects=True, vmem_limit_bytes=limit * 2**20
    )


VMEM = pl.BlockSpec(memory_space=pltpu.VMEM)
ANYWHERE = pl.BlockSpec(memory_space=pl.ANY)


def gather_many(blocks, number):
    count = len(blocks)
    rows, width = blocks[0].shape
    ranks = lax.axis_size("seq")
    each = gather_copies(CHUNKS)

    def kernel(*refs):
        own, out = refs[:count], refs[count : 2 * count]
        local, send, recv = refs[2 * count :]
        ids = ring()
        owner, near, far = ids
        greet(owner, (near[1], near[3], far[0]))
        kept = [
            pltpu.make_async_copy(own[i], out[i].at[near[0]], local.at[i]) for i in range(count)
        ]
        for copy in kept:
            copy.start()
        copies = Copies(owner, send, recv)
        for i in range(count):
            gather_blocks(ids, copies, own[i], out[i], rows, CHUNKS)
        copies.finish()
        for copy in kept:
            copy.wait()

    moved = count * ranks * rows * width * 2
    return pl.pallas_call(
        kernel,
        out_shape=[jax.ShapeDtypeStruct((ranks, rows, width), jnp.bfloat16)] * count,
        in_specs=[ANYWHERE] * count,
        out_specs=[ANYWHERE] * count,
        scratch_shapes=[pltpu.SemaphoreType.DMA((count,))] + semaphores(count * each),
        compiler_params=params(number, 32),
        cost_estimate=pl.CostEstimate(flops=0, bytes_accessed=moved * 16, transcendentals=0),
        name="gather_many",
    )(*blocks)


def mean_square(values):
    return jnp.mean(values * values, axis=-1, keepdims=True)


def branch_kernel(part_of, tokens, gain, middle, hidden, block, local, send, recv, *bufs):
    ids = ring()
    owner, near, far = ids
    rows = tokens.shape[0]
    greet(owner, (near[1], near[3], far[0]))
    copies = Copies(owner, send, recv)

    def done(rows_of, total):
        values = tokens[rows_of].astype(jnp.float32) + total
        middle[rows_of] = values
        factor = lax.rsqrt(mean_square(values) + EPS)
        block[rows_of] = (values * factor * gain[...]).astype(jnp.bfloat16)

    reduce_blocks(ids, copies, part_of, bufs, rows, CHUNKS, done)
    kept = pltpu.make_async_copy(block, hidden.at[near[0]], local)
    kept.start()
    gather_blocks(ids, copies, block, hidden, rows, CHUNKS)
    copies.finish()
    kept.wait()


def add_branch(partial, tokens, gain, number):
    rows, width = tokens.shape
    ranks = lax.axis_size("seq")
    count = reduce_copies(CHUNKS) + gather_copies(CHUNKS)
    return pl.pallas_call(
        branch_kernel,
        out_shape=[
            jax.ShapeDtypeStruct((rows, width), jnp.float32),
            jax.ShapeDtypeStruct((ranks, rows, width), jnp.bfloat16),
        ],
        in_specs=[VMEM] * 3,
        out_specs=[VMEM, ANYWHERE],
        scratch_shapes=[pltpu.VMEM((rows, width), jnp.bfloat16), pltpu.SemaphoreType.DMA]
        + semaphores(count)
        + reduce_scratch(rows, width),
        compiler_params=params(number, 32),
        cost_estimate=pl.CostEstimate(
            flops=0, bytes_accessed=ranks * rows * width * 64, transcendentals=0
        ),
        name="add_branch",
    )(partial.reshape(ranks, rows, width), tokens, gain)


def norm_back_rows(grad, gain, values):
    factor = lax.rsqrt(mean_square(values) + EPS)
    normed = values * factor
    weighted = grad * gain
    back = factor * (weighted - normed * jnp.mean(weighted * normed, axis=-1, keepdims=True))
    return back, grad * normed


def middle_kernel(
    part_of, middle, gain, cotangent, grad_middle, grad_gain, branch, block, local, send, recv, *bufs
):
    ids = ring()
    owner, near, far = ids
    rows = middle.shape[0]
    greet(owner, (near[1], near[3], far[0]))
    copies = Copies(owner, send, recv)
    grad_gain[...] = jnp.zeros_like(grad_gain)

    def done(rows_of, total):
        back, terms = norm_back_rows(total, gain[...], middle[rows_of])
        grad_gain[...] += jnp.sum(terms, axis=0, keepdims=True)
        values = cotangent[rows_of].astype(jnp.float32) + back
        grad_middle[rows_of] = values
        block[rows_of] = values.astype(jnp.bfloat16)

    reduce_blocks(ids, copies, part_of, bufs, rows, CHUNKS, done)
    kept = pltpu.make_async_copy(block, branch.at[near[0]], local)
    kept.start()
    gather_blocks(ids, copies, block, branch, rows, CHUNKS)
    copies.finish()
    kept.wait()


def back_to_middle(partial, middle, gain, cotangent, number):
    rows, width = middle.shape
    ranks = lax.axis_size("seq")
    count = reduce_copies(CHUNKS) + gather_copies(CHUNKS)
    return pl.pallas_call(
        middle_kernel,
        out_shape=[
            jax.ShapeDtypeStruct((rows, width), jnp.float32),
            jax.ShapeDtypeStruct((1, width), jnp.float32),
            jax.ShapeDtypeStruct((ranks, rows, width), jnp.bfloat16),
        ],
        in_specs=[VMEM] * 4,
        out_specs=[VMEM, VMEM, ANYWHERE],
        scratch_shapes=[pltpu.VMEM((rows, width), jnp.bfloat16), pltpu.SemaphoreType.DMA]
        + semaphores(count)
        + reduce_scratch(rows, width),
        compiler_params=params(number, 32),
        cost_estimate=pl.CostEstimate(
            flops=0, bytes_accessed=ranks * rows * width * 64, transcendentals=0
        ),
        name="back_to_middle",
    )(partial.reshape(ranks, rows, width), middle, gain, cotangent)


def tokens_kernel(part_of, tokens, gain, grad_middle, out, grad_gain, send, recv, *bufs):
    ids = ring()
    owner, near, far = ids
    rows = tokens.shape[0]
    greet(owner, (near[1], near[3], far[0]))
    copies = Copies(owner, send, recv)
    grad_gain[...] = jnp.zeros_like(grad_gain)

    def done(rows_of, total):
        back, terms = norm_back_rows(total, gain[...], tokens[rows_of].astype(jnp.float32))
        grad_gain[...] += jnp.sum(terms, axis=0, keepdims=True)
        out[rows_of] = (grad_middle[rows_of] + back).astype(jnp.bfloat16)

    reduce_blocks(ids, copies, part_of, bufs, rows, CHUNKS, done)
    copies.finish()


def back_to_tokens(partial, tokens, gain, grad_middle, number):
    rows, width = tokens.shape
    ranks = lax.axis_size("seq")
    return pl.pallas_call(
        tokens_kernel,
        out_shape=[
            jax.ShapeDtypeStruct((rows, width), jnp.bfloat16),
            jax.ShapeDtypeStruct((1, width), jnp.float32),
        ],
        in_specs=[VMEM] * 4,
        out_specs=[VMEM, VMEM],
        scratch_shapes=semaphores(reduce_copies(CHUNKS)) + reduce_scratch(rows, width),
        compiler_params=params(number, 32),
        cost_estimate=pl.CostEstimate(
            flops=0, bytes_accessed=ranks * rows * width * 32, transcendentals=0
        ),
        name="back_to_tokens",
    )(partial.reshape(ranks, rows, width), tokens, gain, grad_middle)


def layer_kernel(part_of, middle, out, send, recv, *bufs):
    ids = ring()
    owner, near, far = ids
    greet(owner, (near[1], near[3], far[0]))
    copies = Copies(owner, send, recv)

    def done(rows_of, total):
        out[rows_of] = (middle[rows_of] + total).astype(jnp.bfloat16)

    reduce_blocks(ids, copies, part_of, bufs, middle.shape[0], CHUNKS, done)
    copies.finish()


def finish_layer(partial, middle, number):
    rows, width = middle.shape
    ranks = lax.axis_size("seq")
    return pl.pallas_call(
        layer_kernel,
        out_shape=jax.ShapeDtypeStruct((rows, width), jnp.bfloat16),
        in_specs=[VMEM] * 2,
        out_specs=VMEM,
        scratch_shapes=semaphores(reduce_copies(CHUNKS)) + reduce_scratch(rows, width),
        compiler_params=params(number, 32),
        cost_estimate=pl.CostEstimate(
            flops=0, bytes_accessed=ranks * rows * width * 32, transcendentals=0
        ),
        name="finish_layer",
    )(partial.reshape(ranks, rows, width), middle)


def rotate_rows(first, second, cosine, sine):
    return jnp.concatenate([first * cosine - second * sine, second * cosine + first * sine], axis=0)


def bias_tile(start_row, key_tile, query_tile, diagonal):
    keys = key_tile * TILE + lax.broadcasted_iota(jnp.int32, (TILE, TILE), 0)
    seen = keys >= start_row
    if diagonal:
        queries = query_tile * TILE + lax.broadcasted_iota(jnp.int32, (TILE, TILE), 1)
        seen = seen & (keys <= queries)
    return jnp.where(seen, 0.0, NEG)


def forward_kernel(qkv, cosine, sine, starts, attended, lse, queries, keys, key_rows, bias):
    group = queries.shape[0] // HEAD_SIZE
    half = HEAD_SIZE // 2
    tiles = qkv.shape[1] // TILE
    cos, sin = cosine[...], sine[...]

    def rotated(first):
        return rotate_rows(
            qkv[pl.ds(first, half)].astype(jnp.float32),
            qkv[pl.ds(first + half, half)].astype(jnp.float32),
            cos,
            sin,
        ).astype(jnp.bfloat16)

    for head in range(group):
        queries[pl.ds(head * HEAD_SIZE, HEAD_SIZE)] = rotated(head * HEAD_SIZE) * jnp.bfloat16(0.125)
    keys[...] = rotated(group * HEAD_SIZE)
    key_rows[...] = keys[...].T
    for tile in range(tiles):
        lanes = pl.ds(tile * TILE, TILE)
        starts_here = starts[:, lanes]
        for low in range(tile + 1):
            bias[pl.ds(low * TILE, TILE)] = bias_tile(starts_here, low, tile, low == tile)
        count = (tile + 1) * TILE

        def one_head(head, _, lanes=lanes, count=count):
            rows = pl.ds(pl.multiple_of(head * HEAD_SIZE, HEAD_SIZE), HEAD_SIZE)
            scores = jnp.dot(
                key_rows[:count], queries[rows, lanes], preferred_element_type=jnp.float32
            )
            scores += bias[:count]
            highest = jnp.max(scores, axis=0, keepdims=True)
            weights = jnp.exp(scores - highest)
            total = jnp.sum(weights, axis=0, keepdims=True)
            out = jnp.dot(
                qkv[pl.ds((group + 1) * HEAD_SIZE, HEAD_SIZE), :count],
                weights.astype(jnp.bfloat16),
                preferred_element_type=jnp.float32,
            )
            attended[rows, lanes] = (out / total).astype(jnp.bfloat16)
            lse[head, :, lanes] = jnp.broadcast_to(highest + jnp.log(total), (8, TILE))
            return 0

        lax.fori_loop(0, group, one_head, 0)


def attend(qkv, cosine, sine, starts, group):
    length = qkv.shape[1]
    return pl.pallas_call(
        forward_kernel,
        out_shape=[
            jax.ShapeDtypeStruct((group * HEAD_SIZE, length), jnp.bfloat16),
            jax.ShapeDtypeStruct((group, 8, length), jnp.float32),
            jax.ShapeDtypeStruct((group * HEAD_SIZE, length), jnp.bfloat16),
            jax.ShapeDtypeStruct((HEAD_SIZE, length), jnp.bfloat16),
        ],
        in_specs=[VMEM] * 4,
        out_specs=[VMEM] * 4,
        scratch_shapes=[
            pltpu.VMEM((length, HEAD_SIZE), jnp.bfloat16),
            pltpu.VMEM((length, TILE), jnp.float32),
        ],
        compiler_params=pltpu.CompilerParams(vmem_limit_bytes=32 * 2**20),
        cost_estimate=pl.CostEstimate(
            flops=4 * group * length * length * HEAD_SIZE,
            bytes_accessed=group * length * length,
            transcendentals=group * length * length,
        ),
        name="attend",
    )(qkv, cosine, sine, starts)


def backward_kernel(
    qkv,
    queries,
    keys,
    attended,
    lse,
    grads,
    cosine,
    sine,
    starts,
    out,
    key_rows,
    value_rows,
    query_rows,
    grad_rows,
    row_dots,
    key_grad,
    value_grad,
    query_grad,
    bias,
):
    group = queries.shape[0] // HEAD_SIZE
    half = HEAD_SIZE // 2
    tiles = qkv.shape[1] // TILE
    key_rows[...] = keys[...].T
    value_rows[...] = qkv[pl.ds((group + 1) * HEAD_SIZE, HEAD_SIZE)].T
    for head in range(group):
        rows = pl.ds(head * HEAD_SIZE, HEAD_SIZE)
        query_rows[head] = queries[rows].T
        grad_rows[head] = grads[rows].T
        row_dots[head] = jnp.broadcast_to(
            jnp.sum(
                grads[rows].astype(jnp.float32) * attended[rows].astype(jnp.float32),
                axis=0,
                keepdims=True,
            ),
            row_dots.shape[1:],
        )
    key_grad[...] = jnp.zeros_like(key_grad)
    value_grad[...] = jnp.zeros_like(value_grad)
    for tile in range(tiles):
        lanes = pl.ds(tile * TILE, TILE)
        starts_here = starts[:, lanes]
        for low in range(tile + 1):
            bias[low] = bias_tile(starts_here, low, tile, low == tile)

        def one_head(head, _, lanes=lanes, tile=tile):
            rows = pl.ds(pl.multiple_of(head * HEAD_SIZE, HEAD_SIZE), HEAD_SIZE)
            query, grad = queries[rows, lanes], grads[rows, lanes]
            query_row, grad_row = query_rows[head, lanes], grad_rows[head, lanes]
            lse_row = lse[head, 0:1, lanes]
            dot_row = row_dots[head, 0:1, lanes]
            total = jnp.zeros((HEAD_SIZE, TILE), jnp.float32)
            for low in range(tile + 1):
                part = pl.ds(low * TILE, TILE)
                scores = jnp.dot(key_rows[part], query, preferred_element_type=jnp.float32)
                probs = jnp.exp(scores + bias[low] - lse_row)
                grad_probs = jnp.dot(value_rows[part], grad, preferred_element_type=jnp.float32)
                grad_scores = (probs * (grad_probs - dot_row)).astype(jnp.bfloat16)
                value_grad[part] += jnp.dot(
                    probs.astype(jnp.bfloat16), grad_row, preferred_element_type=jnp.float32
                )
                key_grad[part] += jnp.dot(
                    grad_scores, query_row, preferred_element_type=jnp.float32
                )
                total += jnp.dot(keys[:, part], grad_scores, preferred_element_type=jnp.float32)
            query_grad[rows, lanes] = total * 0.125
            return 0

        lax.fori_loop(0, group, one_head, 0)
    cos, sin = cosine[...], sine[...]
    for head in range(group):
        first = head * HEAD_SIZE
        out[pl.ds(first, HEAD_SIZE)] = rotate_rows(
            query_grad[pl.ds(first, half)], query_grad[pl.ds(first + half, half)], cos, -sin
        ).astype(jnp.bfloat16)
    turned = key_grad[...].T
    out[pl.ds(group * HEAD_SIZE, HEAD_SIZE)] = rotate_rows(
        turned[:half], turned[half:], cos, -sin
    ).astype(jnp.bfloat16)
    out[pl.ds((group + 1) * HEAD_SIZE, HEAD_SIZE)] = value_grad[...].T.astype(jnp.bfloat16)


def attend_back(qkv, queries, keys, attended, lse, grads, cosine, sine, starts):
    length = qkv.shape[1]
    group = queries.shape[0] // HEAD_SIZE
    tiles = length // TILE
    return pl.pallas_call(
        backward_kernel,
        out_shape=jax.ShapeDtypeStruct(qkv.shape, jnp.bfloat16),
        in_specs=[VMEM] * 9,
        out_specs=VMEM,
        scratch_shapes=[
            pltpu.VMEM((length, HEAD_SIZE), jnp.bfloat16),
            pltpu.VMEM((length, HEAD_SIZE), jnp.bfloat16),
            pltpu.VMEM((group, length, HEAD_SIZE), jnp.bfloat16),
            pltpu.VMEM((group, length, HEAD_SIZE), jnp.bfloat16),
            pltpu.VMEM((group, 8, length), jnp.float32),
            pltpu.VMEM((length, HEAD_SIZE), jnp.float32),
            pltpu.VMEM((length, HEAD_SIZE), jnp.float32),
            pltpu.VMEM((group * HEAD_SIZE, length), jnp.float32),
            pltpu.VMEM((tiles, TILE, TILE), jnp.float32),
        ],
        compiler_params=pltpu.CompilerParams(vmem_limit_bytes=40 * 2**20),
        cost_estimate=pl.CostEstimate(
            flops=10 * group * length * length * HEAD_SIZE,
            bytes_accessed=2 * group * length * length,
            transcendentals=group * length * length,
        ),
        name="attend_back",
    )(qkv, queries, keys, attended, lse, grads, cosine, sine, starts)


def contract_rows(left, right):
    return jnp.einsum("ta,tb->ab", left, right, preferred_element_type=jnp.float32)


def contract_cols(left, right):
    return jnp.einsum("ta,ba->tb", left, right, preferred_element_type=jnp.float32)


def matmul(left, right):
    return jnp.dot(left, right, preferred_element_type=jnp.float32)


def swap_heads(block):
    pairs = [(t * 16 + g, (g // 2) * 16 + 2 * t + g % 2) for t in range(8) for g in range(16)]
    return lax.ppermute(block, ("seq", "fsdp"), pairs)


def swap_heads_back(block):
    pairs = [((g // 2) * 16 + 2 * t + g % 2, t * 16 + g) for t in range(8) for g in range(16)]
    return lax.ppermute(block, ("seq", "fsdp"), pairs)


def swap_cores(block):
    return lax.ppermute(block, "fsdp", [(f, f ^ 1) for f in range(16)])


def shards(
    tokens,
    segment_ids,
    query_weight,
    key_matrix,
    value_matrix,
    output_weight,
    gate_weight,
    up_weight,
    down_weight,
    attention_gain,
    feed_gain,
    cotangent,
):
    rank = lax.axis_index("seq")
    owner = lax.axis_index("fsdp")
    ranks = lax.axis_size("seq")
    owners = lax.axis_size("fsdp")
    rows, width = query_weight.shape
    kv_cols = key_matrix.shape[1] // ranks
    q_cols = width // ranks
    group = q_cols // kv_cols
    ff = gate_weight.shape[1]
    ff_chunk = ff // owners // ranks
    segment_row = segment_ids[0]
    length = segment_row.shape[0]

    def columns(weight, size):
        return lax.dynamic_slice_in_dim(weight, rank * size, size, 1)

    def ff_columns(weight):
        split = weight.reshape(rows, owners, ranks, ff_chunk)
        return lax.dynamic_slice_in_dim(split, rank, 1, 2).reshape(rows, owners * ff_chunk)

    gains_in = jnp.zeros((16, q_cols + 2 * kv_cols), jnp.bfloat16)
    gains_in = gains_in.at[0, :rows].set(attention_gain).at[1, :rows].set(feed_gain)
    qkv_in = jnp.concatenate(
        [columns(query_weight, q_cols), columns(key_matrix, kv_cols), columns(value_matrix, kv_cols)],
        axis=1,
    )
    qkv_got = lax.all_gather(jnp.concatenate([qkv_in, gains_in], axis=0), "fsdp", axis=0)
    qkv_all = qkv_got[:, :rows].reshape(owners * rows, -1)
    gain_one = qkv_got[:, rows, :rows].reshape(1, -1).astype(jnp.float32)
    gain_two = qkv_got[:, rows + 1, :rows].reshape(1, -1).astype(jnp.float32)
    half = swap_heads(output_weight)
    other = swap_cores(half)
    first = owner % 2 == 0
    output_all = jnp.concatenate(
        [jnp.where(first, half, other), jnp.where(first, other, half)], axis=0
    )
    gate_up_all = lax.all_gather(
        jnp.concatenate([ff_columns(gate_weight), ff_columns(up_weight)], axis=1),
        "fsdp",
        axis=0,
        tiled=True,
    )
    ff_local = owners * ff_chunk
    down_all = lax.all_gather(
        lax.dynamic_slice_in_dim(down_weight, rank * ff_chunk, ff_chunk, 0),
        "fsdp",
        axis=0,
        tiled=True,
    )

    starts = (jnp.arange(length, dtype=jnp.int32) - positions_of(segment_row))[None]
    cosine, sine = (table.T for table in angles_of(segment_row, HEAD_SIZE))
    whole, grad_out = gather_many([tokens[0], cotangent[0]], 0)
    whole = whole.reshape(length, width).astype(jnp.float32)
    grad_out = grad_out.reshape(length, width)
    hidden_one = (whole * lax.rsqrt(mean_square(whole) + EPS) * gain_one).astype(jnp.bfloat16)
    qkv = jnp.einsum("tm,mc->ct", hidden_one, qkv_all, preferred_element_type=jnp.float32)
    qkv = qkv.astype(jnp.bfloat16)
    attended, lse, queries, keys = attend(qkv, cosine, sine, starts, group)
    middle, hidden_two = add_branch(
        contract_rows(attended, output_all).astype(jnp.bfloat16), tokens[0], gain_two, 1
    )
    hidden_two = hidden_two.reshape(length, width)

    gate = matmul(hidden_two, gate_up_all[:, :ff_local])
    up_proj = matmul(hidden_two, gate_up_all[:, ff_local:])
    sig_gate = jax.nn.sigmoid(gate)
    silu_gate = gate * sig_gate
    act = (silu_gate * up_proj).astype(jnp.bfloat16)
    grad_act = contract_cols(grad_out, down_all)
    grad_gate = (grad_act * up_proj * (sig_gate * (1.0 + gate * (1.0 - sig_gate)))).astype(
        jnp.bfloat16
    )
    grad_up = (grad_act * silu_gate).astype(jnp.bfloat16)
    gate_up_grads = jnp.concatenate([grad_gate, grad_up], axis=1)
    down_grad = contract_rows(act, grad_out).astype(jnp.bfloat16)
    down_share = lax.psum_scatter(down_grad, "fsdp", scatter_dimension=0, tiled=True)
    gate_up_grad = contract_rows(hidden_two, gate_up_grads).astype(jnp.bfloat16)
    gate_up_share = lax.psum_scatter(gate_up_grad, "fsdp", scatter_dimension=0, tiled=True)
    ff_whole = lax.all_gather(
        jnp.concatenate([gate_up_share, down_share], axis=0), "seq", axis=0
    )
    gate_up_whole = ff_whole[:, :rows]
    down_whole = ff_whole[:, rows:].reshape(-1, width).astype(jnp.float32)
    grad_middle, grad_gain_two, grad_branch = back_to_middle(
        contract_cols(gate_up_grads, gate_up_all).astype(jnp.bfloat16),
        middle,
        gain_two,
        cotangent[0],
        2,
    )
    grad_branch = grad_branch.reshape(length, width)

    grad_attended = jnp.einsum(
        "tm,fm->ft", grad_branch, output_all, preferred_element_type=jnp.float32
    ).astype(jnp.bfloat16)
    qkv_grads = attend_back(
        qkv, queries, keys, attended, lse, grad_attended, cosine, sine, starts
    )
    output_grad = matmul(attended, grad_branch).astype(jnp.bfloat16)
    output_grad = output_grad.reshape(2, ranks, -1, width).swapaxes(0, 1).reshape(-1, width)
    output_share = swap_heads_back(
        lax.psum_scatter(output_grad, "fsdp", scatter_dimension=0, tiled=True)
    )
    output_whole = lax.all_gather(output_share, "seq", axis=0, tiled=True).astype(jnp.float32)
    grad_inputs, grad_gain_one = back_to_tokens(
        jnp.einsum("ct,mc->tm", qkv_grads, qkv_all, preferred_element_type=jnp.float32).astype(
            jnp.bfloat16
        ),
        tokens[0],
        gain_one,
        grad_middle,
        3,
    )
    qkv_share = lax.psum_scatter(
        jnp.einsum(
            "tm,ct->mc", hidden_one, qkv_grads, preferred_element_type=jnp.float32
        ).astype(jnp.bfloat16),
        "fsdp",
        scatter_dimension=0,
        tiled=True,
    )
    qkv_whole = lax.all_gather(qkv_share, "seq", axis=0)
    layer_out = finish_layer(matmul(act, down_all).astype(jnp.bfloat16), middle, 4)
    gain_totals = lax.psum(jnp.concatenate([grad_gain_one, grad_gain_two]), ("seq", "fsdp"))
    gain_totals = lax.dynamic_slice_in_dim(gain_totals, owner * rows, rows, 1)

    def spread(part):
        return part.swapaxes(0, 1).reshape(rows, -1).astype(jnp.float32)

    def ff_spread(part):
        return (
            part.reshape(ranks, rows, owners, ff_chunk)
            .transpose(1, 2, 0, 3)
            .reshape(rows, ff)
            .astype(jnp.float32)
        )

    return (
        layer_out[None],
        grad_inputs[None],
        spread(qkv_whole[:, :, :q_cols]),
        spread(qkv_whole[:, :, q_cols : q_cols + kv_cols]),
        spread(qkv_whole[:, :, q_cols + kv_cols :]),
        output_whole,
        ff_spread(gate_up_whole[:, :, :ff_local]),
        ff_spread(gate_up_whole[:, :, ff_local:]),
        down_whole,
        gain_totals[0],
        gain_totals[1],
    )


def solution(mesh):
    placed = (
        P("fsdp", "seq", None),
        P("fsdp", None),
        P("fsdp", None),
        P("fsdp", None),
        P("fsdp", None),
        P("fsdp", None),
        P("fsdp", None),
        P("fsdp", None),
        P("fsdp", None),
        P("fsdp"),
        P("fsdp"),
        P("fsdp", "seq", None),
    )
    return jax.shard_map(
        shards,
        mesh=mesh,
        in_specs=placed,
        out_specs=(
            P("fsdp", "seq", None),
            P("fsdp", "seq", None),
            P("fsdp", None),
            P("fsdp", None),
            P("fsdp", None),
            P("fsdp", None),
            P("fsdp", None),
            P("fsdp", None),
            P("fsdp", None),
            P("fsdp"),
            P("fsdp"),
        ),
        check_vma=False,
    )
```

time: 1820 us -> 700 us (0.38)
  waiting for transfers between devices: 1190 us -> 3.77 us
  Pallas kernels: 0 us -> 363 us
  matrix products: 229 us -> 87.7 us
  blocking collectives: 210 us -> 139 us
  other arithmetic: 58.7 us -> 19.8 us
  starting transfers between devices: 31.7 us -> 2.6 us
    reduce_scatter x3 -> x4, waiting for transfers between devices: 607 us -> 2.55 us  [the longest x1 2.53 us: shards(): lax.psum_scatter(gate_up_grad, 'fsdp', scatter_dimension=0, tiled=True)]
    all_gather x7 -> x4, waiting for transfers between devices: 535 us -> 0.03 us  [the longest x1 0.02 us: shards(): lax.all_gather(jnp.concatenate([qkv_in, gains_in], axis=0), 'fsdp', axis=0)]
    pallas_call x0 -> x7, Pallas kernels: none -> 363 us  [the longest x1 97.3 us: gather_many(): pl.pallas_call(kernel, out_shape=[jax.ShapeDtypeStruct((ranks, rows, widt...]
    psum x1, blocking collectives: 172 us -> 66 us  [shards(): lax.psum(jnp.concatenate([grad_gain_one, grad_gain_two]), ('seq', 'fsdp'))]
    dot_general x14 -> x4, matrix products: 135 us -> 32.6 us  [matmul(): return jnp.dot(left, right, preferred_element_type=jnp.float32)]
    all_to_all x6 -> x0, waiting for transfers between devices: 41.2 us -> none  [the longest x1 12 us: shards(): lax.all_to_all(grad_attended, 'seq', split_axis=1, concat_axis=0, tiled=T...]
    all_gather x2, blocking collectives: 37.8 us -> 72.7 us  [the longest x1 36.8 us: shards(): qkv_whole = lax.all_gather(qkv_share, 'seq', axis=0)]
    dot_general x4 -> x3, matrix products: 54.5 us -> 21.3 us  [contract_rows(): jnp.einsum('ta,tb->ab', left, right, preferred_element_type=jnp.float32)]
  transfers between devices with their start and end apart: 17 -> 11, of which waited for: 14 -> 2; matrix products, arithmetic and copies ran while one was open for 10% -> 13% of each run, Pallas kernels for 0% -> 52%
where the time goes in v1:
time: 700 us; the launch traced here: 693 us
  Pallas kernels  363 us (52%)
  blocking collectives  139 us (20%)
  matrix products  87.7 us (13%)
  local copies, waits for them, and re-layouts  62.3 us (9%)
  other arithmetic  19.8 us (3%)
  between operations  15.2 us (2%)
    pallas_call x1, Pallas kernels, gather_many(): pl.pallas_call(kernel, out_shape=[jax.ShapeDtypeStruct((ranks, rows, widt...  97.3 us
    pallas_call x1, Pallas kernels, back_to_middle(): pl.pallas_call(middle_kernel, out_shape=[jax.ShapeDtypeStruct((rows, widt...  87.5 us
    pallas_call x1, Pallas kernels, add_branch(): pl.pallas_call(branch_kernel, out_shape=[jax.ShapeDtypeStruct((rows, widt...  78.4 us
    psum x1, blocking collectives, shards(): lax.psum(jnp.concatenate([grad_gain_one, grad_gain_two]), ('seq', 'fsdp'))  66 us
    pallas_call x1, Pallas kernels, finish_layer(): pl.pallas_call(layer_kernel, out_shape=jax.ShapeDtypeStruct((rows, width)...  44.7 us
    unnamed x78, local copies, waits for them, and re-layouts  38.3 us
    all_gather x1, blocking collectives, shards(): qkv_whole = lax.all_gather(qkv_share, 'seq', axis=0)  36.8 us
    all_gather x1, blocking collectives, shards(): lax.all_gather(output_share, 'seq', axis=0, tiled=True).astype(jnp.float32)  35.8 us
  transfers between devices with their start and end apart: 11, of which 2 were waited for; matrix products, arithmetic and copies ran while one was open for 13% of the time, Pallas kernels for 52%

profile of v1, /device:TPU:0, one launch (start us, length us, event | category | flops | bytes accessed | tf_op | source)
XLA Modules:
  0.0 692.9 jit_solution(16379786522424840790)
XLA Ops:
  12.2 4.1 copy.34
  16.2 4.2 copy.35
  23.7 97.3 %gather_many.1 = (bf16[8,128,2048]{2,1,0:T(8,128)(2,1)S(1)}, bf16[8,128,2048]{2,1,0:T(8,128)(2,1)S(1)}) custom-call(bf16[128,2048]{1,0:T(8,128)(2,1)S(1)} %bitcast.95, bf16[128,2048]{1,0:T(8,128)(2,1)S(1)} %bitcast.101), custom_call_target="tpu_custom_call" | custom-call | bytes 134217728 | tf_op jit(solution)/shard_map/gather_many/pallas_call | solution.py:261
  130.1 3.3 multiply_convert_fusion
  135.3 9.5 %attend.1 = (bf16[256,1024]{1,0:T(8,128)(2,1)S(1)}, f32[4,8,1024]{2,1,0:T(8,128)S(1)}, bf16[256,1024]{1,0:T(8,128)(2,1)S(1)}, bf16[64,1024]{1,0:T(8,128)(2,1)S(1)}) custom-call(bf16[384,1024]{1,0:T(8,128)(2,1)S(1)} %convolution_convert_fusion.8.qkv, f32[32,1024]{1,0:T(8,128)S(1)} %get-tuple-element.88.cosine, f32[32,1024]{1,0:T(8,128)S(1)} %get-tuple-element.87.sine, ...), custom_call_target="tpu_custom_call" | custom-call | flops 1073741824 | bytes 4194304 | tf_op jit(solution)/shard_map/attend/pallas_call | solution.py:506
  146.8 78.4 %add_branch.1 = (f32[128,2048]{1,0:T(8,128)S(1)}, bf16[8,128,2048]{2,1,0:T(8,128)(2,1)S(1)}) custom-call(bf16[8,128,2048]{2,1,0:T(8,128)(2,1)S(1)} %bitcast.94, bf16[128,2048]{1,0:T(8,128)(2,1)S(1)} %bitcast.96, f32[1,2048]{1,0:T(1,128)S(1)} %bitcast.105), custom_call_target="tpu_custom_call" | custom-call | bytes 134217728 | tf_op jit(solution)/shard_map/add_branch/pallas_call | solution.py:302
  227.3 10.4 %fusion.18 = f32[1024,1024]{0,1:T(8,128)} fusion(bf16[1024,2048]{1,0:T(8,128)(2,1)} %bitcast.108, bf16[1024,2048]{1,0:T(8,128)(2,1)} %all-gather.10.cloned.1.call-done), kind=kOutput, calls=%fused_computation.68 | convolution fusion | flops 4294967296 | bytes 12582912 | tf_op jit(solution)/shard_map/ta,ba->tb/dot_general | solution.py:648
  237.6 10.2 %fusion.2 = f32[1024,1024]{0,1:T(8,128)} fusion(bf16[1024,2048]{1,0:T(8,128)(2,1)} %bitcast.110, bf16[2048,2048]{0,1:T(8,128)(2,1)} %all-gather.8.cloned.1.call-done), kind=kOutput, calls=%fused_computation.6 | convolution fusion | flops 4294967296 | bytes 12582912 | tf_op jit(solution)/shard_map/dot_general | solution.py:652
  247.8 11.7 %multiply_convert_fusion.2 = (bf16[1024,1024]{0,1:T(8,128)(2,1)}, bf16[1024,1024]{0,1:T(8,128)(2,1)}, bf16[1024,1024]{0,1:T(8,128)(2,1)S(1)}) fusion(f32[1024,1024]{0,1:T(8,128)S(1)} %copy-done.32, f32[1024,1024]{0,1:T(8,128)} %fusion.2, bf16[1024,2048]{1,0:T(8,128)(2,1)S(1)} %bitcast.112, bf16[2048,2048]{0,1:T(8,128)(2,1)} %all-gather.8.cloned.1.call-done), kind=kOutput, calls=%fused_computation.14 | convolution fusion | flops 4310695936 | bytes 23068672 | tf_op jit(solution)/shard_map/dot_general | solution.py:652
  260.8 6.0 convolution_convert_fusion.4
  266.9 13.9 %convolution_convert_fusion = bf16[2048,2048]{1,0:T(8,128)(2,1)} fusion(bf16[1024,2048]{1,0:T(8,128)(2,1)} %bitcast.111, bf16[1024,1024]{0,1:T(8,128)(2,1)} %get-tuple-element.75, bf16[1024,1024]{0,1:T(8,128)(2,1)} %get-tuple-element.74), kind=kOutput, calls=%fused_computation.5 | convolution fusion | flops 8602517504 | bytes 16777216 | tf_op jit(solution)/shard_map/ta,tb->ab/dot_general | solution.py:644
  280.9 12.9 %convolution_convert_fusion.2 = bf16[1024,2048]{1,0:T(8,128)(2,1)S(1)} fusion(bf16[2048,2048]{0,1:T(8,128)(2,1)} %all-gather.8.cloned.1.call-done, bf16[1024,1024]{0,1:T(8,128)(2,1)} %get-tuple-element.75, bf16[1024,1024]{0,1:T(8,128)(2,1)} %get-tuple-element.74), kind=kOutput, calls=%fused_computation.19 | convolution fusion | flops 8600420352 | bytes 16777216 | tf_op jit(solution)/shard_map/ta,ba->tb/dot_general | solution.py:648
  293.9 87.5 %back_to_middle.1 = (f32[128,2048]{1,0:T(8,128)S(1)}, f32[1,2048]{1,0:T(1,128)S(1)}, bf16[8,128,2048]{2,1,0:T(8,128)(2,1)S(1)}) custom-call(bf16[8,128,2048]{2,1,0:T(8,128)(2,1)S(1)} %bitcast.99, f32[128,2048]{1,0:T(8,128)S(1)} %get-tuple-element.51.middle, f32[1,2048]{1,0:T(1,128)S(1)} %bitcast.106, bf16[128,2048]{1,0:T(8,128)(2,1)S(1)} %bitcast.102), custom_call_target="tpu_custom_call" | custom-call | bytes 134217728 | tf_op jit(solution)/shard_map/back_to_middle/pallas_call | solution.py:358
  384.2 3.5 fusion.1
  389.5 12.9 %attend_back.1 = bf16[384,1024]{1,0:T(8,128)(2,1)S(1)} custom-call(bf16[384,1024]{1,0:T(8,128)(2,1)S(1)} %copy-done.20, bf16[256,1024]{1,0:T(8,128)(2,1)S(1)} %copy-done.22, bf16[64,1024]{1,0:T(8,128)(2,1)S(1)} %get-tuple-element.53.keys, bf16[256,1024]{1,0:T(8,128)(2,1)S(1)} %copy-done.12, f32[4,8,1024]{2,1,0:T(8,128)S(1)} %get-tuple-element.54.lse, ...), custom_call_target="tpu_custom_call" | custom-call | flops 2684354560 | bytes 8388608 | tf_op jit(solution)/shard_map/attend_back/pallas_call | solution.py:617
  402.4 3.5 convolution_convert_fusion.6
  406.1 2.5 reduce-scatter.9.cloned.1.call-done
  410.7 3.9 convolution_convert_fusion.1
  414.6 32.6 %back_to_tokens.1 = (bf16[128,2048]{1,0:T(8,128)(2,1)S(1)}, f32[1,2048]{1,0:T(1,128)S(1)}) custom-call(bf16[8,128,2048]{2,1,0:T(8,128)(2,1)S(1)} %bitcast.100, bf16[128,2048]{1,0:T(8,128)(2,1)S(1)} %bitcast.97, f32[1,2048]{1,0:T(1,128)S(1)} %bitcast.107, f32[128,2048]{1,0:T(8,128)S(1)} %copy-done.9), custom_call_target="tpu_custom_call" | custom-call | bytes 67108864 | tf_op jit(solution)/shard_map/back_to_tokens/pallas_call | solution.py:398
  447.2 66.0 %psum.7 = f32[2,2048]{1,0:T(2,128)S(1)} all-reduce(f32[2,2048]{1,0:T(2,128)S(1)} %pad_maximum_fusion.9), channel_id=1, replica_groups=mesh['seq'=8,'fsdp'=16] {'seq','fsdp'}, use_global_device_ids=true, to_apply=%region_7.8 | all-reduce | flops 4096 | bytes 32768 | tf_op jit(solution)/shard_map/psum | solution.py:807
  513.3 9.5 %convolution_convert_fusion.5 = bf16[1024,2048]{1,0:T(8,128)(2,1)} fusion(bf16[1024,1024]{0,1:T(8,128)(2,1)} %copy-done.31, bf16[1024,2048]{1,0:T(8,128)(2,1)} %all-gather.10.cloned.1.call-done), kind=kOutput, calls=%fused_computation.22 | convolution fusion | flops 4297064448 | bytes 10485760 | tf_op jit(solution)/shard_map/dot_general | solution.py:652
  527.0 44.7 %finish_layer.1 = bf16[128,2048]{1,0:T(8,128)(2,1)S(1)} custom-call(bf16[8,128,2048]{2,1,0:T(8,128)(2,1)S(1)} %bitcast.98, f32[128,2048]{1,0:T(8,128)S(1)} %copy-done.6), custom_call_target="tpu_custom_call" | custom-call | bytes 67108864 | tf_op jit(solution)/shard_map/finish_layer/pallas_call | solution.py:431
  571.7 35.8 %all_gather.33 = bf16[128,2048]{1,0:T(8,128)(2,1)S(1)} all-gather(bf16[16,2048]{1,0:T(8,128)(2,1)S(1)} %collective-permute-done.2), channel_id=1, replica_groups=mesh['seq'=8,'fsdp'=16] {'seq'}, dimensions={0}, use_global_device_ids=true | all-gather | bytes 589824 | tf_op jit(solution)/shard_map/all_gather | solution.py:787
  608.6 36.8 %all-gather.1 = bf16[1024,384]{1,0:T(8,128)(2,1)S(1)} all-gather(bf16[128,384]{1,0:T(8,128)(2,1)} %reduce-scatter.5.cloned.1.call-done), channel_id=3, replica_groups=mesh['seq'=8,'fsdp'=16] {'seq'}, dimensions={0}, use_global_device_ids=true | all-gather | bytes 884736 | tf_op jit(solution)/shard_map/all_gather | solution.py:805
  648.8 3.2 slice.122
  652.1 4.9 fusion.15
  656.9 3.0 copy.53
  660.4 2.3 copy.43
  662.7 5.6 copy.47
  668.3 3.0 copy.52
  674.2 5.7 copy.46
  679.9 4.1 bitcast_convert_fusion
  (143 shorter events, 44.7 us)
Async XLA Ops:
  7.2 4.2 copy-start
  7.2 120.0 %all-gather.12.cloned.1.call-start = ((), (), s32[]{:S(2)}) async-start(), calls=%async_computation.10 | async-start | bytes 1880064 | tf_op jit(solution)/shard_map/all_gather | solution.py:709
  11.3 216.0 %all-gather.10.cloned.1.call-start = ((), (), s32[]{:S(2)}) async-start(), calls=%async_computation.5 | async-start | bytes 4456448 | tf_op jit(solution)/shard_map/all_gather | solution.py:726
  12.1 225.5 %all-gather.8.cloned.1.call-start = ((), (), s32[]{:S(2)}) async-start(), calls=%async_computation.4 | async-start | bytes 8912896 | tf_op jit(solution)/shard_map/all_gather | solution.py:719
  16.2 6.2 copy-start.30
  16.2 6.9 copy-start.28
  16.2 7.5 %copy-start.3 = (bf16[1,128,2048]{2,1,0:T(8,128)(2,1)S(1)}, bf16[1,128,2048]{2,1,0:T(8,128)(2,1)}, u32[]{:S(2)}) copy-start(bf16[1,128,2048]{2,1,0:T(8,128)(2,1)} %param.17) | copy-start | bytes 1572868
  16.2 7.5 %copy-start.7 = (bf16[1,128,2048]{2,1,0:T(8,128)(2,1)S(1)}, bf16[1,128,2048]{2,1,0:T(8,128)(2,1)}, u32[]{:S(2)}) copy-start(bf16[1,128,2048]{2,1,0:T(8,128)(2,1)} %param.28) | copy-start | bytes 1572868
  20.4 104.0 %copy-start.29 = (f32[32]{0:T(128)S(1)}, f32[32]{0:T(128)}, u32[]{:S(2)}) copy-start(f32[32]{0:T(128)} %constant.109.clone) | copy-start | bytes 388
  22.4 383.7 %reduce-scatter.11.cloned.1.call-start = ((), (), s32[]{:S(2)}) async-start(), calls=%async_computation.9 | async-start | bytes 4456448 | tf_op jit(solution)/shard_map/reduce_scatter | solution.py:759
  22.4 101.5 %collective-permute-start = (bf16[128,2048]{1,0:T(8,128)(2,1)S(1)}, bf16[128,2048]{1,0:T(8,128)(2,1)S(1)}, u32[]{:S(2)}, u32[]{:S(2)}) collective-permute-start(bf16[128,2048]{1,0:T(8,128)(2,1)S(1)} %copy-done.30), channel_id=1, source_target_pairs={{0,0},{1,1},{2,16},{3,17},{4,32},{5,33},{6,48},{7,49},{8,64},{9,65... | collective-permute-start | bytes 1572872 | tf_op jit(solution)/shard_map/ppermute | solution.py:657
  123.9 2.1 collective-permute-start.1
  127.2 18.3 %copy-start.23 = (bf16[128,2048]{1,0:T(8,128)(2,1)}, bf16[128,2048]{1,0:T(8,128)(2,1)S(1)}, u32[]{:S(2)}) copy-start(bf16[128,2048]{1,0:T(8,128)(2,1)S(1)} %get-tuple-element.81) | copy-start | bytes 1572868
  127.2 18.3 %copy-start.25 = (bf16[128,2048]{1,0:T(8,128)(2,1)}, bf16[128,2048]{1,0:T(8,128)(2,1)S(1)}, u32[]{:S(2)}) copy-start(bf16[128,2048]{1,0:T(8,128)(2,1)S(1)} %get-tuple-element.82) | copy-start | bytes 1572868
  129.2 4.2 copy-start.27
  135.2 10.3 %copy-start.19 = (bf16[384,1024]{1,0:T(8,128)(2,1)}, bf16[384,1024]{1,0:T(8,128)(2,1)S(1)}, u32[]{:S(2)}) copy-start(bf16[384,1024]{1,0:T(8,128)(2,1)S(1)} %convolution_convert_fusion.8.qkv) | copy-start | bytes 2359300
  227.3 66.6 %copy-start.5 = (f32[128,2048]{1,0:T(8,128)}, f32[128,2048]{1,0:T(8,128)S(1)}, u32[]{:S(2)}) copy-start(f32[128,2048]{1,0:T(8,128)S(1)} %get-tuple-element.51.middle) | copy-start | bytes 3145732
  237.6 10.2 %copy-start.16 = (bf16[8,128,2048]{2,1,0:T(8,128)(2,1)S(1)}, bf16[8,128,2048]{2,1,0:T(8,128)(2,1)}, u32[]{:S(2)}) copy-start(bf16[8,128,2048]{2,1,0:T(8,128)(2,1)} %copy-done.15) | copy-start | bytes 12582916
  237.6 10.2 %copy-start.32 = (f32[1024,1024]{0,1:T(8,128)S(1)}, f32[1024,1024]{0,1:T(8,128)}, u32[]{:S(2)}) copy-start(f32[1024,1024]{0,1:T(8,128)} %fusion.18) | copy-start | bytes 12582916
  247.8 13.0 %copy-start.14 = (bf16[8,128,2048]{2,1,0:T(8,128)(2,1)S(1)}, bf16[8,128,2048]{2,1,0:T(8,128)(2,1)}, u32[]{:S(2)}) copy-start(bf16[8,128,2048]{2,1,0:T(8,128)(2,1)} %copy-done.13) | copy-start | bytes 12582916
  266.9 141.7 %reduce-scatter.9.cloned.1.call-start = ((), (), s32[]{:S(2)}) async-start(), calls=%async_computation.8 | async-start | bytes 8912896 | tf_op jit(solution)/shard_map/reduce_scatter | solution.py:761
  280.9 241.9 %reduce-scatter.7.cloned.1.call-start = ((), (), s32[]{:S(2)}) async-start(), calls=%async_computation.7 | async-start | bytes 1114112 | tf_op jit(solution)/shard_map/reduce_scatter | solution.py:785
  293.9 87.5 %copy-start.11 = (bf16[256,1024]{1,0:T(8,128)(2,1)S(1)}, bf16[256,1024]{1,0:T(8,128)(2,1)}, u32[]{:S(2)}) copy-start(bf16[256,1024]{1,0:T(8,128)(2,1)} %copy-done.10) | copy-start | bytes 1572868
  384.1 224.5 %reduce-scatter.5.cloned.1.call-start = ((), (), s32[]{:S(2)}) async-start(), calls=%async_computation.6 | async-start | bytes 1671168 | tf_op jit(solution)/shard_map/reduce_scatter | solution.py:797
  384.1 3.6 copy-start.18
  384.1 3.7 copy-start.24
  384.2 3.9 copy-start.26
  406.0 242.8 %all-gather.14.cloned.1.call-start = ((), (), s32[]{:S(2)}) async-start(), calls=%async_computation.11 | async-start | bytes 7077888 | tf_op jit(solution)/shard_map/all_gather | solution.py:762
  410.7 3.9 copy-start.9
  513.3 11.5 %copy-start.6 = (f32[128,2048]{1,0:T(8,128)S(1)}, f32[128,2048]{1,0:T(8,128)}, u32[]{:S(2)}) copy-start(f32[128,2048]{1,0:T(8,128)} %copy-done.5) | copy-start | bytes 3145732
  522.8 48.9 %collective-permute-start.2 = (bf16[16,2048]{1,0:T(8,128)(2,1)}, bf16[16,2048]{1,0:T(8,128)(2,1)S(1)}, u32[]{:S(2)}, u32[]{:S(2)}) collective-permute-start(bf16[16,2048]{1,0:T(8,128)(2,1)} %reduce-scatter.7.cloned.1.call-done), channel_id=1, source_target_pairs={{0,0},{1,1},{16,2},{17,3},{32,4},{33,5},{48,6},{49,7},{64,8},{65,9... | collective-permute-start | bytes 196616 | tf_op jit(solution)/shard_map/ppermute | solution.py:662
  674.2 11.5 %copy-start.1 = (bf16[512,2048]{1,0:T(8,128)(2,1)S(1)}, bf16[512,2048]{1,0:T(8,128)(2,1)}, u32[]{:S(2)}) copy-start(bf16[512,2048]{1,0:T(8,128)(2,1)} %param.25) | copy-start | bytes 6291460
  (12 other events, 22.5 us)
Sparse Core Ops, SparseCore 0:
  11.4 38.7 all-gather.11
  52.5 52.2 all-gather.9
  107.0 74.5 all-gather.7
  267.0 65.1 reduce-scatter.10
  334.4 74.1 reduce-scatter.8
  410.8 60.9 reduce-scatter.6
  474.9 61.5 reduce-scatter.4
  539.4 101.7 all-gather.13

commit v2 on v1

--- a/solution.py
+++ b/solution.py
@@ -59,16 +59,30 @@
     return owner, near, far
 
 
-def greet(owner, peers):
+def greet(peers):
     barrier = pltpu.get_barrier_semaphore()
     for peer in peers:
-        pl.semaphore_signal(barrier, inc=1, device_id=(peer, owner), device_id_type=MESH)
+        pl.semaphore_signal(barrier, inc=1, device_id=peer, device_id_type=MESH)
     pl.semaphore_wait(barrier, len(peers))
 
 
+def along_seq(ids):
+    owner, near, far = ids
+    return [(near[1], owner), (near[3], owner), (far[0], owner)]
+
+
+def along_fsdp(ids):
+    owner, near, _ = ids
+    core, place = lax.rem(owner, 2), lax.div(owner, 2)
+    count = lax.axis_size("fsdp") // 2
+    places = [lax.rem(place + step, count) for step in range(count)]
+    mate = (near[0], owner + 1 - 2 * core)
+    return core, mate, places, [(near[0], 2 * other + core) for other in places]
+
+
 class Copies:
-    def __init__(self, owner, send, recv):
-        self.owner, self.send, self.recv = owner, send, recv
+    def __init__(self, send, recv):
+        self.send, self.recv = send, recv
         self.made = []
 
     def start(self, source, target, peer):
@@ -78,7 +92,7 @@
             dst_ref=target,
             send_sem=self.send.at[number],
             recv_sem=self.recv.at[number],
-            device_id=(peer, self.owner),
+            device_id=peer,
             device_id_type=MESH,
         )
         copy.start()
@@ -90,43 +104,58 @@
             copy.wait_send()
 
 
-def gather_blocks(ids, copies, own, out, rows, chunks):
+def by_rows(rows, chunks):
+    size = rows // chunks
+    return lambda ref, index: ref.at[pl.ds(index * size, size)]
+
+
+def by_columns(columns, chunks):
+    size = columns // chunks
+    return lambda ref, index: ref.at[:, pl.ds(index * size, size)]
+
+
+def gather_blocks(ids, copies, arrays, chunks, meanwhile=None):
+    peers = along_seq(ids)
+    to_right_of, to_left_of, to_far_of = peers
     _, near, far = ids
     me, right, opposite, left = near
     partner = far[0]
-    size = rows // chunks
     half = chunks // 2
-
-    def part(index):
-        return pl.ds(index * size, size)
-
-    to_right, to_left, to_far = {}, {}, {}
-    for step in range(chunks):
-        back = chunks - 1 - step
-        to_right[step] = copies.start(own.at[part(step)], out.at[me, part(step)], right)
-        to_left[back] = copies.start(own.at[part(back)], out.at[me, part(back)], left)
-        to_far[step] = copies.start(own.at[part(step)], out.at[me, part(step)], partner)
-    on = {}
-    for step in range(half):
-        back = chunks - 1 - step
-        to_right[step].wait_recv()
-        on[step] = copies.start(out.at[left, part(step)], out.at[left, part(step)], right)
-        to_left[back].wait_recv()
-        on[back] = copies.start(out.at[right, part(back)], out.at[right, part(back)], left)
+    to_right, to_left, to_far, on = {}, {}, {}, {}
+    for key, (own, out, cut) in enumerate(arrays):
+        for step in range(chunks):
+            back = chunks - 1 - step
+            to_right[key, step] = copies.start(cut(own, step), cut(out.at[me], step), to_right_of)
+            to_left[key, back] = copies.start(cut(own, back), cut(out.at[me], back), to_left_of)
+            to_far[key, step] = copies.start(cut(own, step), cut(out.at[me], step), to_far_of)
+    if meanwhile is not None:
+        meanwhile()
+    for key, (_, out, cut) in enumerate(arrays):
+        for step in range(half):
+            back = chunks - 1 - step
+            to_right[key, step].wait_recv()
+            block = cut(out.at[left], step)
+            on[key, step] = copies.start(block, block, to_right_of)
+            to_left[key, back].wait_recv()
+            block = cut(out.at[right], back)
+            on[key, back] = copies.start(block, block, to_left_of)
     rest = []
-    for step in range(chunks):
-        to_far[step].wait_recv()
-        block = out.at[partner, part(step)]
-        rest.append(copies.start(block, block, right))
-        rest.append(copies.start(block, block, left))
-    for step in range(half):
-        for index in (step, chunks - 1 - step):
-            on[index].wait_recv()
-            block = out.at[opposite, part(index)]
-            rest.append(copies.start(block, block, partner))
-    for step in range(half):
-        to_right[chunks - 1 - step].wait_recv()
-        to_left[step].wait_recv()
+    for key, (_, out, cut) in enumerate(arrays):
+        for step in range(chunks):
+            to_far[key, step].wait_recv()
+            block = cut(out.at[partner], step)
+            rest.append(copies.start(block, block, to_right_of))
+            rest.append(copies.start(block, block, to_left_of))
+    for key, (_, out, cut) in enumerate(arrays):
+        for step in range(half):
+            for index in (step, chunks - 1 - step):
+                on[key, index].wait_recv()
+                block = cut(out.at[opposite], index)
+                rest.append(copies.start(block, block, to_far_of))
+    for key in range(len(arrays)):
+        for step in range(half):
+            to_right[key, chunks - 1 - step].wait_recv()
+            to_left[key, step].wait_recv()
     for copy in rest:
         copy.wait_recv()
 
@@ -135,7 +164,8 @@
     return 3 * chunks + chunks + 2 * chunks + chunks
 
 
-def reduce_blocks(ids, copies, part_of, bufs, rows, chunks, done):
+def reduce_blocks(ids, copies, part_of, bufs, rows, chunks, done, meanwhile=None, later=None):
+    to_right_of, to_left_of, to_far_of = along_seq(ids)
     _, near, far = ids
     me, right, opposite, left = near
     partner, far_right, far_opposite, far_left = far
@@ -154,20 +184,26 @@
     for index in order:
         rows_of = part(index)
         one_far[index] = copies.start(
-            part_of.at[far_opposite, rows_of], from_far.at[rows_of], partner
+            part_of.at[far_opposite, rows_of], from_far.at[rows_of], to_far_of
         )
         one_right[index] = copies.start(
-            part_of.at[far_right, rows_of], from_left.at[rows_of], right
+            part_of.at[far_right, rows_of], from_left.at[rows_of], to_right_of
         )
-        one_left[index] = copies.start(part_of.at[far_left, rows_of], from_right.at[rows_of], left)
+        one_left[index] = copies.start(
+            part_of.at[far_left, rows_of], from_right.at[rows_of], to_left_of
+        )
     last_right, last_left, last_far = {}, {}, {}
     for index in range(half):
         rows_of = part(index)
-        last_right[index] = copies.start(part_of.at[right, rows_of], end_left.at[rows_of], right)
+        last_right[index] = copies.start(
+            part_of.at[right, rows_of], end_left.at[rows_of], to_right_of
+        )
         rows_of = part(chunks - 1 - index)
         last_left[chunks - 1 - index] = copies.start(
-            part_of.at[left, rows_of], end_right.at[rows_of], left
+            part_of.at[left, rows_of], end_right.at[rows_of], to_left_of
         )
+    if meanwhile is not None:
+        meanwhile()
     two = {}
     for index in order:
         rows_of = part(index)
@@ -176,7 +212,7 @@
             jnp.bfloat16
         )
         two[index] = copies.start(
-            from_far.at[rows_of], mid.at[rows_of], left if index < half else right
+            from_far.at[rows_of], mid.at[rows_of], to_left_of if index < half else to_right_of
         )
     for index in order:
         rows_of = part(index)
@@ -185,18 +221,22 @@
         from_left[rows_of] = (
             wide(from_left[rows_of]) + wide(from_right[rows_of]) + wide(part_of[partner, rows_of])
         ).astype(jnp.bfloat16)
-        last_far[index] = copies.start(from_left.at[rows_of], end_far.at[rows_of], partner)
+        last_far[index] = copies.start(
+            from_left.at[rows_of], end_far.at[rows_of], to_far_of
+        )
     for index in order:
         rows_of = part(index)
         two[index].wait_recv()
         if index < half:
             mid[rows_of] = (wide(mid[rows_of]) + wide(part_of[left, rows_of])).astype(jnp.bfloat16)
-            last_left[index] = copies.start(mid.at[rows_of], end_right.at[rows_of], left)
+            last_left[index] = copies.start(mid.at[rows_of], end_right.at[rows_of], to_left_of)
         else:
             mid[rows_of] = (wide(mid[rows_of]) + wide(part_of[right, rows_of])).astype(
                 jnp.bfloat16
             )
-            last_right[index] = copies.start(mid.at[rows_of], end_left.at[rows_of], right)
+            last_right[index] = copies.start(mid.at[rows_of], end_left.at[rows_of], to_right_of)
+    if later is not None:
+        later()
     for index in order:
         rows_of = part(index)
         last_far[index].wait_recv()
@@ -233,41 +273,32 @@
 ANYWHERE = pl.BlockSpec(memory_space=pl.ANY)
 
 
-def gather_many(blocks, number):
-    count = len(blocks)
-    rows, width = blocks[0].shape
+def gather_tokens(tokens, number):
+    rows, width = tokens.shape
     ranks = lax.axis_size("seq")
-    each = gather_copies(CHUNKS)
-
-    def kernel(*refs):
-        own, out = refs[:count], refs[count : 2 * count]
-        local, send, recv = refs[2 * count :]
+
+    def kernel(own, out, local, send, recv):
         ids = ring()
-        owner, near, far = ids
-        greet(owner, (near[1], near[3], far[0]))
-        kept = [
-            pltpu.make_async_copy(own[i], out[i].at[near[0]], local.at[i]) for i in range(count)
-        ]
-        for copy in kept:
-            copy.start()
-        copies = Copies(owner, send, recv)
-        for i in range(count):
-            gather_blocks(ids, copies, own[i], out[i], rows, CHUNKS)
+        greet(along_seq(ids))
+        kept = pltpu.make_async_copy(own, out.at[ids[1][0]], local)
+        kept.start()
+        copies = Copies(send, recv)
+        gather_blocks(ids, copies, [(own, out, by_rows(rows, CHUNKS))], CHUNKS)
         copies.finish()
-        for copy in kept:
-            copy.wait()
-
-    moved = count * ranks * rows * width * 2
+        kept.wait()
+
     return pl.pallas_call(
         kernel,
-        out_shape=[jax.ShapeDtypeStruct((ranks, rows, width), jnp.bfloat16)] * count,
-        in_specs=[ANYWHERE] * count,
-        out_specs=[ANYWHERE] * count,
-        scratch_shapes=[pltpu.SemaphoreType.DMA((count,))] + semaphores(count * each),
+        out_shape=jax.ShapeDtypeStruct((ranks, rows, width), jnp.bfloat16),
+        in_specs=[ANYWHERE],
+        out_specs=ANYWHERE,
+        scratch_shapes=[pltpu.SemaphoreType.DMA] + semaphores(gather_copies(CHUNKS)),
         compiler_params=params(number, 32),
-        cost_estimate=pl.CostEstimate(flops=0, bytes_accessed=moved * 16, transcendentals=0),
-        name="gather_many",
-    )(*blocks)
+        cost_estimate=pl.CostEstimate(
+            flops=0, bytes_accessed=ranks * rows * width * 32, transcendentals=0
+        ),
+        name="gather_tokens",
+    )(tokens)
 
 
 def mean_square(values):
@@ -276,10 +307,9 @@
 
 def branch_kernel(part_of, tokens, gain, middle, hidden, block, local, send, recv, *bufs):
     ids = ring()
-    owner, near, far = ids
     rows = tokens.shape[0]
-    greet(owner, (near[1], near[3], far[0]))
-    copies = Copies(owner, send, recv)
+    greet(along_seq(ids))
+    copies = Copies(send, recv)
 
     def done(rows_of, total):
         values = tokens[rows_of].astype(jnp.float32) + total
@@ -288,9 +318,9 @@
         block[rows_of] = (values * factor * gain[...]).astype(jnp.bfloat16)
 
     reduce_blocks(ids, copies, part_of, bufs, rows, CHUNKS, done)
-    kept = pltpu.make_async_copy(block, hidden.at[near[0]], local)
+    kept = pltpu.make_async_copy(block, hidden.at[ids[1][0]], local)
     kept.start()
-    gather_blocks(ids, copies, block, hidden, rows, CHUNKS)
+    gather_blocks(ids, copies, [(block, hidden, by_rows(rows, CHUNKS))], CHUNKS)
     copies.finish()
     kept.wait()
 
@@ -330,10 +360,9 @@
     part_of, middle, gain, cotangent, grad_middle, grad_gain, branch, block, local, send, recv, *bufs
 ):
     ids = ring()
-    owner, near, far = ids
     rows = middle.shape[0]
-    greet(owner, (near[1], near[3], far[0]))
-    copies = Copies(owner, send, recv)
+    greet(along_seq(ids))
+    copies = Copies(send, recv)
     grad_gain[...] = jnp.zeros_like(grad_gain)
 
     def done(rows_of, total):
@@ -344,9 +373,9 @@
         block[rows_of] = values.astype(jnp.bfloat16)
 
     reduce_blocks(ids, copies, part_of, bufs, rows, CHUNKS, done)
-    kept = pltpu.make_async_copy(block, branch.at[near[0]], local)
+    kept = pltpu.make_async_copy(block, branch.at[ids[1][0]], local)
     kept.start()
-    gather_blocks(ids, copies, block, branch, rows, CHUNKS)
+    gather_blocks(ids, copies, [(block, branch, by_rows(rows, CHUNKS))], CHUNKS)
     copies.finish()
     kept.wait()
 
@@ -375,71 +404,430 @@
     )(partial.reshape(ranks, rows, width), middle, gain, cotangent)
 
 
-def tokens_kernel(part_of, tokens, gain, grad_middle, out, grad_gain, send, recv, *bufs):
+def transposed(ids):
+    owner, near, _ = ids
+    return lax.div(owner, 2), 2 * near[0] + lax.rem(owner, 2)
+
+
+def tokens_kernel(
+    part_of,
+    tokens,
+    gain,
+    grad_middle,
+    qkv_parts,
+    heads_parts,
+    out,
+    grad_gain,
+    qkv_share,
+    heads_share,
+    qkv_mate,
+    heads_mate,
+    qkv_got,
+    heads_got,
+    heads_block,
+    heads_here,
+    send,
+    recv,
+    *bufs,
+):
     ids = ring()
-    owner, near, far = ids
     rows = tokens.shape[0]
-    greet(owner, (near[1], near[3], far[0]))
-    copies = Copies(owner, send, recv)
+    core, mate, places, others = along_fsdp(ids)
+    place = places[0]
+    swap = transposed(ids)
+    stays = swap[0] == ids[1][0]
+    barrier = pltpu.get_barrier_semaphore()
+    peers = along_seq(ids) + [mate] + others[1:]
+    for peer in peers:
+        pl.semaphore_signal(barrier, inc=1, device_id=peer, device_id_type=MESH)
+
+    @pl.when(jnp.logical_not(stays))
+    def _():
+        pl.semaphore_signal(barrier, inc=1, device_id=swap, device_id_type=MESH)
+        pl.semaphore_wait(barrier, len(peers) + 1)
+
+    @pl.when(stays)
+    def _():
+        pl.semaphore_wait(barrier, len(peers))
+
+    copies = Copies(send, recv)
     grad_gain[...] = jnp.zeros_like(grad_gain)
+    pair = [
+        copies.start(qkv_parts.at[:, 1 - core], qkv_mate, mate),
+        copies.start(heads_parts.at[1 - core], heads_mate, mate),
+    ]
+    pushed = []
+
+    def meanwhile():
+        for copy in pair:
+            copy.wait_recv()
+
+        def add(index, _):
+            qkv_mate[index] = (
+                qkv_mate[index].astype(jnp.float32) + qkv_parts[index, core].astype(jnp.float32)
+            ).astype(jnp.bfloat16)
+            heads_mate[index] = (
+                heads_mate[index].astype(jnp.float32)
+                + heads_parts[core, index].astype(jnp.float32)
+            ).astype(jnp.bfloat16)
+            return 0
+
+        lax.fori_loop(0, len(places), add, 0)
+        for step in range(1, len(places)):
+            pushed.append(
+                copies.start(qkv_mate.at[places[step]], qkv_got.at[step], others[step])
+            )
+            pushed.append(
+                copies.start(heads_mate.at[places[step]], heads_got.at[step], others[step])
+            )
+
+    def later():
+        for copy in pushed:
+            copy.wait_recv()
+        total = qkv_mate[place].astype(jnp.float32)
+        heads_total = heads_mate[place].astype(jnp.float32)
+        for step in range(1, len(places)):
+            total += qkv_got[step].astype(jnp.float32)
+            heads_total += heads_got[step].astype(jnp.float32)
+        qkv_share[...] = total.astype(jnp.bfloat16)
+        heads_block[...] = heads_total.astype(jnp.bfloat16)
+
+        @pl.when(jnp.logical_not(stays))
+        def _():
+            copy = pltpu.make_async_remote_copy(
+                src_ref=heads_block,
+                dst_ref=heads_here,
+                send_sem=send.at[send.shape[0] - 1],
+                recv_sem=recv.at[recv.shape[0] - 1],
+                device_id=swap,
+                device_id_type=MESH,
+            )
+            copy.start()
 
     def done(rows_of, total):
         back, terms = norm_back_rows(total, gain[...], tokens[rows_of].astype(jnp.float32))
         grad_gain[...] += jnp.sum(terms, axis=0, keepdims=True)
         out[rows_of] = (grad_middle[rows_of] + back).astype(jnp.bfloat16)
 
-    reduce_blocks(ids, copies, part_of, bufs, rows, CHUNKS, done)
+    reduce_blocks(ids, copies, part_of, bufs, rows, CHUNKS, done, meanwhile, later)
     copies.finish()
 
-
-def back_to_tokens(partial, tokens, gain, grad_middle, number):
+    @pl.when(stays)
+    def _():
+        heads_share[...] = heads_block[...]
+
+    @pl.when(jnp.logical_not(stays))
+    def _():
+        pltpu.make_async_remote_copy(
+            src_ref=heads_block,
+            dst_ref=heads_here,
+            send_sem=send.at[send.shape[0] - 1],
+            recv_sem=recv.at[recv.shape[0] - 1],
+            device_id=swap,
+            device_id_type=MESH,
+        ).wait()
+        heads_share[...] = heads_here[...]
+
+
+def back_to_tokens(partial, tokens, gain, grad_middle, qkv_grad, heads_grad, number):
     rows, width = tokens.shape
-    ranks = lax.axis_size("seq")
+    ranks, owners = lax.axis_size("seq"), lax.axis_size("fsdp")
+    places = owners // 2
+    qkv_cols, head_rows = qkv_grad.shape[1], heads_grad.shape[0] // owners
+    count = reduce_copies(CHUNKS) + 2 + 2 * (places - 1) + 1
     return pl.pallas_call(
         tokens_kernel,
         out_shape=[
             jax.ShapeDtypeStruct((rows, width), jnp.bfloat16),
             jax.ShapeDtypeStruct((1, width), jnp.float32),
+            jax.ShapeDtypeStruct((rows, qkv_cols), jnp.bfloat16),
+            jax.ShapeDtypeStruct((head_rows, width), jnp.bfloat16),
         ],
-        in_specs=[VMEM] * 4,
-        out_specs=[VMEM, VMEM],
-        scratch_shapes=semaphores(reduce_copies(CHUNKS)) + reduce_scratch(rows, width),
-        compiler_params=params(number, 32),
+        in_specs=[VMEM] * 6,
+        out_specs=[VMEM] * 4,
+        scratch_shapes=[
+            pltpu.VMEM((places, rows, qkv_cols), jnp.bfloat16),
+            pltpu.VMEM((places, head_rows, width), jnp.bfloat16),
+            pltpu.VMEM((places, rows, qkv_cols), jnp.bfloat16),
+            pltpu.VMEM((places, head_rows, width), jnp.bfloat16),
+            pltpu.VMEM((head_rows, width), jnp.bfloat16),
+            pltpu.VMEM((head_rows, width), jnp.bfloat16),
+        ]
+        + semaphores(count)
+        + reduce_scratch(rows, width),
+        compiler_params=params(number, 40),
         cost_estimate=pl.CostEstimate(
             flops=0, bytes_accessed=ranks * rows * width * 32, transcendentals=0
         ),
         name="back_to_tokens",
-    )(partial.reshape(ranks, rows, width), tokens, gain, grad_middle)
-
-
-def layer_kernel(part_of, middle, out, send, recv, *bufs):
+    )(
+        partial.reshape(ranks, rows, width),
+        tokens,
+        gain,
+        grad_middle,
+        qkv_grad.reshape(places, 2, rows, qkv_cols),
+        heads_grad.reshape(2, places, head_rows, width),
+    )
+
+
+def finish_kernel(
+    gate_up,
+    down,
+    qkv,
+    heads,
+    gain_one,
+    gain_two,
+    gate_up_all,
+    down_all,
+    qkv_all,
+    heads_all,
+    gains,
+    given,
+    from_mate,
+    summed,
+    from_places,
+    for_partner,
+    from_partner,
+    by_column,
+    local,
+    send,
+    recv,
+):
     ids = ring()
-    owner, near, far = ids
-    greet(owner, (near[1], near[3], far[0]))
-    copies = Copies(owner, send, recv)
-
-    def done(rows_of, total):
-        out[rows_of] = (middle[rows_of] + total).astype(jnp.bfloat16)
-
-    reduce_blocks(ids, copies, part_of, bufs, middle.shape[0], CHUNKS, done)
+    _, near, _ = ids
+    me = near[0]
+    side = lax.axis_size("seq") // 2
+    column = lax.rem(me, side)
+    core, mate, places, others = along_fsdp(ids)
+    to_right_of, to_left_of, to_far_of = along_seq(ids)
+    greet(along_seq(ids) + [mate] + others[1:])
+    copies = Copies(send, recv)
+    arrays = [
+        (gate_up, gate_up_all, by_rows(gate_up.shape[0], CHUNKS)),
+        (down, down_all, by_rows(down.shape[0], CHUNKS)),
+        (qkv, qkv_all, by_rows(qkv.shape[0], CHUNKS)),
+        (heads, heads_all, by_columns(heads.shape[1], CHUNKS)),
+    ]
+    kept = [
+        pltpu.make_async_copy(own, out.at[me], local.at[i]) for i, (own, out, _) in enumerate(arrays)
+    ]
+    for copy in kept:
+        copy.start()
+
+    def sum_gains():
+        lanes = given.shape[3]
+        for index in range(2 * len(places)):
+            cols = pl.ds(index * lanes, lanes)
+            given[index // 2, index % 2, 0:1] = gain_one[:, cols]
+            given[index // 2, index % 2, 1:2] = gain_two[:, cols]
+            given[index // 2, index % 2, 2:8] = jnp.zeros((6, lanes), jnp.float32)
+        copy = copies.start(given.at[:, 1 - core], from_mate, mate)
+        copy.wait_recv()
+        summed[...] = given[:, core] + from_mate[...]
+        pushed = [
+            copies.start(summed.at[places[step]], from_places.at[step], others[step])
+            for step in range(1, len(places))
+        ]
+        for copy in pushed:
+            copy.wait_recv()
+        total = summed[places[0]]
+        for step in range(1, len(places)):
+            total += from_places[step]
+        for_partner[...] = total
+        copy = copies.start(for_partner, from_partner, to_far_of)
+        copy.wait_recv()
+        by_column[column] = for_partner[...] + from_partner[...]
+        to_right = copies.start(by_column.at[column], by_column.at[column], to_right_of)
+        to_left = copies.start(by_column.at[column], by_column.at[column], to_left_of)
+        to_right.wait_recv()
+        to_left.wait_recv()
+        after = lax.rem(column + 1, side)
+        copies.start(by_column.at[after], by_column.at[after], to_left_of).wait_recv()
+        gains[...] = (by_column[0] + by_column[1]) + (by_column[2] + by_column[3])
+
+    gather_blocks(ids, copies, arrays, CHUNKS, sum_gains)
     copies.finish()
-
-
-def finish_layer(partial, middle, number):
-    rows, width = middle.shape
-    ranks = lax.axis_size("seq")
+    for copy in kept:
+        copy.wait()
+
+
+def finish_grads(gate_up, down, qkv, heads, gain_one, gain_two, number):
+    ranks, owners = lax.axis_size("seq"), lax.axis_size("fsdp")
+    blocks = (gate_up, down, qkv, heads)
+    places = owners // 2
+    lanes = gain_one.shape[1] // owners
+    size = sum(block.size for block in blocks)
+    count = len(blocks) * gather_copies(CHUNKS) + 1 + (places - 1) + 1 + 3
+
+    def table(*shape):
+        return pltpu.VMEM((*shape, 8, lanes), jnp.float32)
+
     return pl.pallas_call(
-        layer_kernel,
-        out_shape=jax.ShapeDtypeStruct((rows, width), jnp.bfloat16),
-        in_specs=[VMEM] * 2,
-        out_specs=VMEM,
-        scratch_shapes=semaphores(reduce_copies(CHUNKS)) + reduce_scratch(rows, width),
+        finish_kernel,
+        out_shape=[jax.ShapeDtypeStruct((ranks, *block.shape), block.dtype) for block in blocks]
+        + [jax.ShapeDtypeStruct((8, lanes), jnp.float32)],
+        in_specs=[ANYWHERE] * 4 + [VMEM] * 2,
+        out_specs=[ANYWHERE] * 4 + [VMEM],
+        scratch_shapes=[
+            table(places, 2),
+            table(places),
+            table(places),
+            table(places),
+            table(),
+            table(),
+            table(ranks // 2),
+            pltpu.SemaphoreType.DMA((len(blocks),)),
+        ]
+        + semaphores(count),
         compiler_params=params(number, 32),
         cost_estimate=pl.CostEstimate(
-            flops=0, bytes_accessed=ranks * rows * width * 32, transcendentals=0
+            flops=0, bytes_accessed=ranks * size * 32, transcendentals=0
         ),
-        name="finish_layer",
-    )(partial.reshape(ranks, rows, width), middle)
+        name="finish_grads",
+    )(*blocks, gain_one, gain_two)
+
+
+def merge_lanes(first, second):
+    half = first.shape[1] // 2
+    low = lax.broadcasted_iota(jnp.int32, first.shape, 1) < half
+    return (
+        jnp.where(low, first, pltpu.roll(second, half, 1)),
+        jnp.where(low, pltpu.roll(first, half, 1), second),
+    )
+
+
+def place_kernel(gate, up, down, query, pair, heads, gate_out, up_out, down_out, query_out, key_out, value_out, heads_out):
+    lanes = gate.shape[2]
+    blocks = gate.shape[0] // 2
+    for part, out in ((gate, gate_out), (up, up_out)):
+        for index in range(blocks):
+            low, high = merge_lanes(
+                part[2 * index].astype(jnp.float32), part[2 * index + 1].astype(jnp.float32)
+            )
+            out[:, pl.ds(index * lanes, lanes)] = low
+            out[:, pl.ds((blocks + index) * lanes, lanes)] = high
+    key, value = merge_lanes(pair[0].astype(jnp.float32), pair[1].astype(jnp.float32))
+    key_out[...] = key
+    value_out[...] = value
+    down_out[...] = down[0].astype(jnp.float32)
+    query_out[...] = query[0].astype(jnp.float32)
+    heads_out[...] = heads[0].astype(jnp.float32)
+
+
+def place_grads(gate_up, down, qkv, heads):
+    ranks, rows, both = gate_up.shape
+    lanes = 128
+    steps = both // 2 // lanes
+    down_rows, width = down.shape[1:]
+    head_rows = heads.shape[1]
+    query_cols = qkv.shape[2] - lanes
+    assert steps == ranks and lanes == 2 * HEAD_SIZE
+    real = jnp.float32
+    return pl.pallas_call(
+        place_kernel,
+        grid=(steps,),
+        out_shape=[
+            jax.ShapeDtypeStruct((rows, ranks * both // 2), real),
+            jax.ShapeDtypeStruct((rows, ranks * both // 2), real),
+            jax.ShapeDtypeStruct((ranks * down_rows, width), real),
+            jax.ShapeDtypeStruct((rows, ranks * query_cols), real),
+            jax.ShapeDtypeStruct((rows, ranks * HEAD_SIZE), real),
+            jax.ShapeDtypeStruct((rows, ranks * HEAD_SIZE), real),
+            jax.ShapeDtypeStruct((ranks * head_rows, width), real),
+        ],
+        in_specs=[
+            pl.BlockSpec((ranks, rows, lanes), lambda i: (0, 0, i)),
+            pl.BlockSpec((ranks, rows, lanes), lambda i: (0, 0, steps + i)),
+            pl.BlockSpec((1, down_rows, width), lambda i: (i, 0, 0)),
+            pl.BlockSpec((1, rows, query_cols), lambda i: (i, 0, 0)),
+            pl.BlockSpec((2, rows, lanes), lambda i: (i // 2, 0, query_cols // lanes)),
+            pl.BlockSpec((1, head_rows, width), lambda i: (i, 0, 0)),
+        ],
+        out_specs=[
+            pl.BlockSpec((rows, ranks * lanes), lambda i: (0, i)),
+            pl.BlockSpec((rows, ranks * lanes), lambda i: (0, i)),
+            pl.BlockSpec((down_rows, width), lambda i: (i, 0)),
+            pl.BlockSpec((rows, query_cols), lambda i: (0, i)),
+            pl.BlockSpec((rows, lanes), lambda i: (0, i // 2)),
+            pl.BlockSpec((rows, lanes), lambda i: (0, i // 2)),
+            pl.BlockSpec((head_rows, width), lambda i: (i, 0)),
+        ],
+        compiler_params=pltpu.CompilerParams(vmem_limit_bytes=32 * 2**20),
+        name="place_grads",
+    )(gate_up, gate_up, down, qkv, qkv, heads)
+
+
+def pick_kernel(
+    query, key, value, gate, up, gain_one, gain_two, qkv_out, gate_up_out, wide, narrow, sems
+):
+    rank, ranks = lax.axis_index("seq"), lax.axis_size("seq")
+    rows = query.shape[0]
+    lanes = 128
+    owners = wide.shape[1]
+    pair = lax.div(rank, 2)
+    odd = lax.rem(rank, 2)
+    query_cols = query.shape[1] // ranks
+    stride = gate.shape[1] // owners
+    count = 0
+    made = []
+
+    def fetch(source, target):
+        nonlocal count
+        copy = pltpu.make_async_copy(source, target, sems.at[count])
+        copy.start()
+        made.append(copy)
+        count += 1
+
+    fetch(
+        query.at[:, pl.ds(pl.multiple_of(rank * query_cols, lanes), query_cols)],
+        qkv_out.at[pl.ds(0, rows), pl.ds(0, query_cols)],
+    )
+    for index, source in enumerate((key, value)):
+        fetch(source.at[:, pl.ds(pl.multiple_of(pair * lanes, lanes), lanes)], narrow.at[index])
+    for which, source in enumerate((gate, up)):
+        for owner in range(owners):
+            first = pl.multiple_of(owner * stride + pair * lanes, lanes)
+            fetch(source.at[:, pl.ds(first, lanes)], wide.at[which, owner])
+    line = lax.broadcasted_iota(jnp.int32, (16, rows), 0)
+    first, second = (gain[...].astype(jnp.float32) for gain in (gain_one, gain_two))
+    gains = jnp.where(line == 0, first, jnp.where(line == 1, second, 0.0))
+    qkv_out[pl.ds(rows, 16)] = jnp.zeros((16, qkv_out.shape[1]), jnp.bfloat16)
+    qkv_out[pl.ds(rows, 16), pl.ds(0, rows)] = gains.astype(jnp.bfloat16)
+    for copy in made:
+        copy.wait()
+
+    def chosen(first, second):
+        low, high = merge_lanes(first.astype(jnp.float32), second.astype(jnp.float32))
+        return jnp.where(odd == 0, low, high).astype(jnp.bfloat16)
+
+    qkv_out[pl.ds(0, rows), pl.ds(query_cols, lanes)] = chosen(narrow[0], narrow[1])
+    for which in range(2):
+        for index in range(owners // 2):
+            cols = pl.ds((which * (owners // 2) + index) * lanes, lanes)
+            gate_up_out[:, cols] = chosen(wide[which, 2 * index], wide[which, 2 * index + 1])
+
+
+def pick_columns(query, key, value, gate, up, gain_one, gain_two):
+    rows, width = query.shape
+    ranks, owners = lax.axis_size("seq"), lax.axis_size("fsdp")
+    lanes = 128
+    assert gate.shape[1] // owners // ranks == HEAD_SIZE == lanes // 2
+    return pl.pallas_call(
+        pick_kernel,
+        out_shape=[
+            jax.ShapeDtypeStruct((rows + 16, width // ranks + lanes), jnp.bfloat16),
+            jax.ShapeDtypeStruct((rows, owners * lanes), jnp.bfloat16),
+        ],
+        in_specs=[ANYWHERE] * 5 + [VMEM] * 2,
+        out_specs=[VMEM] * 2,
+        scratch_shapes=[
+            pltpu.VMEM((2, owners, rows, lanes), jnp.bfloat16),
+            pltpu.VMEM((2, rows, lanes), jnp.bfloat16),
+            pltpu.SemaphoreType.DMA((2 * owners + 3,)),
+        ],
+        compiler_params=pltpu.CompilerParams(vmem_limit_bytes=32 * 2**20),
+        name="pick_columns",
+    )(query, key, value, gate, up, gain_one[None], gain_two[None])
 
 
 def rotate_rows(first, second, cosine, sine):
@@ -455,7 +843,7 @@
     return jnp.where(seen, 0.0, NEG)
 
 
-def forward_kernel(qkv, cosine, sine, starts, attended, lse, queries, keys, key_rows, bias):
+def attend_tiles(qkv, cosine, sine, starts, attended, lse, queries, keys, key_rows, bias):
     group = queries.shape[0] // HEAD_SIZE
     half = HEAD_SIZE // 2
     tiles = qkv.shape[1] // TILE
@@ -501,8 +889,95 @@
         lax.fori_loop(0, group, one_head, 0)
 
 
-def attend(qkv, cosine, sine, starts, group):
+def forward_kernel(
+    qkv,
+    cosine,
+    sine,
+    starts,
+    cotangent,
+    heads,
+    attended,
+    lse,
+    queries,
+    keys,
+    gathered,
+    heads_all,
+    key_rows,
+    bias,
+    local,
+    send,
+    recv,
+):
+    ids = ring()
+    rows = cotangent.shape[0]
+    core, mate, _, _ = along_fsdp(ids)
+    swap = transposed(ids)
+    stays = swap[0] == ids[1][0]
+    barrier = pltpu.get_barrier_semaphore()
+    peers = along_seq(ids) + [mate]
+    for peer in peers:
+        pl.semaphore_signal(barrier, inc=1, device_id=peer, device_id_type=MESH)
+
+    @pl.when(jnp.logical_not(stays))
+    def _():
+        pl.semaphore_signal(barrier, inc=1, device_id=swap, device_id_type=MESH)
+        pl.semaphore_wait(barrier, len(peers) + 1)
+
+    @pl.when(stays)
+    def _():
+        pl.semaphore_wait(barrier, len(peers))
+
+    last = send.shape[0] - 1
+
+    def exchange():
+        return pltpu.make_async_remote_copy(
+            src_ref=heads,
+            dst_ref=heads_all.at[core],
+            send_sem=send.at[last],
+            recv_sem=recv.at[last],
+            device_id=swap,
+            device_id_type=MESH,
+        )
+
+    def keep():
+        return pltpu.make_async_copy(heads, heads_all.at[core], local.at[1])
+
+    @pl.when(jnp.logical_not(stays))
+    def _():
+        exchange().start()
+
+    @pl.when(stays)
+    def _():
+        keep().start()
+
+    kept = pltpu.make_async_copy(cotangent, gathered.at[ids[1][0]], local.at[0])
+    kept.start()
+    copies = Copies(send, recv)
+
+    def meanwhile():
+        attend_tiles(qkv, cosine, sine, starts, attended, lse, queries, keys, key_rows, bias)
+
+        @pl.when(jnp.logical_not(stays))
+        def _():
+            exchange().wait()
+
+        @pl.when(stays)
+        def _():
+            keep().wait()
+
+        passed.append(copies.start(heads_all.at[core], heads_all.at[core], mate))
+
+    passed = []
+    gather_blocks(ids, copies, [(cotangent, gathered, by_rows(rows, CHUNKS))], CHUNKS, meanwhile)
+    passed[0].wait_recv()
+    copies.finish()
+    kept.wait()
+
+
+def attend(qkv, cosine, sine, starts, cotangent, heads, group, number):
     length = qkv.shape[1]
+    rows, width = cotangent.shape
+    ranks = lax.axis_size("seq")
     return pl.pallas_call(
         forward_kernel,
         out_shape=[
@@ -510,24 +985,28 @@
             jax.ShapeDtypeStruct((group, 8, length), jnp.float32),
             jax.ShapeDtypeStruct((group * HEAD_SIZE, length), jnp.bfloat16),
             jax.ShapeDtypeStruct((HEAD_SIZE, length), jnp.bfloat16),
+            jax.ShapeDtypeStruct((ranks, rows, width), jnp.bfloat16),
+            jax.ShapeDtypeStruct((2, *heads.shape), jnp.bfloat16),
         ],
-        in_specs=[VMEM] * 4,
-        out_specs=[VMEM] * 4,
+        in_specs=[VMEM] * 4 + [ANYWHERE] * 2,
+        out_specs=[VMEM] * 4 + [ANYWHERE] * 2,
         scratch_shapes=[
             pltpu.VMEM((length, HEAD_SIZE), jnp.bfloat16),
             pltpu.VMEM((length, TILE), jnp.float32),
-        ],
-        compiler_params=pltpu.CompilerParams(vmem_limit_bytes=32 * 2**20),
+            pltpu.SemaphoreType.DMA((2,)),
+        ]
+        + semaphores(gather_copies(CHUNKS) + 2),
+        compiler_params=params(number, 40),
         cost_estimate=pl.CostEstimate(
             flops=4 * group * length * length * HEAD_SIZE,
-            bytes_accessed=group * length * length,
+            bytes_accessed=ranks * rows * width * 32,
             transcendentals=group * length * length,
         ),
         name="attend",
-    )(qkv, cosine, sine, starts)
-
-
-def backward_kernel(
+    )(qkv, cosine, sine, starts, cotangent, heads)
+
+
+def back_tiles(
     qkv,
     queries,
     keys,
@@ -610,15 +1089,39 @@
     out[pl.ds((group + 1) * HEAD_SIZE, HEAD_SIZE)] = value_grad[...].T.astype(jnp.bfloat16)
 
 
-def attend_back(qkv, queries, keys, attended, lse, grads, cosine, sine, starts):
+def backward_kernel(*refs):
+    ins, (part_of, middle), (out, layer_out) = refs[:9], refs[9:11], refs[11:13]
+    scratch, (send, recv), bufs = refs[13:22], refs[22:24], refs[24:]
+    ids = ring()
+    greet(along_seq(ids))
+    copies = Copies(send, recv)
+
+    def meanwhile():
+        back_tiles(*ins, out, *scratch)
+
+    def done(rows_of, total):
+        layer_out[rows_of] = (middle[rows_of] + total).astype(jnp.bfloat16)
+
+    reduce_blocks(ids, copies, part_of, bufs, middle.shape[0], CHUNKS, done, meanwhile)
+    copies.finish()
+
+
+def attend_back(
+    qkv, queries, keys, attended, lse, grads, cosine, sine, starts, partial, middle, number
+):
     length = qkv.shape[1]
     group = queries.shape[0] // HEAD_SIZE
     tiles = length // TILE
+    rows, width = middle.shape
+    ranks = lax.axis_size("seq")
     return pl.pallas_call(
         backward_kernel,
-        out_shape=jax.ShapeDtypeStruct(qkv.shape, jnp.bfloat16),
-        in_specs=[VMEM] * 9,
-        out_specs=VMEM,
+        out_shape=[
+            jax.ShapeDtypeStruct(qkv.shape, jnp.bfloat16),
+            jax.ShapeDtypeStruct((rows, width), jnp.bfloat16),
+        ],
+        in_specs=[VMEM] * 11,
+        out_specs=[VMEM] * 2,
         scratch_shapes=[
             pltpu.VMEM((length, HEAD_SIZE), jnp.bfloat16),
             pltpu.VMEM((length, HEAD_SIZE), jnp.bfloat16),
@@ -629,15 +1132,29 @@
             pltpu.VMEM((length, HEAD_SIZE), jnp.float32),
             pltpu.VMEM((group * HEAD_SIZE, length), jnp.float32),
             pltpu.VMEM((tiles, TILE, TILE), jnp.float32),
-        ],
-        compiler_params=pltpu.CompilerParams(vmem_limit_bytes=40 * 2**20),
+        ]
+        + semaphores(reduce_copies(CHUNKS))
+        + reduce_scratch(rows, width),
+        compiler_params=params(number, 48),
         cost_estimate=pl.CostEstimate(
             flops=10 * group * length * length * HEAD_SIZE,
-            bytes_accessed=2 * group * length * length,
+            bytes_accessed=ranks * rows * width * 32,
             transcendentals=group * length * length,
         ),
         name="attend_back",
-    )(qkv, queries, keys, attended, lse, grads, cosine, sine, starts)
+    )(
+        qkv,
+        queries,
+        keys,
+        attended,
+        lse,
+        grads,
+        cosine,
+        sine,
+        starts,
+        partial.reshape(ranks, rows, width),
+        middle,
+    )
 
 
 def contract_rows(left, right):
@@ -650,20 +1167,6 @@
 
 def matmul(left, right):
     return jnp.dot(left, right, preferred_element_type=jnp.float32)
-
-
-def swap_heads(block):
-    pairs = [(t * 16 + g, (g // 2) * 16 + 2 * t + g % 2) for t in range(8) for g in range(16)]
-    return lax.ppermute(block, ("seq", "fsdp"), pairs)
-
-
-def swap_heads_back(block):
-    pairs = [((g // 2) * 16 + 2 * t + g % 2, t * 16 + g) for t in range(8) for g in range(16)]
-    return lax.ppermute(block, ("seq", "fsdp"), pairs)
-
-
-def swap_cores(block):
-    return lax.ppermute(block, "fsdp", [(f, f ^ 1) for f in range(16)])
 
 
 def shards(
@@ -693,35 +1196,14 @@
     segment_row = segment_ids[0]
     length = segment_row.shape[0]
 
-    def columns(weight, size):
-        return lax.dynamic_slice_in_dim(weight, rank * size, size, 1)
-
-    def ff_columns(weight):
-        split = weight.reshape(rows, owners, ranks, ff_chunk)
-        return lax.dynamic_slice_in_dim(split, rank, 1, 2).reshape(rows, owners * ff_chunk)
-
-    gains_in = jnp.zeros((16, q_cols + 2 * kv_cols), jnp.bfloat16)
-    gains_in = gains_in.at[0, :rows].set(attention_gain).at[1, :rows].set(feed_gain)
-    qkv_in = jnp.concatenate(
-        [columns(query_weight, q_cols), columns(key_matrix, kv_cols), columns(value_matrix, kv_cols)],
-        axis=1,
-    )
-    qkv_got = lax.all_gather(jnp.concatenate([qkv_in, gains_in], axis=0), "fsdp", axis=0)
+    qkv_in, gate_up_in = pick_columns(
+        query_weight, key_matrix, value_matrix, gate_weight, up_weight, attention_gain, feed_gain
+    )
+    qkv_got = lax.all_gather(qkv_in, "fsdp", axis=0)
     qkv_all = qkv_got[:, :rows].reshape(owners * rows, -1)
     gain_one = qkv_got[:, rows, :rows].reshape(1, -1).astype(jnp.float32)
     gain_two = qkv_got[:, rows + 1, :rows].reshape(1, -1).astype(jnp.float32)
-    half = swap_heads(output_weight)
-    other = swap_cores(half)
-    first = owner % 2 == 0
-    output_all = jnp.concatenate(
-        [jnp.where(first, half, other), jnp.where(first, other, half)], axis=0
-    )
-    gate_up_all = lax.all_gather(
-        jnp.concatenate([ff_columns(gate_weight), ff_columns(up_weight)], axis=1),
-        "fsdp",
-        axis=0,
-        tiled=True,
-    )
+    gate_up_all = lax.all_gather(gate_up_in, "fsdp", axis=0, tiled=True)
     ff_local = owners * ff_chunk
     down_all = lax.all_gather(
         lax.dynamic_slice_in_dim(down_weight, rank * ff_chunk, ff_chunk, 0),
@@ -732,15 +1214,17 @@
 
     starts = (jnp.arange(length, dtype=jnp.int32) - positions_of(segment_row))[None]
     cosine, sine = (table.T for table in angles_of(segment_row, HEAD_SIZE))
-    whole, grad_out = gather_many([tokens[0], cotangent[0]], 0)
-    whole = whole.reshape(length, width).astype(jnp.float32)
-    grad_out = grad_out.reshape(length, width)
+    whole = gather_tokens(tokens[0], 0).reshape(length, width).astype(jnp.float32)
     hidden_one = (whole * lax.rsqrt(mean_square(whole) + EPS) * gain_one).astype(jnp.bfloat16)
     qkv = jnp.einsum("tm,mc->ct", hidden_one, qkv_all, preferred_element_type=jnp.float32)
     qkv = qkv.astype(jnp.bfloat16)
-    attended, lse, queries, keys = attend(qkv, cosine, sine, starts, group)
+    attended, lse, queries, keys, grad_out, output_all = attend(
+        qkv, cosine, sine, starts, cotangent[0], output_weight, group, 1
+    )
+    grad_out = grad_out.reshape(length, width)
+    output_all = output_all.reshape(q_cols, width)
     middle, hidden_two = add_branch(
-        contract_rows(attended, output_all).astype(jnp.bfloat16), tokens[0], gain_two, 1
+        contract_rows(attended, output_all).astype(jnp.bfloat16), tokens[0], gain_two, 2
     )
     hidden_two = hidden_two.reshape(length, width)
 
@@ -759,77 +1243,66 @@
     down_share = lax.psum_scatter(down_grad, "fsdp", scatter_dimension=0, tiled=True)
     gate_up_grad = contract_rows(hidden_two, gate_up_grads).astype(jnp.bfloat16)
     gate_up_share = lax.psum_scatter(gate_up_grad, "fsdp", scatter_dimension=0, tiled=True)
-    ff_whole = lax.all_gather(
-        jnp.concatenate([gate_up_share, down_share], axis=0), "seq", axis=0
-    )
-    gate_up_whole = ff_whole[:, :rows]
-    down_whole = ff_whole[:, rows:].reshape(-1, width).astype(jnp.float32)
+    layer_partial = matmul(act, down_all).astype(jnp.bfloat16)
     grad_middle, grad_gain_two, grad_branch = back_to_middle(
         contract_cols(gate_up_grads, gate_up_all).astype(jnp.bfloat16),
         middle,
         gain_two,
         cotangent[0],
-        2,
+        3,
     )
     grad_branch = grad_branch.reshape(length, width)
 
     grad_attended = jnp.einsum(
         "tm,fm->ft", grad_branch, output_all, preferred_element_type=jnp.float32
     ).astype(jnp.bfloat16)
-    qkv_grads = attend_back(
-        qkv, queries, keys, attended, lse, grad_attended, cosine, sine, starts
-    )
-    output_grad = matmul(attended, grad_branch).astype(jnp.bfloat16)
-    output_grad = output_grad.reshape(2, ranks, -1, width).swapaxes(0, 1).reshape(-1, width)
-    output_share = swap_heads_back(
-        lax.psum_scatter(output_grad, "fsdp", scatter_dimension=0, tiled=True)
-    )
-    output_whole = lax.all_gather(output_share, "seq", axis=0, tiled=True).astype(jnp.float32)
-    grad_inputs, grad_gain_one = back_to_tokens(
+    qkv_grads, layer_out = attend_back(
+        qkv,
+        queries,
+        keys,
+        attended,
+        lse,
+        grad_attended,
+        cosine,
+        sine,
+        starts,
+        layer_partial,
+        middle,
+        4,
+    )
+    heads_grad = matmul(attended, grad_branch).astype(jnp.bfloat16)
+    qkv_grad = jnp.einsum(
+        "tm,ct->mc", hidden_one, qkv_grads, preferred_element_type=jnp.float32
+    ).astype(jnp.bfloat16)
+    grad_inputs, grad_gain_one, qkv_share, heads_share = back_to_tokens(
         jnp.einsum("ct,mc->tm", qkv_grads, qkv_all, preferred_element_type=jnp.float32).astype(
             jnp.bfloat16
         ),
         tokens[0],
         gain_one,
         grad_middle,
-        3,
-    )
-    qkv_share = lax.psum_scatter(
-        jnp.einsum(
-            "tm,ct->mc", hidden_one, qkv_grads, preferred_element_type=jnp.float32
-        ).astype(jnp.bfloat16),
-        "fsdp",
-        scatter_dimension=0,
-        tiled=True,
-    )
-    qkv_whole = lax.all_gather(qkv_share, "seq", axis=0)
-    layer_out = finish_layer(matmul(act, down_all).astype(jnp.bfloat16), middle, 4)
-    gain_totals = lax.psum(jnp.concatenate([grad_gain_one, grad_gain_two]), ("seq", "fsdp"))
-    gain_totals = lax.dynamic_slice_in_dim(gain_totals, owner * rows, rows, 1)
-
-    def spread(part):
-        return part.swapaxes(0, 1).reshape(rows, -1).astype(jnp.float32)
-
-    def ff_spread(part):
-        return (
-            part.reshape(ranks, rows, owners, ff_chunk)
-            .transpose(1, 2, 0, 3)
-            .reshape(rows, ff)
-            .astype(jnp.float32)
-        )
-
+        qkv_grad,
+        heads_grad,
+        5,
+    )
+    *gathered, gains = finish_grads(
+        gate_up_share, down_share, qkv_share, heads_share, grad_gain_one, grad_gain_two, 6
+    )
+    gate_grad, up_grad, down_total, query_grad, key_grad, value_grad, heads_total = place_grads(
+        *gathered
+    )
     return (
         layer_out[None],
         grad_inputs[None],
-        spread(qkv_whole[:, :, :q_cols]),
-        spread(qkv_whole[:, :, q_cols : q_cols + kv_cols]),
-        spread(qkv_whole[:, :, q_cols + kv_cols :]),
-        output_whole,
-        ff_spread(gate_up_whole[:, :, :ff_local]),
-        ff_spread(gate_up_whole[:, :, ff_local:]),
-        down_whole,
-        gain_totals[0],
-        gain_totals[1],
+        query_grad,
+        key_grad,
+        value_grad,
+        heads_total,
+        gate_grad,
+        up_grad,
+        down_total,
+        gains[0],
+        gains[1],
     )
 
 

time: 700 us -> 573 us (0.82)
  blocking collectives: 139 us -> 0 us
  Pallas kernels: 363 us -> 425 us
  local copies, waits for them, and re-layouts: 62.3 us -> 24 us
  other arithmetic: 19.8 us -> 10.7 us
    all_gather x2 -> x0, blocking collectives: 72.7 us -> none  [the longest x1 36.8 us: shards(): qkv_whole = lax.all_gather(qkv_share, 'seq', axis=0)]
    psum x1 -> x0, blocking collectives: 66 us -> none  [shards(): lax.psum(jnp.concatenate([grad_gain_one, grad_gain_two]), ('seq', 'fsdp'))]
    pallas_call x1, Pallas kernels: 9.46 us -> 51.9 us  [attend(): pl.pallas_call(forward_kernel, out_shape=[jax.ShapeDtypeStruct((group * H...]
    unnamed x78 -> x74, local copies, waits for them, and re-layouts: 38.3 us -> 20 us
    pallas_call x1, Pallas kernels: 78.4 us -> 90.7 us  [add_branch(): pl.pallas_call(branch_kernel, out_shape=[jax.ShapeDtypeStruct((rows, widt...]
    pallas_call x3 -> x5, Pallas kernels: 155 us -> 144 us  [the longest x1 64.4 us: finish_grads(): pl.pallas_call(finish_kernel, out_shape=[jax.ShapeDtypeStruct((ranks, *bl...]
    pallas_call x1, Pallas kernels: 87.5 us -> 96.9 us  [back_to_middle(): pl.pallas_call(middle_kernel, out_shape=[jax.ShapeDtypeStruct((rows, widt...]
    pallas_call x1, Pallas kernels: 32.6 us -> 41.4 us  [back_to_tokens(): pl.pallas_call(tokens_kernel, out_shape=[jax.ShapeDtypeStruct((rows, widt...]
  transfers between devices with their start and end apart: 11 -> 5, of which waited for: 2 -> 0; matrix products, arithmetic and copies ran while one was open for 13% -> 14% of each run, Pallas kernels for 52% -> 62%
where the time goes in v2:
time: 573 us; the launch traced here: 564 us
  Pallas kernels  425 us (74%)
  matrix products  89.2 us (16%)
  local copies, waits for them, and re-layouts  24 us (4%)
  between operations  14.7 us (3%)
  other arithmetic  10.7 us (2%)
    pallas_call x1, Pallas kernels, back_to_middle(): pl.pallas_call(middle_kernel, out_shape=[jax.ShapeDtypeStruct((rows, widt...  96.9 us
    pallas_call x1, Pallas kernels, add_branch(): pl.pallas_call(branch_kernel, out_shape=[jax.ShapeDtypeStruct((rows, widt...  90.7 us
    pallas_call x1, Pallas kernels, finish_grads(): pl.pallas_call(finish_kernel, out_shape=[jax.ShapeDtypeStruct((ranks, *bl...  64.4 us
    pallas_call x1, Pallas kernels, attend(): pl.pallas_call(forward_kernel, out_shape=[jax.ShapeDtypeStruct((group * H...  51.9 us
    pallas_call x1, Pallas kernels, back_to_tokens(): pl.pallas_call(tokens_kernel, out_shape=[jax.ShapeDtypeStruct((rows, widt...  41.4 us
    pallas_call x1, Pallas kernels, gather_tokens(): pl.pallas_call(kernel, out_shape=jax.ShapeDtypeStruct((ranks, rows, width...  38.8 us
    pallas_call x1, Pallas kernels, attend_back(): pl.pallas_call(backward_kernel, out_shape=[jax.ShapeDtypeStruct(qkv.shape...  31.5 us
    dot_general x3, matrix products, contract_rows(): jnp.einsum('ta,tb->ab', left, right, preferred_element_type=jnp.float32)  29.9 us
  transfers between devices with their start and end apart: 5, of which 0 were waited for; matrix products, arithmetic and copies ran while one was open for 14% of the time, Pallas kernels for 62%

profile of v2, /device:TPU:0, one launch (start us, length us, event | category | flops | bytes accessed | tf_op | source)
XLA Modules:
  0.0 564.1 jit_solution(3416425576169808600)
XLA Ops:
  7.3 1.7 copy-done.4
  9.0 1.6 copy-done.5
  10.6 1.0 copy-done.11
  14.8 1.9 pick_columns.1
  18.9 38.8 %gather_tokens.1 = bf16[8,128,2048]{2,1,0:T(8,128)(2,1)S(1)} custom-call(bf16[128,2048]{1,0:T(8,128)(2,1)S(1)} %bitcast.67), custom_call_target="tpu_custom_call" | custom-call | bytes 67108864 | tf_op jit(solution)/shard_map/gather_tokens/pallas_call | solution.py:290
  58.0 1.8 copy-done.2
  61.2 1.6 slice.49
  63.8 3.2 multiply_convert_fusion
  67.1 1.9 convolution_convert_fusion.8.qkv.refs_0_
  69.0 51.9 %attend.1 = (bf16[256,1024]{1,0:T(8,128)(2,1)S(1)}, f32[4,8,1024]{2,1,0:T(8,128)S(1)}, bf16[256,1024]{1,0:T(8,128)(2,1)S(1)}, bf16[64,1024]{1,0:T(8,128)(2,1)S(1...) custom-call(bf16[384,1024]{1,0:T(8,128)(2,1)S(1)} %convolution_convert_fusion.8.qkv.refs_0_, ...), custom_call_target="tpu_custom_call" | custom-call | flops 1073741824 | bytes 67108864 | tf_op jit(solution)/shard_map/attend/pallas_call | solution.py:981
  121.0 1.3 convolution_convert_fusion.3
  123.4 90.7 %add_branch.1 = (f32[128,2048]{1,0:T(8,128)S(1)}, bf16[8,128,2048]{2,1,0:T(8,128)(2,1)S(1)}) custom-call(bf16[8,128,2048]{2,1,0:T(8,128)(2,1)S(1)} %bitcast.66, bf16[128,2048]{1,0:T(8,128)(2,1)S(1)} %bitcast.68, f32[1,2048]{1,0:T(1,128)S(1)} %bitcast.80), custom_call_target="tpu_custom_call" | custom-call | bytes 134217728 | tf_op jit(solution)/shard_map/add_branch/pallas_call | solution.py:332
  214.1 2.0 copy-done.19
  216.2 9.9 %fusion.14 = f32[1024,1024]{0,1:T(8,128)} fusion(bf16[1024,2048]{1,0:T(8,128)(2,1)} %bitcast.90, bf16[1024,2048]{1,0:T(8,128)(2,1)} %all-gather.5.cloned.1.call-done), kind=kOutput, calls=%fused_computation.47 | convolution fusion | flops 4294967296 | bytes 12582912 | tf_op jit(solution)/shard_map/ta,ba->tb/dot_general | solution.py:1165
  226.1 10.2 %fusion.2 = f32[1024,1024]{0,1:T(8,128)} fusion(bf16[1024,2048]{1,0:T(8,128)(2,1)} %bitcast.85, bf16[2048,2048]{1,0:T(8,128)(2,1)} %all-gather.7.cloned.1.call-done), kind=kOutput, calls=%fused_computation.6 | convolution fusion | flops 4294967296 | bytes 12582912 | tf_op jit(solution)/shard_map/dot_general | solution.py:1169
  236.3 10.8 %multiply_convert_fusion.1 = (bf16[1024,1024]{0,1:T(8,128)(2,1)S(1)}, bf16[1024,1024]{0,1:T(8,128)(2,1)}, bf16[1024,1024]{0,1:T(8,128)(2,1)}) fusion(f32[1024,1024]{0,1:T(8,128)} %fusion.2, f32[1024,1024]{0,1:T(8,128)S(1)} %copy-done.33, bf16[1024,2048]{1,0:T(8,128)(2,1)S(1)} %bitcast.87, bf16[2048,2048]{1,0:T(8,128)(2,1)} %all-gather.7.cloned.1.call-done), kind=kOutput, calls=%fused_computation.11 | convolution fusion | flops 4310695936 | bytes 23068672 | tf_op jit(solution)/shard_map/dot_general | solution.py:1169
  247.0 1.4 copy-done.31
  248.4 6.0 %convolution_convert_fusion.4 = bf16[1024,2048]{1,0:T(8,128)(2,1)} fusion(bf16[1024,1024]{0,1:T(8,128)(2,1)S(1)} %get-tuple-element.75, bf16[1024,2048]{1,0:T(8,128)(2,1)S(1)} %bitcast.91), kind=kOutput, calls=%fused_computation.19 | convolution fusion | flops 4297064448 | bytes 10485760 | tf_op jit(solution)/shard_map/ta,tb->ab/dot_general | solution.py:1161
  254.5 22.6 %convolution_convert_fusion = bf16[2048,2048]{1,0:T(8,128)(2,1)} fusion(bf16[1024,2048]{1,0:T(8,128)(2,1)} %bitcast.86, bf16[1024,1024]{0,1:T(8,128)(2,1)} %get-tuple-element.77, bf16[1024,1024]{0,1:T(8,128)(2,1)} %get-tuple-element.76), kind=kOutput, calls=%fused_computation.5 | convolution fusion | flops 8602517504 | bytes 16777216 | tf_op jit(solution)/shard_map/ta,tb->ab/dot_general | solution.py:1161
  277.1 5.4 fusion.1
  282.6 11.4 %convolution_convert_fusion.2 = bf16[1024,2048]{1,0:T(8,128)(2,1)S(1)} fusion(bf16[2048,2048]{1,0:T(8,128)(2,1)} %all-gather.7.cloned.1.call-done, bf16[1024,1024]{0,1:T(8,128)(2,1)S(1)} %copy-done.35, bf16[1024,1024]{0,1:T(8,128)(2,1)S(1)} %copy-done.34), kind=kOutput, calls=%fused_computation.17 | convolution fusion | flops 8600420352 | bytes 16777216 | tf_op jit(solution)/shard_map/ta,ba->tb/dot_general | solution.py:1165
  294.0 96.9 %back_to_middle.1 = (f32[128,2048]{1,0:T(8,128)S(1)}, f32[1,2048]{1,0:T(1,128)S(1)}, bf16[8,128,2048]{2,1,0:T(8,128)(2,1)S(1)}) custom-call(bf16[8,128,2048]{2,1,0:T(8,128)(2,1)S(1)} %bitcast.71, f32[128,2048]{1,0:T(8,128)S(1)} %get-tuple-element.51.middle.refs_10_, f32[1,2048]{1,0:T(1,128)S(1)} %bitcast.81, bf16[128,2048]{1,0:T(8,128)(2,1)S(1)} %bitcast.79), custom_call_target="tpu_custom_call" | custom-call | bytes 134217728 | tf_op jit(solution)/shard_map/back_to_middle/pallas_call | solution.py:387
  391.0 1.3 convolution_convert_fusion.9.refs_5_
  393.9 6.1 %convolution_convert_fusion.5 = bf16[1024,2048]{1,0:T(8,128)(2,1)} fusion(bf16[1024,1024]{0,1:T(8,128)(2,1)S(1)} %copy-done.32, bf16[1024,2048]{1,0:T(8,128)(2,1)S(1)} %copy-done.30), kind=kOutput, calls=%fused_computation.20 | convolution fusion | flops 4297064448 | bytes 10485760 | tf_op jit(solution)/shard_map/dot_general | solution.py:1169
  400.0 31.5 %attend_back.1 = (bf16[384,1024]{1,0:T(8,128)(2,1)S(1)}, bf16[128,2048]{1,0:T(8,128)(2,1)S(1)}) custom-call(bf16[384,1024]{1,0:T(8,128)(2,1)S(1)} %convolution_convert_fusion.8.qkv.refs_0_, bf16[256,1024]{1,0:T(8,128)(2,1)S(1)} %copy-done.25, bf16[64,1024]{1,0:T(8,128)(2,1)S(1)} %get-tuple-element.44.refs_2_, ...), custom_call_target="tpu_custom_call" | custom-call | flops 2684354560 | bytes 67108864 | tf_op jit(solution)/shard_map/attend_back/pallas_call | solution.py:1117
  431.5 4.0 convolution_convert_fusion.1
  435.5 1.3 convolution_convert_fusion.7
  437.7 2.5 convolution_convert_fusion.6
  440.2 41.4 %back_to_tokens.1 = (bf16[128,2048]{1,0:T(8,128)(2,1)S(1)}, f32[1,2048]{1,0:T(1,128)S(1)}, bf16[128,384]{1,0:T(8,128)(2,1)S(1)}, bf16[16,2048]{1,0:T(8,128)(2,1)S(1)}) custom-call(bf16[8,128,2048]{2,1,0:T(8,128)(2,1)S(1)} %bitcast.70, bf16[128,2048]{1,0:T(8,128)(2,1)S(1)} %bitcast.69, f32[1,2048]{1,0:T(1,128)S(1)} %bitcast.82, ...), custom_call_target="tpu_custom_call" | custom-call | bytes 67108864 | tf_op jit(solution)/shard_map/back_to_tokens/pallas_call | solution.py:538
  481.7 1.0 copy-done.10
  483.6 64.4 %finish_grads.1 = (bf16[8,128,2048]{2,1,0:T(8,128)(2,1)S(1)}, bf16[8,64,2048]{2,1,0:T(8,128)(2,1)S(1)}, bf16[8,128,384]{2,1,0:T(8,128)(2,1)S(1)}, bf16[8,16,2048]{2,1,0:T(8,128)(2,1)S(1)}, f32[8,128]{1,0:T(8,128)S(1)}) custom-call(bf16[128,2048]{1,0:T(8,128)(2,1)S(1)} %copy-done.10, bf16[64,2048]{1,0:T(8,128)(2,1)S(1)} %copy-done.14, ...), custom_call_target="tpu_custom_call" | custom-call | bytes 121634816 | tf_op jit(solution)/shard_map/finish_grads/pallas_call | solution.py:665
  548.6 7.0 %place_grads.1 = (f32[128,8192]{1,0:T(8,128)}, f32[128,8192]{1,0:T(8,128)}, f32[512,2048]{1,0:T(8,128)}, f32[128,2048]{1,0:T(8,128)}, f32[128,512]{1,0:T(8,128)}...) custom-call(bf16[8,128,2048]{2,1,0:T(8,128)(2,1)S(1)} %get-tuple-element.61.gate.up, ...), custom_call_target="tpu_custom_call" | custom-call | tf_op jit(solution)/shard_map/place_grads/pallas_call | solution.py:726
  (98 shorter events, 14.8 us)
Async XLA Ops:
  7.2 9.6 %copy-start = (bf16[512,2048]{1,0:T(8,128)(2,1)S(1)}, bf16[512,2048]{1,0:T(8,128)(2,1)}, u32[]{:S(2)}) copy-start(bf16[512,2048]{1,0:T(8,128)(2,1)} %param.21) | copy-start | bytes 6291460
  7.2 11.7 %copy-start.3 = (bf16[1,128,2048]{2,1,0:T(8,128)(2,1)S(1)}, bf16[1,128,2048]{2,1,0:T(8,128)(2,1)}, u32[]{:S(2)}) copy-start(bf16[1,128,2048]{2,1,0:T(8,128)(2,1)} %param.13) | copy-start | bytes 1572868
  7.2 54.0 %all-gather.9.cloned.1.call-start = ((), (), s32[]{:S(2)}) async-start(), calls=%async_computation.6 | async-start | bytes 1880064 | tf_op jit(solution)/shard_map/all_gather | solution.py:1202
  7.3 1.7 copy-start.4
  9.0 1.6 copy-start.5
  14.8 3.5 copy-start.28
  16.7 199.5 %all-gather.5.cloned.1.call-start = ((), (), s32[]{:S(2)}) async-start(), calls=%async_computation.2 | async-start | bytes 4456448 | tf_op jit(solution)/shard_map/all_gather | solution.py:1208
  17.5 208.6 %all-gather.7.cloned.1.call-start = ((), (), s32[]{:S(2)}) async-start(), calls=%async_computation.3 | async-start | bytes 8912896 | tf_op jit(solution)/shard_map/all_gather | solution.py:1206
  18.3 463.4 %reduce-scatter.5.cloned.1.call-start = ((), (), s32[]{:S(2)}) async-start(), calls=%async_computation.5 | async-start | bytes 4456448 | tf_op jit(solution)/shard_map/reduce_scatter | solution.py:1243
  18.9 41.8 %copy-start.29 = (f32[32]{0:T(128)S(1)}, f32[32]{0:T(128)}, u32[]{:S(2)}) copy-start(f32[32]{0:T(128)} %constant.33.clone) | copy-start | bytes 388
  57.7 2.0 copy-start.2
  62.8 6.1 %copy-start.27 = (bf16[16,128,384]{2,1,0:T(8,128)(2,1)}, bf16[16,128,384]{2,1,0:T(8,128)(2,1)S(1)}, u32[]{:S(2)}) copy-start(bf16[16,128,384]{2,1,0:T(8,128)(2,1)S(1)} %slice.49) | copy-start | bytes 4718596
  67.0 1.9 copy-start.12
  67.0 1.9 copy-start.21
  120.9 2.4 copy-start.22
  120.9 2.5 copy-start.24
  214.1 2.0 copy-start.19
  226.1 10.2 %copy-start.20 = (bf16[8,128,2048]{2,1,0:T(8,128)(2,1)S(1)}, bf16[8,128,2048]{2,1,0:T(8,128)(2,1)}, u32[]{:S(2)}) copy-start(bf16[8,128,2048]{2,1,0:T(8,128)(2,1)} %copy-done.19) | copy-start | bytes 12582916
  226.1 10.2 %copy-start.33 = (f32[1024,1024]{0,1:T(8,128)S(1)}, f32[1024,1024]{0,1:T(8,128)}, u32[]{:S(2)}) copy-start(f32[1024,1024]{0,1:T(8,128)} %fusion.14) | copy-start | bytes 12582916
  236.3 12.1 %copy-start.23 = (bf16[8,128,2048]{2,1,0:T(8,128)(2,1)S(1)}, bf16[8,128,2048]{2,1,0:T(8,128)(2,1)}, u32[]{:S(2)}) copy-start(bf16[8,128,2048]{2,1,0:T(8,128)(2,1)} %copy-done.22) | copy-start | bytes 12582916
  254.5 227.2 %reduce-scatter.3.cloned.1.call-start = ((), (), s32[]{:S(2)}) async-start(), calls=%async_computation.4 | async-start | bytes 8912896 | tf_op jit(solution)/shard_map/reduce_scatter | solution.py:1245
  277.1 5.5 copy-start.34
  277.1 5.5 copy-start.35
  282.6 11.5 %copy-start.13 = (bf16[1,128,2048]{2,1,0:T(8,128)(2,1)S(1)}, bf16[1,128,2048]{2,1,0:T(8,128)(2,1)}, u32[]{:S(2)}) copy-start(bf16[1,128,2048]{2,1,0:T(8,128)(2,1)} %param.24) | copy-start | bytes 1572868
  294.0 97.0 %copy-start.7 = (bf16[2,128,2048]{2,1,0:T(8,128)(2,1)S(1)}, bf16[2,128,2048]{2,1,0:T(8,128)(2,1)}, u32[]{:S(2)}) copy-start(bf16[2,128,2048]{2,1,0:T(8,128)(2,1)} %copy-done.6) | copy-start | bytes 3145732
  391.0 2.2 copy-start.30
  391.0 2.9 copy-start.32
  393.9 6.1 %copy-start.25 = (bf16[256,1024]{1,0:T(8,128)(2,1)S(1)}, bf16[256,1024]{1,0:T(8,128)(2,1)}, u32[]{:S(2)}) copy-start(bf16[256,1024]{1,0:T(8,128)(2,1)} %copy-done.24) | copy-start | bytes 1572868
  431.5 4.0 copy-start.8
  435.5 2.2 copy-start.26
  548.6 7.0 %copy-start.9 = (bf16[128,2048]{1,0:T(8,128)(2,1)S(1)}, bf16[128,2048]{1,0:T(8,128)(2,1)}, u32[]{:S(2)}) copy-start(bf16[128,2048]{1,0:T(8,128)(2,1)} %copy-done.8) | copy-start | bytes 1572868
  548.6 8.6 %copy-start.1 = (bf16[512,2048]{1,0:T(8,128)(2,1)S(1)}, bf16[512,2048]{1,0:T(8,128)(2,1)}, u32[]{:S(2)}) copy-start(bf16[512,2048]{1,0:T(8,128)(2,1)} %param.21) | copy-start | bytes 6291460
  (9 other events, 8.9 us)
Sparse Core Ops, SparseCore 0:
  16.8 37.7 all-gather.8
  56.9 46.3 all-gather.4
  105.5 95.3 all-gather.6
  254.6 66.5 reduce-scatter.4
  323.5 74.2 reduce-scatter.2

commit v3 on v2

--- a/solution.py
+++ b/solution.py
@@ -46,17 +46,37 @@
 TILE = 256
 
 
-def ring():
+class Ring:
+    def __init__(self, place, count, index_of, device_of):
+        side = count // 2
+        row, col = lax.div(place, side), lax.rem(place, side)
+
+        def at(which, step):
+            return index_of(which * side + lax.rem(col + step, side))
+
+        self.near = [at(row, step) for step in range(side)]
+        self.far = [at(1 - row, step) for step in range(side)]
+        self.right = device_of(self.near[1])
+        self.left = device_of(self.near[3])
+        self.partner = device_of(self.far[0])
+        self.peers = [self.right, self.left, self.partner]
+
+
+def seq_ring():
     rank, owner = lax.axis_index("seq"), lax.axis_index("fsdp")
-    side = lax.axis_size("seq") // 2
-    row, col = lax.div(rank, side), lax.rem(rank, side)
-
-    def at(which, step):
-        return which * side + lax.rem(col + step, side)
-
-    near = [at(row, step) for step in range(side)]
-    far = [at(1 - row, step) for step in range(side)]
-    return owner, near, far
+    return Ring(rank, lax.axis_size("seq"), lambda place: place, lambda index: (index, owner))
+
+
+def fsdp_ring():
+    rank, owner = lax.axis_index("seq"), lax.axis_index("fsdp")
+    core = lax.rem(owner, 2)
+    ring = Ring(
+        lax.div(owner, 2),
+        lax.axis_size("fsdp") // 2,
+        lambda place: 2 * place + core,
+        lambda index: (rank, index),
+    )
+    return ring, core, (rank, owner + 1 - 2 * core)
 
 
 def greet(peers):
@@ -66,18 +86,40 @@
     pl.semaphore_wait(barrier, len(peers))
 
 
-def along_seq(ids):
-    owner, near, far = ids
-    return [(near[1], owner), (near[3], owner), (far[0], owner)]
-
-
-def along_fsdp(ids):
-    owner, near, _ = ids
+def greet_also(peers, other, apart):
+    barrier = pltpu.get_barrier_semaphore()
+    for peer in peers:
+        pl.semaphore_signal(barrier, inc=1, device_id=peer, device_id_type=MESH)
+
+    @pl.when(apart)
+    def _():
+        pl.semaphore_signal(barrier, inc=1, device_id=other, device_id_type=MESH)
+        pl.semaphore_wait(barrier, len(peers) + 1)
+
+    @pl.when(jnp.logical_not(apart))
+    def _():
+        pl.semaphore_wait(barrier, len(peers))
+
+
+def transposed():
+    rank, owner = lax.axis_index("seq"), lax.axis_index("fsdp")
+    other = (lax.div(owner, 2), 2 * rank + lax.rem(owner, 2))
+    return other, other[0] != rank
+
+
+def along_fsdp():
+    rank, owner = lax.axis_index("seq"), lax.axis_index("fsdp")
     core, place = lax.rem(owner, 2), lax.div(owner, 2)
     count = lax.axis_size("fsdp") // 2
     places = [lax.rem(place + step, count) for step in range(count)]
-    mate = (near[0], owner + 1 - 2 * core)
-    return core, mate, places, [(near[0], 2 * other + core) for other in places]
+    mate = (rank, owner + 1 - 2 * core)
+    return core, mate, places, [(rank, 2 * other + core) for other in places]
+
+
+def in_turn(*walks):
+    left = list(walks)
+    while left:
+        left = [walk for walk in left if next(walk, walk) is not walk]
 
 
 class Copies:
@@ -114,61 +156,95 @@
     return lambda ref, index: ref.at[:, pl.ds(index * size, size)]
 
 
-def gather_blocks(ids, copies, arrays, chunks, meanwhile=None):
-    peers = along_seq(ids)
-    to_right_of, to_left_of, to_far_of = peers
-    _, near, far = ids
-    me, right, opposite, left = near
-    partner = far[0]
+def gather_walk(ring, copies, own, out, cut, chunks, deep=False, mate=None):
+    me, right, opposite, left = ring.near
+    partner, far_right, _, far_left = ring.far
     half = chunks // 2
+    passed = []
+
+    def share(place, index):
+        if mate is not None:
+            block = cut(out.at[place], index)
+            passed.append(copies.start(block, block, mate))
+
     to_right, to_left, to_far, on = {}, {}, {}, {}
-    for key, (own, out, cut) in enumerate(arrays):
-        for step in range(chunks):
-            back = chunks - 1 - step
-            to_right[key, step] = copies.start(cut(own, step), cut(out.at[me], step), to_right_of)
-            to_left[key, back] = copies.start(cut(own, back), cut(out.at[me], back), to_left_of)
-            to_far[key, step] = copies.start(cut(own, step), cut(out.at[me], step), to_far_of)
-    if meanwhile is not None:
-        meanwhile()
-    for key, (_, out, cut) in enumerate(arrays):
+    for step in range(chunks):
+        back = chunks - 1 - step
+        to_far[step] = copies.start(cut(own, step), cut(out.at[me], step), ring.partner)
+        to_right[step] = copies.start(cut(own, step), cut(out.at[me], step), ring.right)
+        to_left[back] = copies.start(cut(own, back), cut(out.at[me], back), ring.left)
+        if mate is not None:
+            passed.append(copies.start(cut(own, step), cut(out.at[me], step), mate))
+    yield
+    for step in range(half):
+        back = chunks - 1 - step
+        to_right[step].wait_recv()
+        block = cut(out.at[left], step)
+        on[step] = copies.start(block, block, ring.right)
+        share(left, step)
+        to_left[back].wait_recv()
+        block = cut(out.at[right], back)
+        on[back] = copies.start(block, block, ring.left)
+        share(right, back)
+        yield
+    far_on, rest = {}, []
+    for step in range(chunks):
+        to_far[step].wait_recv()
+        block = cut(out.at[partner], step)
+        far_on[0, step] = copies.start(block, block, ring.right)
+        far_on[1, step] = copies.start(block, block, ring.left)
+        share(partner, step)
+        yield
+    if deep:
         for step in range(half):
             back = chunks - 1 - step
-            to_right[key, step].wait_recv()
-            block = cut(out.at[left], step)
-            on[key, step] = copies.start(block, block, to_right_of)
-            to_left[key, back].wait_recv()
-            block = cut(out.at[right], back)
-            on[key, back] = copies.start(block, block, to_left_of)
-    rest = []
-    for key, (_, out, cut) in enumerate(arrays):
-        for step in range(chunks):
-            to_far[key, step].wait_recv()
-            block = cut(out.at[partner], step)
-            rest.append(copies.start(block, block, to_right_of))
-            rest.append(copies.start(block, block, to_left_of))
-    for key, (_, out, cut) in enumerate(arrays):
-        for step in range(half):
-            for index in (step, chunks - 1 - step):
-                on[key, index].wait_recv()
+            far_on[0, step].wait_recv()
+            block = cut(out.at[far_left], step)
+            rest.append((step, copies.start(block, block, ring.right)))
+            share(far_left, step)
+            far_on[1, back].wait_recv()
+            block = cut(out.at[far_right], back)
+            rest.append((back, copies.start(block, block, ring.left)))
+            share(far_right, back)
+            yield
+    for step in range(half):
+        for index in (step, chunks - 1 - step):
+            on[index].wait_recv()
+            if not deep:
                 block = cut(out.at[opposite], index)
-                rest.append(copies.start(block, block, to_far_of))
-    for key in range(len(arrays)):
-        for step in range(half):
-            to_right[key, chunks - 1 - step].wait_recv()
-            to_left[key, step].wait_recv()
-    for copy in rest:
+                rest.append((index, copies.start(block, block, ring.partner)))
+            share(opposite, index)
+        yield
+    for step in range(half):
+        back = chunks - 1 - step
+        to_right[back].wait_recv()
+        share(left, back)
+        to_left[step].wait_recv()
+        share(right, step)
+        if deep:
+            far_on[0, back].wait_recv()
+            share(far_left, back)
+            far_on[1, step].wait_recv()
+            share(far_right, step)
+        yield
+    if not deep:
+        for copy in far_on.values():
+            copy.wait_recv()
+    for index, copy in rest:
         copy.wait_recv()
-
-
-def gather_copies(chunks):
-    return 3 * chunks + chunks + 2 * chunks + chunks
-
-
-def reduce_blocks(ids, copies, part_of, bufs, rows, chunks, done, meanwhile=None, later=None):
-    to_right_of, to_left_of, to_far_of = along_seq(ids)
-    _, near, far = ids
-    me, right, opposite, left = near
-    partner, far_right, far_opposite, far_left = far
+        share(ring.far[2], index)
+    yield
+    for copy in passed:
+        copy.wait_recv()
+
+
+def gather_copies(chunks, mate=False):
+    return 7 * chunks + (8 * chunks if mate else 0)
+
+
+def reduce_walk(ring, copies, part_of, bufs, rows, chunks, done):
+    me, right, opposite, left = ring.near
+    partner, far_right, far_opposite, far_left = ring.far
     from_left, from_right, from_far, mid, end_left, end_right, end_far = bufs
     size = rows // chunks
     half = chunks // 2
@@ -184,26 +260,25 @@
     for index in order:
         rows_of = part(index)
         one_far[index] = copies.start(
-            part_of.at[far_opposite, rows_of], from_far.at[rows_of], to_far_of
+            part_of.at[far_opposite, rows_of], from_far.at[rows_of], ring.partner
         )
         one_right[index] = copies.start(
-            part_of.at[far_right, rows_of], from_left.at[rows_of], to_right_of
+            part_of.at[far_right, rows_of], from_left.at[rows_of], ring.right
         )
         one_left[index] = copies.start(
-            part_of.at[far_left, rows_of], from_right.at[rows_of], to_left_of
+            part_of.at[far_left, rows_of], from_right.at[rows_of], ring.left
         )
     last_right, last_left, last_far = {}, {}, {}
     for index in range(half):
         rows_of = part(index)
         last_right[index] = copies.start(
-            part_of.at[right, rows_of], end_left.at[rows_of], to_right_of
+            part_of.at[right, rows_of], end_left.at[rows_of], ring.right
         )
         rows_of = part(chunks - 1 - index)
         last_left[chunks - 1 - index] = copies.start(
-            part_of.at[left, rows_of], end_right.at[rows_of], to_left_of
-        )
-    if meanwhile is not None:
-        meanwhile()
+            part_of.at[left, rows_of], end_right.at[rows_of], ring.left
+        )
+    yield
     two = {}
     for index in order:
         rows_of = part(index)
@@ -212,8 +287,9 @@
             jnp.bfloat16
         )
         two[index] = copies.start(
-            from_far.at[rows_of], mid.at[rows_of], to_left_of if index < half else to_right_of
-        )
+            from_far.at[rows_of], mid.at[rows_of], ring.left if index < half else ring.right
+        )
+        yield
     for index in order:
         rows_of = part(index)
         one_right[index].wait_recv()
@@ -222,21 +298,21 @@
             wide(from_left[rows_of]) + wide(from_right[rows_of]) + wide(part_of[partner, rows_of])
         ).astype(jnp.bfloat16)
         last_far[index] = copies.start(
-            from_left.at[rows_of], end_far.at[rows_of], to_far_of
-        )
+            from_left.at[rows_of], end_far.at[rows_of], ring.partner
+        )
+        yield
     for index in order:
         rows_of = part(index)
         two[index].wait_recv()
         if index < half:
             mid[rows_of] = (wide(mid[rows_of]) + wide(part_of[left, rows_of])).astype(jnp.bfloat16)
-            last_left[index] = copies.start(mid.at[rows_of], end_right.at[rows_of], to_left_of)
+            last_left[index] = copies.start(mid.at[rows_of], end_right.at[rows_of], ring.left)
         else:
             mid[rows_of] = (wide(mid[rows_of]) + wide(part_of[right, rows_of])).astype(
                 jnp.bfloat16
             )
-            last_right[index] = copies.start(mid.at[rows_of], end_left.at[rows_of], to_right_of)
-    if later is not None:
-        later()
+            last_right[index] = copies.start(mid.at[rows_of], end_left.at[rows_of], ring.right)
+        yield
     for index in order:
         rows_of = part(index)
         last_far[index].wait_recv()
@@ -249,10 +325,105 @@
             + wide(end_right[rows_of])
             + wide(end_far[rows_of]),
         )
+        yield
 
 
 def reduce_copies(chunks):
     return 3 * chunks + 2 * chunks + chunks + chunks
+
+
+def owners_walk(ring, core, mate, copies, grads, own, other, sems, bufs, rows, done):
+    mids, from_lefts, from_rights, from_far = bufs[:2], bufs[2:4], bufs[4:6], bufs[6]
+    half = rows // 2
+    low, high = pl.ds(0, half), pl.ds(half, half)
+    near, far = ([lax.div(index, 2) for index in row] for row in (ring.near, ring.far))
+    order = [far[2], near[2], far[1], far[3], near[1], near[3], far[0], near[0]]
+    got, kept = [], []
+    for number, place in enumerate(order):
+        got.append(copies.start(grads.at[place, 1 - core], other.at[place], mate))
+        copy = pltpu.make_async_copy(grads.at[place, core], own.at[place], sems.at[number])
+        copy.start()
+        kept.append(copy)
+    yield
+
+    def wide(ref):
+        return ref.astype(jnp.float32)
+
+    def add(*numbers):
+        for number in numbers:
+            got[number].wait_recv()
+            kept[number].wait()
+            place = order[number]
+            own[place] = (wide(own[place]) + wide(other[place])).astype(jnp.bfloat16)
+
+    add(0, 1)
+    on = []
+    for which, row in enumerate((far, near)):
+        block = own.at[row[2]]
+        on.append(copies.start(block.at[low], mids[which].at[low], ring.left))
+        on.append(copies.start(block.at[high], mids[which].at[high], ring.right))
+    yield
+    ends = []
+    for which, row in enumerate((far, near)):
+        add(2 + 2 * which, 3 + 2 * which)
+        ends.append(
+            copies.start(own.at[row[1], low], from_lefts[which].at[low], ring.right)
+        )
+        ends.append(
+            copies.start(own.at[row[3], high], from_rights[which].at[high], ring.left)
+        )
+        yield
+    add(6, 7)
+    yield
+    for which, row in enumerate((far, near)):
+        mid = mids[which]
+        on[2 * which].wait_recv()
+        mid[low] = (wide(mid[low]) + wide(own[row[3], low])).astype(jnp.bfloat16)
+        ends.append(copies.start(mid.at[low], from_rights[which].at[low], ring.left))
+        yield
+        on[2 * which + 1].wait_recv()
+        mid[high] = (wide(mid[high]) + wide(own[row[1], high])).astype(jnp.bfloat16)
+        ends.append(copies.start(mid.at[high], from_lefts[which].at[high], ring.right))
+        yield
+    last = []
+    for rows_of, numbers in ((low, (0, 4, 1, 5)), (high, (0, 4, 1, 5))):
+        if not last:
+            for number in numbers:
+                ends[number].wait_recv()
+        total = (
+            wide(from_lefts[0][rows_of])
+            + wide(from_rights[0][rows_of])
+            + wide(own[far[0], rows_of])
+        )
+        from_lefts[0][rows_of] = total.astype(jnp.bfloat16)
+        last.append(
+            copies.start(from_lefts[0].at[rows_of], from_far.at[rows_of], ring.partner)
+        )
+    yield
+    for number in (2, 6, 3, 7):
+        ends[number].wait_recv()
+    yield
+    for rows_of, copy in zip((low, high), last):
+        copy.wait_recv()
+        done(
+            rows_of,
+            wide(from_lefts[1][rows_of])
+            + wide(from_rights[1][rows_of])
+            + wide(own[near[0], rows_of])
+            + wide(from_far[rows_of]),
+        )
+        yield
+
+
+OWNERS_COPIES = 8 + 4 + 4 + 4 + 2
+
+
+def owners_scratch(places, rows, width):
+    return (
+        [pltpu.VMEM((places, rows, width), jnp.bfloat16) for _ in range(2)]
+        + [pltpu.SemaphoreType.DMA((places,))]
+        + [pltpu.VMEM((rows, width), jnp.bfloat16) for _ in range(7)]
+    )
 
 
 def reduce_scratch(rows, width):
@@ -273,32 +444,62 @@
 ANYWHERE = pl.BlockSpec(memory_space=pl.ANY)
 
 
-def gather_tokens(tokens, number):
-    rows, width = tokens.shape
-    ranks = lax.axis_size("seq")
-
-    def kernel(own, out, local, send, recv):
-        ids = ring()
-        greet(along_seq(ids))
-        kept = pltpu.make_async_copy(own, out.at[ids[1][0]], local)
-        kept.start()
+def gather_first(tokens, qkv, gate_up, number):
+    blocks = (tokens, qkv, gate_up)
+    ranks, owners = lax.axis_size("seq"), lax.axis_size("fsdp")
+
+    def kernel(tokens, qkv, gate_up, tokens_all, qkv_all, gate_up_all, local, send, recv):
+        ring = seq_ring()
+        weights_ring, _, mate = fsdp_ring()
+        greet(ring.peers + weights_ring.peers + [mate])
         copies = Copies(send, recv)
-        gather_blocks(ids, copies, [(own, out, by_rows(rows, CHUNKS))], CHUNKS)
+        kept = [
+            pltpu.make_async_copy(own, out.at[at.near[0]], local.at[index])
+            for index, (own, out, at) in enumerate(
+                (
+                    (tokens, tokens_all, ring),
+                    (qkv, qkv_all, weights_ring),
+                    (gate_up, gate_up_all, weights_ring),
+                )
+            )
+        ]
+        for copy in kept:
+            copy.start()
+        in_turn(
+            gather_walk(
+                weights_ring, copies, qkv, qkv_all, by_rows(qkv.shape[0], 2), 2, True, mate
+            ),
+            gather_walk(
+                ring, copies, tokens, tokens_all, by_rows(tokens.shape[0], CHUNKS), CHUNKS
+            ),
+            gather_walk(
+                weights_ring,
+                copies,
+                gate_up,
+                gate_up_all,
+                by_rows(gate_up.shape[0], CHUNKS),
+                CHUNKS,
+                True,
+                mate,
+            ),
+        )
         copies.finish()
-        kept.wait()
-
+        for copy in kept:
+            copy.wait()
+
+    count = gather_copies(CHUNKS) + gather_copies(CHUNKS, True) + gather_copies(2, True)
     return pl.pallas_call(
         kernel,
-        out_shape=jax.ShapeDtypeStruct((ranks, rows, width), jnp.bfloat16),
-        in_specs=[ANYWHERE],
-        out_specs=ANYWHERE,
-        scratch_shapes=[pltpu.SemaphoreType.DMA] + semaphores(gather_copies(CHUNKS)),
+        out_shape=[
+            jax.ShapeDtypeStruct((size, *block.shape), jnp.bfloat16)
+            for size, block in zip((ranks, owners, owners), blocks)
+        ],
+        in_specs=[ANYWHERE] * 3,
+        out_specs=[ANYWHERE] * 3,
+        scratch_shapes=[pltpu.SemaphoreType.DMA((3,))] + semaphores(count),
         compiler_params=params(number, 32),
-        cost_estimate=pl.CostEstimate(
-            flops=0, bytes_accessed=ranks * rows * width * 32, transcendentals=0
-        ),
-        name="gather_tokens",
-    )(tokens)
+        name="gather_first",
+    )(*blocks)
 
 
 def mean_square(values):
@@ -306,9 +507,9 @@
 
 
 def branch_kernel(part_of, tokens, gain, middle, hidden, block, local, send, recv, *bufs):
-    ids = ring()
+    ring = seq_ring()
     rows = tokens.shape[0]
-    greet(along_seq(ids))
+    greet(ring.peers)
     copies = Copies(send, recv)
 
     def done(rows_of, total):
@@ -317,10 +518,10 @@
         factor = lax.rsqrt(mean_square(values) + EPS)
         block[rows_of] = (values * factor * gain[...]).astype(jnp.bfloat16)
 
-    reduce_blocks(ids, copies, part_of, bufs, rows, CHUNKS, done)
-    kept = pltpu.make_async_copy(block, hidden.at[ids[1][0]], local)
+    in_turn(reduce_walk(ring, copies, part_of, bufs, rows, CHUNKS, done))
+    kept = pltpu.make_async_copy(block, hidden.at[ring.near[0]], local)
     kept.start()
-    gather_blocks(ids, copies, [(block, hidden, by_rows(rows, CHUNKS))], CHUNKS)
+    in_turn(gather_walk(ring, copies, block, hidden, by_rows(rows, CHUNKS), CHUNKS))
     copies.finish()
     kept.wait()
 
@@ -341,9 +542,6 @@
         + semaphores(count)
         + reduce_scratch(rows, width),
         compiler_params=params(number, 32),
-        cost_estimate=pl.CostEstimate(
-            flops=0, bytes_accessed=ranks * rows * width * 64, transcendentals=0
-        ),
         name="add_branch",
     )(partial.reshape(ranks, rows, width), tokens, gain)
 
@@ -357,11 +555,28 @@
 
 
 def middle_kernel(
-    part_of, middle, gain, cotangent, grad_middle, grad_gain, branch, block, local, send, recv, *bufs
+    part_of,
+    middle,
+    gain,
+    cotangent,
+    grads,
+    grad_middle,
+    grad_gain,
+    branch,
+    grads_share,
+    block,
+    local,
+    send,
+    recv,
+    own,
+    other,
+    sems,
+    *bufs,
 ):
-    ids = ring()
+    ring = seq_ring()
+    weights_ring, core, mate = fsdp_ring()
     rows = middle.shape[0]
-    greet(along_seq(ids))
+    greet(ring.peers + weights_ring.peers + [mate])
     copies = Copies(send, recv)
     grad_gain[...] = jnp.zeros_like(grad_gain)
 
@@ -372,41 +587,65 @@
         grad_middle[rows_of] = values
         block[rows_of] = values.astype(jnp.bfloat16)
 
-    reduce_blocks(ids, copies, part_of, bufs, rows, CHUNKS, done)
-    kept = pltpu.make_async_copy(block, branch.at[ids[1][0]], local)
-    kept.start()
-    gather_blocks(ids, copies, [(block, branch, by_rows(rows, CHUNKS))], CHUNKS)
+    def owned(rows_of, total):
+        grads_share[rows_of] = total.astype(jnp.bfloat16)
+
+    kept = pltpu.make_async_copy(block, branch.at[ring.near[0]], local)
+
+    def walk():
+        yield from reduce_walk(ring, copies, part_of, bufs[7:], rows, CHUNKS, done)
+        kept.start()
+        yield from gather_walk(ring, copies, block, branch, by_rows(rows, CHUNKS), CHUNKS)
+
+    in_turn(
+        owners_walk(
+            weights_ring,
+            core,
+            mate,
+            copies,
+            grads,
+            own,
+            other,
+            sems,
+            bufs[:7],
+            grads_share.shape[0],
+            owned,
+        ),
+        walk(),
+    )
     copies.finish()
     kept.wait()
 
 
-def back_to_middle(partial, middle, gain, cotangent, number):
+def back_to_middle(partial, middle, gain, cotangent, grads, number):
     rows, width = middle.shape
-    ranks = lax.axis_size("seq")
-    count = reduce_copies(CHUNKS) + gather_copies(CHUNKS)
+    ranks, owners = lax.axis_size("seq"), lax.axis_size("fsdp")
+    places = owners // 2
+    grad_rows, grad_cols = grads.shape[0] // owners, grads.shape[1]
+    count = reduce_copies(CHUNKS) + gather_copies(CHUNKS) + OWNERS_COPIES
     return pl.pallas_call(
         middle_kernel,
         out_shape=[
             jax.ShapeDtypeStruct((rows, width), jnp.float32),
             jax.ShapeDtypeStruct((1, width), jnp.float32),
             jax.ShapeDtypeStruct((ranks, rows, width), jnp.bfloat16),
+            jax.ShapeDtypeStruct((grad_rows, grad_cols), jnp.bfloat16),
         ],
-        in_specs=[VMEM] * 4,
-        out_specs=[VMEM, VMEM, ANYWHERE],
+        in_specs=[VMEM] * 4 + [ANYWHERE],
+        out_specs=[VMEM, VMEM, ANYWHERE, VMEM],
         scratch_shapes=[pltpu.VMEM((rows, width), jnp.bfloat16), pltpu.SemaphoreType.DMA]
         + semaphores(count)
+        + owners_scratch(places, grad_rows, grad_cols)
         + reduce_scratch(rows, width),
-        compiler_params=params(number, 32),
-        cost_estimate=pl.CostEstimate(
-            flops=0, bytes_accessed=ranks * rows * width * 64, transcendentals=0
-        ),
+        compiler_params=params(number, 48),
         name="back_to_middle",
-    )(partial.reshape(ranks, rows, width), middle, gain, cotangent)
-
-
-def transposed(ids):
-    owner, near, _ = ids
-    return lax.div(owner, 2), 2 * near[0] + lax.rem(owner, 2)
+    )(
+        partial.reshape(ranks, rows, width),
+        middle,
+        gain,
+        cotangent,
+        grads.reshape(places, 2, grad_rows, grad_cols),
+    )
 
 
 def tokens_kernel(
@@ -430,26 +669,12 @@
     recv,
     *bufs,
 ):
-    ids = ring()
+    ring = seq_ring()
     rows = tokens.shape[0]
-    core, mate, places, others = along_fsdp(ids)
+    core, mate, places, others = along_fsdp()
     place = places[0]
-    swap = transposed(ids)
-    stays = swap[0] == ids[1][0]
-    barrier = pltpu.get_barrier_semaphore()
-    peers = along_seq(ids) + [mate] + others[1:]
-    for peer in peers:
-        pl.semaphore_signal(barrier, inc=1, device_id=peer, device_id_type=MESH)
-
-    @pl.when(jnp.logical_not(stays))
-    def _():
-        pl.semaphore_signal(barrier, inc=1, device_id=swap, device_id_type=MESH)
-        pl.semaphore_wait(barrier, len(peers) + 1)
-
-    @pl.when(stays)
-    def _():
-        pl.semaphore_wait(barrier, len(peers))
-
+    swap, apart = transposed()
+    greet_also(ring.peers + [mate] + others[1:], swap, apart)
     copies = Copies(send, recv)
     grad_gain[...] = jnp.zeros_like(grad_gain)
     pair = [
@@ -492,7 +717,7 @@
         qkv_share[...] = total.astype(jnp.bfloat16)
         heads_block[...] = heads_total.astype(jnp.bfloat16)
 
-        @pl.when(jnp.logical_not(stays))
+        @pl.when(apart)
         def _():
             copy = pltpu.make_async_remote_copy(
                 src_ref=heads_block,
@@ -509,14 +734,21 @@
         grad_gain[...] += jnp.sum(terms, axis=0, keepdims=True)
         out[rows_of] = (grad_middle[rows_of] + back).astype(jnp.bfloat16)
 
-    reduce_blocks(ids, copies, part_of, bufs, rows, CHUNKS, done, meanwhile, later)
+    def weights():
+        yield
+        meanwhile()
+        for _ in range(2 * CHUNKS):
+            yield
+        later()
+
+    in_turn(reduce_walk(ring, copies, part_of, bufs, rows, CHUNKS, done), weights())
     copies.finish()
 
-    @pl.when(stays)
+    @pl.when(jnp.logical_not(apart))
     def _():
         heads_share[...] = heads_block[...]
 
-    @pl.when(jnp.logical_not(stays))
+    @pl.when(apart)
     def _():
         pltpu.make_async_remote_copy(
             src_ref=heads_block,
@@ -556,9 +788,6 @@
         + semaphores(count)
         + reduce_scratch(rows, width),
         compiler_params=params(number, 40),
-        cost_estimate=pl.CostEstimate(
-            flops=0, bytes_accessed=ranks * rows * width * 32, transcendentals=0
-        ),
         name="back_to_tokens",
     )(
         partial.reshape(ranks, rows, width),
@@ -593,14 +822,12 @@
     send,
     recv,
 ):
-    ids = ring()
-    _, near, _ = ids
-    me = near[0]
+    ring = seq_ring()
+    me = ring.near[0]
     side = lax.axis_size("seq") // 2
     column = lax.rem(me, side)
-    core, mate, places, others = along_fsdp(ids)
-    to_right_of, to_left_of, to_far_of = along_seq(ids)
-    greet(along_seq(ids) + [mate] + others[1:])
+    core, mate, places, others = along_fsdp()
+    greet(ring.peers + [mate] + others[1:])
     copies = Copies(send, recv)
     arrays = [
         (gate_up, gate_up_all, by_rows(gate_up.shape[0], CHUNKS)),
@@ -622,30 +849,38 @@
             given[index // 2, index % 2, 1:2] = gain_two[:, cols]
             given[index // 2, index % 2, 2:8] = jnp.zeros((6, lanes), jnp.float32)
         copy = copies.start(given.at[:, 1 - core], from_mate, mate)
+        yield
         copy.wait_recv()
         summed[...] = given[:, core] + from_mate[...]
         pushed = [
             copies.start(summed.at[places[step]], from_places.at[step], others[step])
             for step in range(1, len(places))
         ]
+        yield
         for copy in pushed:
             copy.wait_recv()
         total = summed[places[0]]
         for step in range(1, len(places)):
             total += from_places[step]
         for_partner[...] = total
-        copy = copies.start(for_partner, from_partner, to_far_of)
+        copy = copies.start(for_partner, from_partner, ring.partner)
+        yield
         copy.wait_recv()
         by_column[column] = for_partner[...] + from_partner[...]
-        to_right = copies.start(by_column.at[column], by_column.at[column], to_right_of)
-        to_left = copies.start(by_column.at[column], by_column.at[column], to_left_of)
+        to_right = copies.start(by_column.at[column], by_column.at[column], ring.right)
+        to_left = copies.start(by_column.at[column], by_column.at[column], ring.left)
+        yield
         to_right.wait_recv()
         to_left.wait_recv()
         after = lax.rem(column + 1, side)
-        copies.start(by_column.at[after], by_column.at[after], to_left_of).wait_recv()
+        copy = copies.start(by_column.at[after], by_column.at[after], ring.left)
+        yield
+        copy.wait_recv()
         gains[...] = (by_column[0] + by_column[1]) + (by_column[2] + by_column[3])
 
-    gather_blocks(ids, copies, arrays, CHUNKS, sum_gains)
+    in_turn(
+        *(gather_walk(ring, copies, own, out, cut, CHUNKS) for own, out, cut in arrays), sum_gains()
+    )
     copies.finish()
     for copy in kept:
         copy.wait()
@@ -680,9 +915,6 @@
         ]
         + semaphores(count),
         compiler_params=params(number, 32),
-        cost_estimate=pl.CostEstimate(
-            flops=0, bytes_accessed=ranks * size * 32, transcendentals=0
-        ),
         name="finish_grads",
     )(*blocks, gain_one, gain_two)
 
@@ -791,7 +1023,7 @@
     line = lax.broadcasted_iota(jnp.int32, (16, rows), 0)
     first, second = (gain[...].astype(jnp.float32) for gain in (gain_one, gain_two))
     gains = jnp.where(line == 0, first, jnp.where(line == 1, second, 0.0))
-    qkv_out[pl.ds(rows, 16)] = jnp.zeros((16, qkv_out.shape[1]), jnp.bfloat16)
+    qkv_out[pl.ds(rows, 32)] = jnp.zeros((32, qkv_out.shape[1]), jnp.bfloat16)
     qkv_out[pl.ds(rows, 16), pl.ds(0, rows)] = gains.astype(jnp.bfloat16)
     for copy in made:
         copy.wait()
@@ -815,7 +1047,7 @@
     return pl.pallas_call(
         pick_kernel,
         out_shape=[
-            jax.ShapeDtypeStruct((rows + 16, width // ranks + lanes), jnp.bfloat16),
+            jax.ShapeDtypeStruct((rows + 32, width // ranks + lanes), jnp.bfloat16),
             jax.ShapeDtypeStruct((rows, owners * lanes), jnp.bfloat16),
         ],
         in_specs=[ANYWHERE] * 5 + [VMEM] * 2,
@@ -896,37 +1128,24 @@
     starts,
     cotangent,
     heads,
+    down,
     attended,
     lse,
     queries,
     keys,
     gathered,
     heads_all,
+    down_all,
     key_rows,
     bias,
     local,
     send,
     recv,
 ):
-    ids = ring()
-    rows = cotangent.shape[0]
-    core, mate, _, _ = along_fsdp(ids)
-    swap = transposed(ids)
-    stays = swap[0] == ids[1][0]
-    barrier = pltpu.get_barrier_semaphore()
-    peers = along_seq(ids) + [mate]
-    for peer in peers:
-        pl.semaphore_signal(barrier, inc=1, device_id=peer, device_id_type=MESH)
-
-    @pl.when(jnp.logical_not(stays))
-    def _():
-        pl.semaphore_signal(barrier, inc=1, device_id=swap, device_id_type=MESH)
-        pl.semaphore_wait(barrier, len(peers) + 1)
-
-    @pl.when(stays)
-    def _():
-        pl.semaphore_wait(barrier, len(peers))
-
+    ring = seq_ring()
+    weights_ring, core, mate = fsdp_ring()
+    swap, apart = transposed()
+    greet_also(ring.peers + weights_ring.peers + [mate], swap, apart)
     last = send.shape[0] - 1
 
     def exchange():
@@ -940,41 +1159,64 @@
         )
 
     def keep():
-        return pltpu.make_async_copy(heads, heads_all.at[core], local.at[1])
-
-    @pl.when(jnp.logical_not(stays))
-    def _():
-        exchange().start()
-
-    @pl.when(stays)
-    def _():
-        keep().start()
-
-    kept = pltpu.make_async_copy(cotangent, gathered.at[ids[1][0]], local.at[0])
-    kept.start()
+        return pltpu.make_async_copy(heads, heads_all.at[core], local.at[2])
+
+    kept = [
+        pltpu.make_async_copy(cotangent, gathered.at[ring.near[0]], local.at[0]),
+        pltpu.make_async_copy(down, down_all.at[weights_ring.near[0]], local.at[1]),
+    ]
+    for copy in kept:
+        copy.start()
     copies = Copies(send, recv)
 
-    def meanwhile():
+    def heads_walk():
+        @pl.when(apart)
+        def _():
+            exchange().start()
+
+        @pl.when(jnp.logical_not(apart))
+        def _():
+            keep().start()
+
+        yield
         attend_tiles(qkv, cosine, sine, starts, attended, lse, queries, keys, key_rows, bias)
-
-        @pl.when(jnp.logical_not(stays))
+        yield
+
+        @pl.when(apart)
         def _():
             exchange().wait()
 
-        @pl.when(stays)
+        @pl.when(jnp.logical_not(apart))
         def _():
             keep().wait()
 
-        passed.append(copies.start(heads_all.at[core], heads_all.at[core], mate))
-
-    passed = []
-    gather_blocks(ids, copies, [(cotangent, gathered, by_rows(rows, CHUNKS))], CHUNKS, meanwhile)
-    passed[0].wait_recv()
+        copy = copies.start(heads_all.at[core], heads_all.at[core], mate)
+        for _ in range(2 * CHUNKS):
+            yield
+        copy.wait_recv()
+
+    in_turn(
+        gather_walk(
+            ring, copies, cotangent, gathered, by_rows(cotangent.shape[0], CHUNKS), CHUNKS
+        ),
+        gather_walk(
+            weights_ring,
+            copies,
+            down,
+            down_all,
+            by_rows(down.shape[0], CHUNKS),
+            CHUNKS,
+            True,
+            mate,
+        ),
+        heads_walk(),
+    )
     copies.finish()
-    kept.wait()
-
-
-def attend(qkv, cosine, sine, starts, cotangent, heads, group, number):
+    for copy in kept:
+        copy.wait()
+
+
+def attend(qkv, cosine, sine, starts, cotangent, heads, down, group, number):
     length = qkv.shape[1]
     rows, width = cotangent.shape
     ranks = lax.axis_size("seq")
@@ -987,23 +1229,19 @@
             jax.ShapeDtypeStruct((HEAD_SIZE, length), jnp.bfloat16),
             jax.ShapeDtypeStruct((ranks, rows, width), jnp.bfloat16),
             jax.ShapeDtypeStruct((2, *heads.shape), jnp.bfloat16),
+            jax.ShapeDtypeStruct((lax.axis_size("fsdp"), *down.shape), jnp.bfloat16),
         ],
-        in_specs=[VMEM] * 4 + [ANYWHERE] * 2,
-        out_specs=[VMEM] * 4 + [ANYWHERE] * 2,
+        in_specs=[VMEM] * 4 + [ANYWHERE] * 3,
+        out_specs=[VMEM] * 4 + [ANYWHERE] * 3,
         scratch_shapes=[
             pltpu.VMEM((length, HEAD_SIZE), jnp.bfloat16),
             pltpu.VMEM((length, TILE), jnp.float32),
-            pltpu.SemaphoreType.DMA((2,)),
+            pltpu.SemaphoreType.DMA((3,)),
         ]
-        + semaphores(gather_copies(CHUNKS) + 2),
+        + semaphores(gather_copies(CHUNKS) + gather_copies(CHUNKS, True) + 2),
         compiler_params=params(number, 40),
-        cost_estimate=pl.CostEstimate(
-            flops=4 * group * length * length * HEAD_SIZE,
-            bytes_accessed=ranks * rows * width * 32,
-            transcendentals=group * length * length,
-        ),
         name="attend",
-    )(qkv, cosine, sine, starts, cotangent, heads)
+    )(qkv, cosine, sine, starts, cotangent, heads, down)
 
 
 def back_tiles(
@@ -1090,38 +1328,79 @@
 
 
 def backward_kernel(*refs):
-    ins, (part_of, middle), (out, layer_out) = refs[:9], refs[9:11], refs[11:13]
-    scratch, (send, recv), bufs = refs[13:22], refs[22:24], refs[24:]
-    ids = ring()
-    greet(along_seq(ids))
+    ins, (part_of, middle, grads), (out, layer_out, grads_share) = (
+        refs[:9],
+        refs[9:12],
+        refs[12:15],
+    )
+    scratch, (send, recv), (own, other, sems) = refs[15:24], refs[24:26], refs[26:29]
+    bufs = refs[29:]
+    ring = seq_ring()
+    weights_ring, core, mate = fsdp_ring()
+    greet(ring.peers + weights_ring.peers + [mate])
     copies = Copies(send, recv)
 
-    def meanwhile():
+    def compute():
+        yield
         back_tiles(*ins, out, *scratch)
 
     def done(rows_of, total):
         layer_out[rows_of] = (middle[rows_of] + total).astype(jnp.bfloat16)
 
-    reduce_blocks(ids, copies, part_of, bufs, middle.shape[0], CHUNKS, done, meanwhile)
+    def owned(rows_of, total):
+        grads_share[rows_of] = total.astype(jnp.bfloat16)
+
+    in_turn(
+        owners_walk(
+            weights_ring,
+            core,
+            mate,
+            copies,
+            grads,
+            own,
+            other,
+            sems,
+            bufs[:7],
+            grads_share.shape[0],
+            owned,
+        ),
+        reduce_walk(ring, copies, part_of, bufs[7:], middle.shape[0], CHUNKS, done),
+        compute(),
+    )
     copies.finish()
 
 
 def attend_back(
-    qkv, queries, keys, attended, lse, grads, cosine, sine, starts, partial, middle, number
+    qkv,
+    queries,
+    keys,
+    attended,
+    lse,
+    grads,
+    cosine,
+    sine,
+    starts,
+    partial,
+    middle,
+    down_grad,
+    number,
 ):
     length = qkv.shape[1]
     group = queries.shape[0] // HEAD_SIZE
     tiles = length // TILE
     rows, width = middle.shape
-    ranks = lax.axis_size("seq")
+    ranks, owners = lax.axis_size("seq"), lax.axis_size("fsdp")
+    places = owners // 2
+    grad_rows = down_grad.shape[0] // owners
     return pl.pallas_call(
         backward_kernel,
         out_shape=[
             jax.ShapeDtypeStruct(qkv.shape, jnp.bfloat16),
             jax.ShapeDtypeStruct((rows, width), jnp.bfloat16),
+            jax.ShapeDtypeStruct((grad_rows, width), jnp.bfloat16),
         ],
-        in_specs=[VMEM] * 11,
-        out_specs=[VMEM] * 2,
+        in_specs=[VMEM] * 11 + [ANYWHERE],
+        out_specs=[VMEM] * 3,
         scratch_shapes=[
             pltpu.VMEM((length, HEAD_SIZE), jnp.bfloat16),
             pltpu.VMEM((length, HEAD_SIZE), jnp.bfloat16),
@@ -1133,14 +1412,10 @@
             pltpu.VMEM((group * HEAD_SIZE, length), jnp.float32),
             pltpu.VMEM((tiles, TILE, TILE), jnp.float32),
         ]
-        + semaphores(reduce_copies(CHUNKS))
+        + semaphores(reduce_copies(CHUNKS) + OWNERS_COPIES)
+        + owners_scratch(places, grad_rows, width)
         + reduce_scratch(rows, width),
         compiler_params=params(number, 48),
-        cost_estimate=pl.CostEstimate(
-            flops=10 * group * length * length * HEAD_SIZE,
-            bytes_accessed=ranks * rows * width * 32,
-            transcendentals=group * length * length,
-        ),
         name="attend_back",
     )(
         qkv,
@@ -1154,6 +1429,7 @@
         starts,
         partial.reshape(ranks, rows, width),
         middle,
+        down_grad.reshape(places, 2, grad_rows, width),
     )
 
 
@@ -1199,28 +1475,24 @@
     qkv_in, gate_up_in = pick_columns(
         query_weight, key_matrix, value_matrix, gate_weight, up_weight, attention_gain, feed_gain
     )
-    qkv_got = lax.all_gather(qkv_in, "fsdp", axis=0)
+    whole, qkv_got, gate_up_all = gather_first(tokens[0], qkv_in, gate_up_in, 0)
+    gate_up_all = gate_up_all.reshape(width, -1)
     qkv_all = qkv_got[:, :rows].reshape(owners * rows, -1)
     gain_one = qkv_got[:, rows, :rows].reshape(1, -1).astype(jnp.float32)
     gain_two = qkv_got[:, rows + 1, :rows].reshape(1, -1).astype(jnp.float32)
-    gate_up_all = lax.all_gather(gate_up_in, "fsdp", axis=0, tiled=True)
     ff_local = owners * ff_chunk
-    down_all = lax.all_gather(
-        lax.dynamic_slice_in_dim(down_weight, rank * ff_chunk, ff_chunk, 0),
-        "fsdp",
-        axis=0,
-        tiled=True,
-    )
+    down_in = lax.dynamic_slice_in_dim(down_weight, rank * ff_chunk, ff_chunk, 0)
 
     starts = (jnp.arange(length, dtype=jnp.int32) - positions_of(segment_row))[None]
     cosine, sine = (table.T for table in angles_of(segment_row, HEAD_SIZE))
-    whole = gather_tokens(tokens[0], 0).reshape(length, width).astype(jnp.float32)
+    whole = whole.reshape(length, width).astype(jnp.float32)
     hidden_one = (whole * lax.rsqrt(mean_square(whole) + EPS) * gain_one).astype(jnp.bfloat16)
     qkv = jnp.einsum("tm,mc->ct", hidden_one, qkv_all, preferred_element_type=jnp.float32)
     qkv = qkv.astype(jnp.bfloat16)
-    attended, lse, queries, keys, grad_out, output_all = attend(
-        qkv, cosine, sine, starts, cotangent[0], output_weight, group, 1
-    )
+    attended, lse, queries, keys, grad_out, output_all, down_all = attend(
+        qkv, cosine, sine, starts, cotangent[0], output_weight, down_in, group, 1
+    )
+    down_all = down_all.reshape(ff_local, width)
     grad_out = grad_out.reshape(length, width)
     output_all = output_all.reshape(q_cols, width)
     middle, hidden_two = add_branch(
@@ -1240,15 +1512,14 @@
     grad_up = (grad_act * silu_gate).astype(jnp.bfloat16)
     gate_up_grads = jnp.concatenate([grad_gate, grad_up], axis=1)
     down_grad = contract_rows(act, grad_out).astype(jnp.bfloat16)
-    down_share = lax.psum_scatter(down_grad, "fsdp", scatter_dimension=0, tiled=True)
     gate_up_grad = contract_rows(hidden_two, gate_up_grads).astype(jnp.bfloat16)
-    gate_up_share = lax.psum_scatter(gate_up_grad, "fsdp", scatter_dimension=0, tiled=True)
     layer_partial = matmul(act, down_all).astype(jnp.bfloat16)
-    grad_middle, grad_gain_two, grad_branch = back_to_middle(
+    grad_middle, grad_gain_two, grad_branch, gate_up_share = back_to_middle(
         contract_cols(gate_up_grads, gate_up_all).astype(jnp.bfloat16),
         middle,
         gain_two,
         cotangent[0],
+        gate_up_grad,
         3,
     )
     grad_branch = grad_branch.reshape(length, width)
@@ -1256,7 +1527,7 @@
     grad_attended = jnp.einsum(
         "tm,fm->ft", grad_branch, output_all, preferred_element_type=jnp.float32
     ).astype(jnp.bfloat16)
-    qkv_grads, layer_out = attend_back(
+    qkv_grads, layer_out, down_share = attend_back(
         qkv,
         queries,
         keys,
@@ -1268,6 +1539,7 @@
         starts,
         layer_partial,
         middle,
+        down_grad,
         4,
     )
     heads_grad = matmul(attended, grad_branch).astype(jnp.bfloat16)

time: 573 us -> 546 us (0.953)
  between operations: 14.7 us -> 1.18 us
  local copies, waits for them, and re-layouts: 24 us -> 18 us
    pallas_call x1, Pallas kernels: 90.7 us -> 66.4 us  [add_branch(): pl.pallas_call(branch_kernel, out_shape=[jax.ShapeDtypeStruct((rows, widt...]
    pallas_call x2, Pallas kernels: 40.8 us -> 56.7 us  [the longest x1 55.6 us: gather_first(): pl.pallas_call(kernel, out_shape=[jax.ShapeDtypeStruct((size, *block.shap...]
    pallas_call x1, Pallas kernels: 31.5 us -> 46.3 us  [attend_back(): pl.pallas_call(backward_kernel, out_shape=[jax.ShapeDtypeStruct(qkv.shape...]
    pallas_call x1, Pallas kernels: 96.9 us -> 88.6 us  [back_to_middle(): pl.pallas_call(middle_kernel, out_shape=[jax.ShapeDtypeStruct((rows, widt...]
    dot_general x3, matrix products: 29.9 us -> 22.5 us  [contract_rows(): jnp.einsum('ta,tb->ab', left, right, preferred_element_type=jnp.float32)]
    unnamed x74 -> x52, local copies, waits for them, and re-layouts: 20 us -> 17 us
  transfers between devices with their start and end apart: 5 -> 0, of which waited for: 0 -> 0; matrix products, arithmetic and copies ran while one was open for 14% -> 0% of each run, Pallas kernels for 62% -> 0%
where the time goes in v3:
time: 546 us; the launch traced here: 537 us
  Pallas kernels  426 us (78%)
  matrix products  84.3 us (15%)
  local copies, waits for them, and re-layouts  18 us (3%)
  other arithmetic  7.52 us (1%)
    pallas_call x1, Pallas kernels, back_to_middle(): pl.pallas_call(middle_kernel, out_shape=[jax.ShapeDtypeStruct((rows, widt...  88.6 us
    pallas_call x1, Pallas kernels, add_branch(): pl.pallas_call(branch_kernel, out_shape=[jax.ShapeDtypeStruct((rows, widt...  66.4 us
    pallas_call x1, Pallas kernels, finish_grads(): pl.pallas_call(finish_kernel, out_shape=[jax.ShapeDtypeStruct((ranks, *bl...  65.9 us
    pallas_call x1, Pallas kernels, gather_first(): pl.pallas_call(kernel, out_shape=[jax.ShapeDtypeStruct((size, *block.shap...  55.6 us
    pallas_call x1, Pallas kernels, attend(): pl.pallas_call(forward_kernel, out_shape=[jax.ShapeDtypeStruct((group * H...  54.9 us
    pallas_call x1, Pallas kernels, attend_back(): pl.pallas_call(backward_kernel, out_shape=[jax.ShapeDtypeStruct(qkv.shape...  46.3 us
    pallas_call x1, Pallas kernels, back_to_tokens(): pl.pallas_call(tokens_kernel, out_shape=[jax.ShapeDtypeStruct((rows, widt...  40.2 us
    dot_general x4, matrix products, matmul(): return jnp.dot(left, right, preferred_element_type=jnp.float32)  30.7 us

profile of v3, /device:TPU:0, one launch (start us, length us, event | category | flops | bytes accessed | tf_op | source)
XLA Modules:
  0.0 537.1 jit_solution(12117854005862227363)
XLA Ops:
  0.7 0.9 compare_reduce_fusion
  2.3 1.2 multiply_sine_fusion
  3.5 1.6 copy-done.3
  5.1 1.6 copy-done.4
  6.7 1.0 copy-done.7
  10.9 1.1 pick_columns.1
  12.0 55.6 %gather_first.1 = (bf16[8,128,2048]{2,1,0:T(8,128)(2,1)S(1)}, bf16[16,160,384]{2,1,0:T(8,128)(2,1)S(1)}, bf16[16,128,2048]{2,1,0:T(8,128)(2,1)S(1)}) custom-call(bf16[128,2048]{1,0:T(8,128)(2,1)S(1)} %bitcast.72, bf16[160,384]{1,0:T(8,128)(2,1)S(1)} %get-tuple-element.48.qkv, bf16[128,2048]{1,0:T(8,128)(2,1)S(1)} %get-tuple-element.49.gate_up), custom_call_target="tpu_custom_call" | custom-call | tf_op jit(solution)/shard_map/gather_first/pallas_call | solution.py:491
  67.7 3.3 copy-done.12
  72.1 3.0 fusion.1
  75.1 1.0 multiply_convert_fusion
  76.1 1.8 convolution_convert_fusion.8.qkv.refs_0_
  78.0 54.9 %attend.1 = (bf16[256,1024]{1,0:T(8,128)(2,1)S(1)}, f32[4,8,1024]{2,1,0:T(8,128)S(1)}, bf16[256,1024]{1,0:T(8,128)(2,1)S(1)}, bf16[64,1024]{1,0:T(8,128)(2,1)S(1...) custom-call(bf16[384,1024]{1,0:T(8,128)(2,1)S(1)} %convolution_convert_fu, ...), custom_call_target="tpu_custom_call" | custom-call | tf_op jit(solution)/shard_map/attend/pallas_call | solution.py:1223
  132.9 1.9 copy-done.13
  134.9 1.3 convolution_convert_fusion.3
  137.0 66.4 %add_branch.1 = (f32[128,2048]{1,0:T(8,128)S(1)}, bf16[8,128,2048]{2,1,0:T(8,128)(2,1)S(1)}) custom-call(bf16[8,128,2048]{2,1,0:T(8,128)(2,1)S(1)} %bitcast.71, bf16[128,2048]{1,0:T(8,128)(2,1)S(1)} %bitcast.73, f32[1,2048]{1,0:T(1,128)S(1)} %get-tuple-element.91.gain), custom_call_target="tpu_custom_call" | custom-call | tf_op jit(solution)/shard_map/add_branch/pallas_call | solution.py:533
  203.5 2.0 copy-done.17
  205.5 8.5 %fusion.2 = f32[1024,1024]{0,1:T(8,128)} fusion(bf16[1024,2048]{1,0:T(8,128)(2,1)} %bitcast.95, bf16[2048,2048]{1,0:T(8,128)(2,1)S(1)} %bitcast.90), kind=kOutput, calls=%fused_computation.6 | convolution fusion | flops 4294967296 | bytes 12582912 | tf_op jit(solution)/shard_map/dot_general | solution.py:1445
  214.0 6.3 %fusion.13 = f32[1024,1024]{0,1:T(8,128)} fusion(bf16[1024,2048]{1,0:T(8,128)(2,1)S(1)} %bitcast.94, bf16[1024,2048]{1,0:T(8,128)(2,1)S(1)} %bitcast.91), kind=kOutput, calls=%fused_computation.46 | convolution fusion | flops 4294967296 | bytes 12582912 | tf_op jit(solution)/shard_map/ta,ba->tb/dot_general | solution.py:1441
  220.2 12.4 %multiply_convert_fusion.1 = (bf16[1024,1024]{0,1:T(8,128)(2,1)S(1)}, bf16[1024,1024]{0,1:T(8,128)(2,1)}, bf16[1024,1024]{0,1:T(8,128)(2,1)}) fusion(f32[1024,1024]{0,1:T(8,128)} %fusion.2, f32[1024,1024]{0,1:T(8,128)} %fusion.13, bf16[1024,2048]{1,0:T(8,128)(2,1)} %bitcast.96, bf16[2048,2048]{1,0:T(8,128)(2,1)} %bitcast.86), kind=kOutput, calls=%fused_computation.11 | convolution fusion | flops 4310695936 | bytes 23068672 | tf_op jit(solution)/shard_map/dot_general | solution.py:1445
  232.7 14.5 %convolution_convert_fusion.2 = bf16[1024,2048]{1,0:T(8,128)(2,1)} fusion(bf16[2048,2048]{1,0:T(8,128)(2,1)} %bitcast.87, bf16[1024,1024]{0,1:T(8,128)(2,1)} %get-tuple-element.89, bf16[1024,1024]{0,1:T(8,128)(2,1)} %get-tuple-element.88), kind=kOutput, calls=%fused_computation.17 | convolution fusion | flops 8600420352 | bytes 16777216 | tf_op jit(solution)/shard_map/ta,ba->tb/dot_general | solution.py:1441
  247.2 8.2 %convolution_convert_fusion.4 = bf16[1024,2048]{1,0:T(8,128)(2,1)} fusion(bf16[1024,1024]{0,1:T(8,128)(2,1)S(1)} %get-tuple-element.87, bf16[1024,2048]{1,0:T(8,128)(2,1)} %bitcast.93), kind=kOutput, calls=%fused_computation.19 | convolution fusion | flops 4297064448 | bytes 10485760 | tf_op jit(solution)/shard_map/ta,tb->ab/dot_general | solution.py:1437
  255.4 6.2 %convolution_convert_fusion.5 = bf16[1024,2048]{1,0:T(8,128)(2,1)} fusion(bf16[1024,1024]{0,1:T(8,128)(2,1)S(1)} %get-tuple-element.87, bf16[1024,2048]{1,0:T(8,128)(2,1)S(1)} %bitcast.92), kind=kOutput, calls=%fused_computation.20 | convolution fusion | flops 4297064448 | bytes 10485760 | tf_op jit(solution)/shard_map/dot_general | solution.py:1445
  261.6 13.0 %convolution_convert_fusion = bf16[2048,2048]{1,0:T(8,128)(2,1)} fusion(bf16[1024,2048]{1,0:T(8,128)(2,1)S(1)} %bitcast.97, bf16[1024,1024]{0,1:T(8,128)(2,1)} %get-tuple-element.89, bf16[1024,1024]{0,1:T(8,128)(2,1)S(1)} %copy-done.22), kind=kOutput, calls=%fused_computation.5 | convolution fusion | flops 8602517504 | bytes 16777216 | tf_op jit(solution)/shard_map/ta,tb->ab/dot_general | solution.py:1437
  274.6 88.6 %back_to_middle.1 = (f32[128,2048]{1,0:T(8,128)S(1)}, f32[1,2048]{1,0:T(1,128)S(1)}, bf16[8,128,2048]{2,1,0:T(8,128)(2,1)}, bf16[128,2048]{1,0:T(8,128)(2,1)S(1)}) custom-call(bf16[8,128,2048]{2,1,0:T(8,128)(2,1)} %bitcast.99, f32[128,2048]{1,0:T(8,128)S(1)} %get-tuple-element.61.middle.refs_10_, f32[1,2048]{1,0:T(1,128)S(1)} %get-tuple-element.91.gain, ...), custom_call_target="tpu_custom_call" | custom-call | tf_op jit(solution)/shard_map/back_to_middle/pallas_call | solution.py:626
  363.2 3.6 convolution_convert_fusion.9.refs_5_
  366.8 46.3 %attend_back.1 = (bf16[384,1024]{1,0:T(8,128)(2,1)S(1)}, bf16[128,2048]{1,0:T(8,128)(2,1)S(1)}, bf16[64,2048]{1,0:T(8,128)(2,1)S(1)}) custom-call(bf16[384,1024]{1,0:T(8,128)(2,1)S(1)} %convolution_convert_fusion.8.qkv.refs_0_, bf16[256,1024]{1,0:T(8,128)(2,1)S(1)} %get-tuple-element.52.refs_1_, bf16[64,1024]{1,0:T(8,128)(2,1)S(1)} %get-tuple-element.53.refs_2_, ...), custom_call_target="tpu_custom_call" | custom-call | tf_op jit(solution)/shard_map/attend_back/pallas_call | solution.py:1395
  413.2 3.6 convolution_convert_fusion.7
  416.8 2.5 convolution_convert_fusion.6
  419.2 2.4 convolution_convert_fusion.1
  421.7 40.2 %back_to_tokens.1 = (bf16[128,2048]{1,0:T(8,128)(2,1)S(1)}, f32[1,2048]{1,0:T(1,128)S(1)}, bf16[128,384]{1,0:T(8,128)(2,1)S(1)}, bf16[16,2048]{1,0:T(8,128)(2,1)S(1)}) custom-call(bf16[8,128,2048]{2,1,0:T(8,128)(2,1)S(1)} %bitcast.75, bf16[128,2048]{1,0:T(8,128)(2,1)S(1)} %bitcast.74, f32[1,2048]{1,0:T(1,128)S(1)} %get-tuple-element.90.gain, ...), custom_call_target="tpu_custom_call" | custom-call | tf_op jit(solution)/shard_map/back_to_tokens/pallas_call | solution.py:770
  461.9 65.9 %finish_grads.1 = (bf16[8,128,2048]{2,1,0:T(8,128)(2,1)S(1)}, bf16[8,64,2048]{2,1,0:T(8,128)(2,1)S(1)}, bf16[8,128,384]{2,1,0:T(8,128)(2,1)S(1)}, bf16[8,16,2048]{2,1,0:T(8,128)(2,1)S(1)}, f32[8,128]{1,0:T(8,128)S(1)}) custom-call(bf16[128,2048]{1,0:T(8,128)(2,1)S(1)} %get-tuple-element.67.gate_up, bf16[64,2048]{1,0:T(8,128)(2,1)S(1)} %get-tuple-element.68.down, ...), custom_call_target="tpu_custom_call" | custom-call | tf_op jit(solution)/shard_map/finish_grads/pallas_call | solution.py:900
  528.3 7.0 %place_grads.1 = (f32[128,8192]{1,0:T(8,128)}, f32[128,8192]{1,0:T(8,128)}, f32[512,2048]{1,0:T(8,128)}, f32[128,2048]{1,0:T(8,128)}, f32[128,512]{1,0:T(8,128)}...) custom-call(bf16[8,128,2048]{2,1,0:T(8,128)(2,1)S(1)} %get-tuple-element.73.gate.up, ...), custom_call_target="tpu_custom_call" | custom-call | tf_op jit(solution)/shard_map/place_grads/pallas_call | solution.py:958
  (60 shorter events, 8.0 us)
Async XLA Ops:
  0.6 2.8 copy-start
  0.7 11.4 %copy-start.2 = (bf16[1,128,2048]{2,1,0:T(8,128)(2,1)S(1)}, bf16[1,128,2048]{2,1,0:T(8,128)(2,1)}, u32[]{:S(2)}) copy-start(bf16[1,128,2048]{2,1,0:T(8,128)(2,1)} %param.13) | copy-start | bytes 1572868
  3.5 1.6 copy-start.3
  5.1 1.6 copy-start.4
  6.7 1.0 copy-start.7
  7.8 0.9 copy-start.8
  8.7 0.9 copy-start.9
  9.6 0.7 copy-start.10
  10.2 0.7 copy-start.11
  67.7 3.3 copy-start.12
  72.1 4.0 copy-start.20
  76.1 1.9 copy-start.5
  76.1 1.9 copy-start.6
  78.0 127.5 %slice-start = ((s8[8388608]{0:T(1024)(128)(4,1)}), s8[4194304]{0:T(1024)(128)(4,1)S(1)}, s32[]{:S(2)}) async-start(s8[8388608]{0:T(1024)(128)(4,1)} %bitcast.88), calls=%async_computation | async-start | bytes 8388608
  132.9 1.9 copy-start.13
  134.9 2.1 copy-start.15
  134.9 70.6 %slice-start.1 = ((s8[8388608]{0:T(1024)(128)(4,1)}), s8[4194304]{0:T(1024)(128)(4,1)S(1)}, s32[]{:S(2)}) async-start(s8[8388608]{0:T(1024)(128)(4,1)} %bitcast.88), calls=%async_computation.1 | async-start | bytes 8388608
  203.5 2.0 copy-start.17
  205.5 8.5 %copy-start.14 = (bf16[16,64,2048]{2,1,0:T(8,128)(2,1)S(1)}, bf16[16,64,2048]{2,1,0:T(8,128)(2,1)}, u32[]{:S(2)}) copy-start(bf16[16,64,2048]{2,1,0:T(8,128)(2,1)} %copy-done.13) | copy-start | bytes 12582916
  205.5 8.5 %copy-start.16 = (bf16[8,128,2048]{2,1,0:T(8,128)(2,1)S(1)}, bf16[8,128,2048]{2,1,0:T(8,128)(2,1)}, u32[]{:S(2)}) copy-start(bf16[8,128,2048]{2,1,0:T(8,128)(2,1)} %copy-done.15) | copy-start | bytes 12582916
  255.4 6.2 %copy-start.18 = (bf16[8,128,2048]{2,1,0:T(8,128)(2,1)S(1)}, bf16[8,128,2048]{2,1,0:T(8,128)(2,1)}, u32[]{:S(2)}) copy-start(bf16[8,128,2048]{2,1,0:T(8,128)(2,1)} %copy-done.17) | copy-start | bytes 12582916
  255.4 6.2 %copy-start.22 = (bf16[1024,1024]{0,1:T(8,128)(2,1)S(1)}, bf16[1024,1024]{0,1:T(8,128)(2,1)}, u32[]{:S(2)}) copy-start(bf16[1024,1024]{0,1:T(8,128)(2,1)} %get-tuple-element.88) | copy-start | bytes 6291460
  413.1 3.6 copy-start.19
  416.8 2.5 copy-start.21
  528.3 8.6 %copy-start.1 = (bf16[512,2048]{1,0:T(8,128)(2,1)S(1)}, bf16[512,2048]{1,0:T(8,128)(2,1)}, u32[]{:S(2)}) copy-start(bf16[512,2048]{1,0:T(8,128)(2,1)} %param.21) | copy-start | bytes 6291460

commit v4 on v3

--- a/solution.py
+++ b/solution.py
@@ -49,6 +49,7 @@
 class Ring:
     def __init__(self, place, count, index_of, device_of):
         side = count // 2
+        self.place = place
         row, col = lax.div(place, side), lax.rem(place, side)
 
         def at(which, step):
@@ -107,19 +108,25 @@
     return other, other[0] != rank
 
 
-def along_fsdp():
-    rank, owner = lax.axis_index("seq"), lax.axis_index("fsdp")
-    core, place = lax.rem(owner, 2), lax.div(owner, 2)
-    count = lax.axis_size("fsdp") // 2
-    places = [lax.rem(place + step, count) for step in range(count)]
-    mate = (rank, owner + 1 - 2 * core)
-    return core, mate, places, [(rank, 2 * other + core) for other in places]
-
-
-def in_turn(*walks):
+def in_step(*walks):
     left = list(walks)
     while left:
         left = [walk for walk in left if next(walk, walk) is not walk]
+        yield
+
+
+def beside(main, *sides):
+    sides = [(walk, list(places)) for walk, places in sides]
+    step = 0
+    for _ in main:
+        for walk, places in sides:
+            while places and places[0] <= step:
+                places.pop(0)
+                next(walk, None)
+        step += 1
+    for walk, _ in sides:
+        for _ in walk:
+            pass
 
 
 class Copies:
@@ -332,27 +339,24 @@
     return 3 * chunks + 2 * chunks + chunks + chunks
 
 
-def owners_walk(ring, core, mate, copies, grads, own, other, sems, bufs, rows, done):
+def owners_walk(ring, mate, copies, produce, own, other, bufs, rows, done):
     mids, from_lefts, from_rights, from_far = bufs[:2], bufs[2:4], bufs[4:6], bufs[6]
     half = rows // 2
     low, high = pl.ds(0, half), pl.ds(half, half)
     near, far = ([lax.div(index, 2) for index in row] for row in (ring.near, ring.far))
     order = [far[2], near[2], far[1], far[3], near[1], near[3], far[0], near[0]]
-    got, kept = [], []
-    for number, place in enumerate(order):
-        got.append(copies.start(grads.at[place, 1 - core], other.at[place], mate))
-        copy = pltpu.make_async_copy(grads.at[place, core], own.at[place], sems.at[number])
-        copy.start()
-        kept.append(copy)
-    yield
+    awaited = []
+    for place in order:
+        awaited.append(produce(place))
+        yield
 
     def wide(ref):
         return ref.astype(jnp.float32)
 
     def add(*numbers):
         for number in numbers:
-            got[number].wait_recv()
-            kept[number].wait()
+            for wait in awaited[number]:
+                wait()
             place = order[number]
             own[place] = (wide(own[place]) + wide(other[place])).astype(jnp.bfloat16)
 
@@ -415,15 +419,30 @@
         yield
 
 
-OWNERS_COPIES = 8 + 4 + 4 + 4 + 2
+OWNERS_COPIES = 4 + 4 + 4 + 2
 
 
 def owners_scratch(places, rows, width):
-    return (
-        [pltpu.VMEM((places, rows, width), jnp.bfloat16) for _ in range(2)]
-        + [pltpu.SemaphoreType.DMA((places,))]
-        + [pltpu.VMEM((rows, width), jnp.bfloat16) for _ in range(7)]
-    )
+    return [pltpu.VMEM((places, rows, width), jnp.bfloat16) for _ in range(2)] + [
+        pltpu.VMEM((rows, width), jnp.bfloat16) for _ in range(7)
+    ]
+
+
+def fetched(copies, core, mate, pieces, own, other, sems):
+    count = 0
+
+    def produce(place):
+        nonlocal count
+        waits = []
+        for piece, part in pieces:
+            sent = copies.start(piece(place, 1 - core), part(other.at[place]), mate)
+            copy = pltpu.make_async_copy(piece(place, core), part(own.at[place]), sems.at[count])
+            copy.start()
+            count += 1
+            waits += [sent.wait_recv, copy.wait]
+        return waits
+
+    return produce
 
 
 def reduce_scratch(rows, width):
@@ -444,59 +463,45 @@
 ANYWHERE = pl.BlockSpec(memory_space=pl.ANY)
 
 
-def gather_first(tokens, qkv, gate_up, number):
-    blocks = (tokens, qkv, gate_up)
+def gather_first(tokens, qkv, number):
+    blocks = (tokens, qkv)
     ranks, owners = lax.axis_size("seq"), lax.axis_size("fsdp")
 
-    def kernel(tokens, qkv, gate_up, tokens_all, qkv_all, gate_up_all, local, send, recv):
+    def kernel(tokens, qkv, tokens_all, qkv_all, local, send, recv):
         ring = seq_ring()
         weights_ring, _, mate = fsdp_ring()
         greet(ring.peers + weights_ring.peers + [mate])
         copies = Copies(send, recv)
         kept = [
-            pltpu.make_async_copy(own, out.at[at.near[0]], local.at[index])
-            for index, (own, out, at) in enumerate(
-                (
-                    (tokens, tokens_all, ring),
-                    (qkv, qkv_all, weights_ring),
-                    (gate_up, gate_up_all, weights_ring),
-                )
-            )
+            pltpu.make_async_copy(tokens, tokens_all.at[ring.near[0]], local.at[0]),
+            pltpu.make_async_copy(qkv, qkv_all.at[weights_ring.near[0]], local.at[1]),
         ]
         for copy in kept:
             copy.start()
-        in_turn(
-            gather_walk(
-                weights_ring, copies, qkv, qkv_all, by_rows(qkv.shape[0], 2), 2, True, mate
-            ),
-            gather_walk(
-                ring, copies, tokens, tokens_all, by_rows(tokens.shape[0], CHUNKS), CHUNKS
-            ),
-            gather_walk(
-                weights_ring,
-                copies,
-                gate_up,
-                gate_up_all,
-                by_rows(gate_up.shape[0], CHUNKS),
-                CHUNKS,
-                True,
-                mate,
+        rows, weight_rows = tokens.shape[0], qkv.shape[0]
+        beside(
+            gather_walk(ring, copies, tokens, tokens_all, by_rows(rows, CHUNKS), CHUNKS),
+            (
+                gather_walk(
+                    weights_ring, copies, qkv, qkv_all, by_rows(weight_rows, 2), 2, True, mate
+                ),
+                (0, 0, 2, 2, 4, 6, 6, 8),
             ),
         )
         copies.finish()
         for copy in kept:
             copy.wait()
 
-    count = gather_copies(CHUNKS) + gather_copies(CHUNKS, True) + gather_copies(2, True)
+    count = gather_copies(CHUNKS) + gather_copies(2, True)
     return pl.pallas_call(
         kernel,
         out_shape=[
             jax.ShapeDtypeStruct((size, *block.shape), jnp.bfloat16)
-            for size, block in zip((ranks, owners, owners), blocks)
+            for size, block in zip((ranks, owners), blocks)
         ],
-        in_specs=[ANYWHERE] * 3,
-        out_specs=[ANYWHERE] * 3,
-        scratch_shapes=[pltpu.SemaphoreType.DMA((3,))] + semaphores(count),
+        in_specs=[ANYWHERE] * 2,
+        out_specs=[ANYWHERE] * 2,
+        scratch_shapes=[pltpu.SemaphoreType.DMA((2,))] + semaphores(count),
         compiler_params=params(number, 32),
         name="gather_first",
     )(*blocks)
@@ -506,10 +511,30 @@
     return jnp.mean(values * values, axis=-1, keepdims=True)
 
 
-def branch_kernel(part_of, tokens, gain, middle, hidden, block, local, send, recv, *bufs):
+BESIDE_BOTH = (0, 4, 4, 8, 8, 9, 10, 17, 18, 20, 21, 22, 23, 24)
+BESIDE_GATHER = (0, 1, 2, 3, 4, 5, 6, 7, 8, 8, 9, 9, 10, 10)
+
+
+def branch_kernel(
+    part_of,
+    tokens,
+    gain,
+    up,
+    down,
+    middle,
+    hidden,
+    up_all,
+    down_all,
+    block,
+    local,
+    send,
+    recv,
+    *bufs,
+):
     ring = seq_ring()
+    weights_ring, _, mate = fsdp_ring()
     rows = tokens.shape[0]
-    greet(ring.peers)
+    greet(ring.peers + weights_ring.peers + [mate])
     copies = Copies(send, recv)
 
     def done(rows_of, total):
@@ -518,32 +543,49 @@
         factor = lax.rsqrt(mean_square(values) + EPS)
         block[rows_of] = (values * factor * gain[...]).astype(jnp.bfloat16)
 
-    in_turn(reduce_walk(ring, copies, part_of, bufs, rows, CHUNKS, done))
-    kept = pltpu.make_async_copy(block, hidden.at[ring.near[0]], local)
-    kept.start()
-    in_turn(gather_walk(ring, copies, block, hidden, by_rows(rows, CHUNKS), CHUNKS))
+    kept = [
+        pltpu.make_async_copy(up, up_all.at[weights_ring.near[0]], local.at[0]),
+        pltpu.make_async_copy(down, down_all.at[weights_ring.near[0]], local.at[1]),
+        pltpu.make_async_copy(block, hidden.at[ring.near[0]], local.at[2]),
+    ]
+    kept[0].start()
+    kept[1].start()
+
+    def walk():
+        yield from reduce_walk(ring, copies, part_of, bufs, rows, CHUNKS, done)
+        kept[2].start()
+        yield from gather_walk(ring, copies, block, hidden, by_rows(rows, CHUNKS), CHUNKS)
+
+    def weights(own, out):
+        cut = by_rows(own.shape[0], CHUNKS)
+        return gather_walk(weights_ring, copies, own, out, cut, CHUNKS, True, mate)
+
+    beside(walk(), (weights(up, up_all), BESIDE_BOTH), (weights(down, down_all), BESIDE_BOTH))
     copies.finish()
-    kept.wait()
-
-
-def add_branch(partial, tokens, gain, number):
+    for copy in kept:
+        copy.wait()
+
+
+def add_branch(partial, tokens, gain, up, down, number):
     rows, width = tokens.shape
-    ranks = lax.axis_size("seq")
-    count = reduce_copies(CHUNKS) + gather_copies(CHUNKS)
+    ranks, owners = lax.axis_size("seq"), lax.axis_size("fsdp")
+    count = reduce_copies(CHUNKS) + gather_copies(CHUNKS) + 2 * gather_copies(CHUNKS, True)
     return pl.pallas_call(
         branch_kernel,
         out_shape=[
             jax.ShapeDtypeStruct((rows, width), jnp.float32),
             jax.ShapeDtypeStruct((ranks, rows, width), jnp.bfloat16),
+            jax.ShapeDtypeStruct((owners, *up.shape), jnp.bfloat16),
+            jax.ShapeDtypeStruct((owners, *down.shape), jnp.bfloat16),
         ],
-        in_specs=[VMEM] * 3,
-        out_specs=[VMEM, ANYWHERE],
-        scratch_shapes=[pltpu.VMEM((rows, width), jnp.bfloat16), pltpu.SemaphoreType.DMA]
+        in_specs=[VMEM] * 3 + [ANYWHERE] * 2,
+        out_specs=[VMEM] + [ANYWHERE] * 3,
+        scratch_shapes=[pltpu.VMEM((rows, width), jnp.bfloat16), pltpu.SemaphoreType.DMA((3,))]
         + semaphores(count)
         + reduce_scratch(rows, width),
         compiler_params=params(number, 32),
         name="add_branch",
-    )(partial.reshape(ranks, rows, width), tokens, gain)
+    )(partial.reshape(ranks, rows, width), tokens, gain, up, down)
 
 
 def norm_back_rows(grad, gain, values):
@@ -554,23 +596,49 @@
     return back, grad * normed
 
 
+PRODUCT = 512
+
+
+def product(left, right, store):
+    def columns(index, _):
+        cols = pl.ds(pl.multiple_of(index * PRODUCT, PRODUCT), PRODUCT)
+        store(cols, jnp.dot(left, right[:, cols], preferred_element_type=jnp.float32))
+        return 0
+
+    lax.fori_loop(0, right.shape[1] // PRODUCT, columns, 0)
+
+
 def middle_kernel(
     part_of,
     middle,
     gain,
     cotangent,
-    grads,
+    hidden,
+    gate_grads,
+    up_grads,
+    act,
+    grad_out,
+    down,
     grad_middle,
     grad_gain,
     branch,
     grads_share,
+    down_grad,
+    layer_part,
     block,
     local,
     send,
     recv,
+    left_wide,
+    right_wide,
+    act_here,
+    turned,
+    for_mate,
+    staged,
+    loads,
+    stores,
     own,
     other,
-    sems,
     *bufs,
 ):
     ring = seq_ring()
@@ -580,6 +648,20 @@
     copies = Copies(send, recv)
     grad_gain[...] = jnp.zeros_like(grad_gain)
 
+    def load(source, target, number):
+        return pltpu.make_async_copy(source, target, loads.at[number])
+
+    units = gate_grads.shape[1]
+    first = [
+        load(hidden, left_wide, 0),
+        load(gate_grads, right_wide.at[:, pl.ds(0, units)], 1),
+        load(up_grads, right_wide.at[:, pl.ds(units, units)], 2),
+        load(act, act_here, 3),
+    ]
+    second = [load(grad_out, left_wide, 4), load(down, right_wide, 5)]
+    for copy in first:
+        copy.start()
+
     def done(rows_of, total):
         back, terms = norm_back_rows(total, gain[...], middle[rows_of])
         grad_gain[...] += jnp.sum(terms, axis=0, keepdims=True)
@@ -597,32 +679,100 @@
         kept.start()
         yield from gather_walk(ring, copies, block, branch, by_rows(rows, CHUNKS), CHUNKS)
 
-    in_turn(
-        owners_walk(
-            weights_ring,
-            core,
-            mate,
-            copies,
-            grads,
-            own,
-            other,
-            sems,
-            bufs[:7],
-            grads_share.shape[0],
-            owned,
+    def produce(place):
+        if first:
+            for _ in range(3):
+                first.pop(0).wait()
+            waited.append(first.pop(0))
+        lanes = pl.ds(pl.multiple_of(place * 2 * rows, 2 * rows), 2 * rows)
+        turned[...] = left_wide[:, lanes].T
+        here, there = pl.ds(core * rows, rows), pl.ds((1 - core) * rows, rows)
+
+        def store_own(cols, value):
+            own[place, :, cols] = value.astype(jnp.bfloat16)
+
+        def store_mate(cols, value):
+            for_mate[place, :, cols] = value.astype(jnp.bfloat16)
+
+        product(turned[there], right_wide, store_mate)
+        sent = copies.start(for_mate.at[place], other.at[place], mate)
+        product(turned[here], right_wide, store_own)
+        return [sent.wait_recv]
+
+    waited = []
+
+    def others():
+        for copy in second:
+            copy.start()
+        waited[0].wait()
+        yield
+        second[0].wait()
+        flights = [None, None]
+
+        def flush(slot, target):
+            copy = pltpu.make_async_copy(staged.at[slot], target, stores.at[slot])
+            copy.start()
+            flights[slot] = copy
+
+        def store(slot):
+            def put(cols, value):
+                staged[slot, :, cols] = value.astype(jnp.bfloat16)
+
+            return put
+
+        pieces = act_here.shape[1] // rows
+        for index in range(pieces):
+            slot = index % 2
+            if flights[slot] is not None:
+                flights[slot].wait()
+            product(act_here[:, pl.ds(index * rows, rows)].T, left_wide, store(slot))
+            flush(slot, down_grad.at[index])
+            yield
+        second[1].wait()
+        for index in range(part_of.shape[0]):
+            slot = index % 2
+            flights[slot].wait()
+            product(act_here[pl.ds(index * rows, rows)], right_wide, store(slot))
+            flush(slot, layer_part.at[index])
+            yield
+        for copy in flights:
+            copy.wait()
+
+    beside(
+        walk(),
+        (
+            owners_walk(
+                weights_ring,
+                mate,
+                copies,
+                produce,
+                own,
+                other,
+                bufs[:7],
+                grads_share.shape[0],
+                owned,
+            ),
+            (0,) * 8 + (0, 0, 0, 0, 8, 8, 8, 8, 17, 19, 24, 24),
         ),
-        walk(),
+        (
+            others(),
+            (8, 9, 10, 11, 12, 13, 14, 15, 16, 18, 19, 20, 21, 22, 23, 24, 25),
+        ),
     )
     copies.finish()
     kept.wait()
 
 
-def back_to_middle(partial, middle, gain, cotangent, grads, number):
+def back_to_middle(
+    partial, middle, gain, cotangent, hidden, gate_grads, up_grads, act, grad_out, down, number
+):
     rows, width = middle.shape
+    length = hidden.shape[0]
     ranks, owners = lax.axis_size("seq"), lax.axis_size("fsdp")
     places = owners // 2
-    grad_rows, grad_cols = grads.shape[0] // owners, grads.shape[1]
-    count = reduce_copies(CHUNKS) + gather_copies(CHUNKS) + OWNERS_COPIES
+    grad_rows, grad_cols = width // owners, 2 * gate_grads.shape[1]
+    pieces = act.shape[1] // rows
+    count = reduce_copies(CHUNKS) + gather_copies(CHUNKS) + OWNERS_COPIES + places
     return pl.pallas_call(
         middle_kernel,
         out_shape=[
@@ -630,21 +780,38 @@
             jax.ShapeDtypeStruct((1, width), jnp.float32),
             jax.ShapeDtypeStruct((ranks, rows, width), jnp.bfloat16),
             jax.ShapeDtypeStruct((grad_rows, grad_cols), jnp.bfloat16),
+            jax.ShapeDtypeStruct((pieces, rows, width), jnp.bfloat16),
+            jax.ShapeDtypeStruct((ranks, rows, width), jnp.bfloat16),
         ],
-        in_specs=[VMEM] * 4 + [ANYWHERE],
-        out_specs=[VMEM, VMEM, ANYWHERE, VMEM],
+        in_specs=[VMEM] * 4 + [ANYWHERE] * 6,
+        out_specs=[VMEM, VMEM, ANYWHERE, VMEM, ANYWHERE, ANYWHERE],
         scratch_shapes=[pltpu.VMEM((rows, width), jnp.bfloat16), pltpu.SemaphoreType.DMA]
         + semaphores(count)
+        + [
+            pltpu.VMEM((length, width), jnp.bfloat16),
+            pltpu.VMEM((length, width), jnp.bfloat16),
+            pltpu.VMEM(act.shape, jnp.bfloat16),
+            pltpu.VMEM((2 * grad_rows, length), jnp.bfloat16),
+            pltpu.VMEM((places, grad_rows, grad_cols), jnp.bfloat16),
+            pltpu.VMEM((2, rows, width), jnp.bfloat16),
+            pltpu.SemaphoreType.DMA((6,)),
+            pltpu.SemaphoreType.DMA((2,)),
+        ]
         + owners_scratch(places, grad_rows, grad_cols)
         + reduce_scratch(rows, width),
-        compiler_params=params(number, 48),
+        compiler_params=params(number, 52),
         name="back_to_middle",
     )(
         partial.reshape(ranks, rows, width),
         middle,
         gain,
         cotangent,
-        grads.reshape(places, 2, grad_rows, grad_cols),
+        hidden,
+        gate_grads,
+        up_grads,
+        act,
+        grad_out,
+        down,
     )
 
 
@@ -653,139 +820,116 @@
     tokens,
     gain,
     grad_middle,
-    qkv_parts,
-    heads_parts,
+    qkv_grad,
+    heads_grad,
     out,
     grad_gain,
-    qkv_share,
-    heads_share,
-    qkv_mate,
-    heads_mate,
-    qkv_got,
-    heads_got,
+    share,
     heads_block,
     heads_here,
+    fetches,
     send,
     recv,
+    own,
+    other,
     *bufs,
 ):
     ring = seq_ring()
+    weights_ring, core, mate = fsdp_ring()
     rows = tokens.shape[0]
-    core, mate, places, others = along_fsdp()
-    place = places[0]
     swap, apart = transposed()
-    greet_also(ring.peers + [mate] + others[1:], swap, apart)
+    greet_also(ring.peers + weights_ring.peers + [mate], swap, apart)
     copies = Copies(send, recv)
     grad_gain[...] = jnp.zeros_like(grad_gain)
-    pair = [
-        copies.start(qkv_parts.at[:, 1 - core], qkv_mate, mate),
-        copies.start(heads_parts.at[1 - core], heads_mate, mate),
-    ]
-    pushed = []
-
-    def meanwhile():
-        for copy in pair:
-            copy.wait_recv()
-
-        def add(index, _):
-            qkv_mate[index] = (
-                qkv_mate[index].astype(jnp.float32) + qkv_parts[index, core].astype(jnp.float32)
-            ).astype(jnp.bfloat16)
-            heads_mate[index] = (
-                heads_mate[index].astype(jnp.float32)
-                + heads_parts[core, index].astype(jnp.float32)
-            ).astype(jnp.bfloat16)
-            return 0
-
-        lax.fori_loop(0, len(places), add, 0)
-        for step in range(1, len(places)):
-            pushed.append(
-                copies.start(qkv_mate.at[places[step]], qkv_got.at[step], others[step])
-            )
-            pushed.append(
-                copies.start(heads_mate.at[places[step]], heads_got.at[step], others[step])
-            )
-
-    def later():
-        for copy in pushed:
-            copy.wait_recv()
-        total = qkv_mate[place].astype(jnp.float32)
-        heads_total = heads_mate[place].astype(jnp.float32)
-        for step in range(1, len(places)):
-            total += qkv_got[step].astype(jnp.float32)
-            heads_total += heads_got[step].astype(jnp.float32)
-        qkv_share[...] = total.astype(jnp.bfloat16)
-        heads_block[...] = heads_total.astype(jnp.bfloat16)
-
-        @pl.when(apart)
-        def _():
-            copy = pltpu.make_async_remote_copy(
-                src_ref=heads_block,
-                dst_ref=heads_here,
-                send_sem=send.at[send.shape[0] - 1],
-                recv_sem=recv.at[recv.shape[0] - 1],
-                device_id=swap,
-                device_id_type=MESH,
-            )
-            copy.start()
-
-    def done(rows_of, total):
-        back, terms = norm_back_rows(total, gain[...], tokens[rows_of].astype(jnp.float32))
-        grad_gain[...] += jnp.sum(terms, axis=0, keepdims=True)
-        out[rows_of] = (grad_middle[rows_of] + back).astype(jnp.bfloat16)
-
-    def weights():
-        yield
-        meanwhile()
-        for _ in range(2 * CHUNKS):
-            yield
-        later()
-
-    in_turn(reduce_walk(ring, copies, part_of, bufs, rows, CHUNKS, done), weights())
-    copies.finish()
-
-    @pl.when(jnp.logical_not(apart))
-    def _():
-        heads_share[...] = heads_block[...]
-
-    @pl.when(apart)
-    def _():
-        pltpu.make_async_remote_copy(
+    qkv_cols = qkv_grad.shape[3]
+    heads_cols = share.shape[1] - qkv_cols
+    qkv_part, heads_part = pl.ds(0, qkv_cols), pl.ds(qkv_cols, heads_cols)
+
+    def heads_of(place, which):
+        first = pl.multiple_of(place * heads_cols, heads_cols)
+        return heads_grad.at[which, :, pl.ds(first, heads_cols)]
+
+    pieces = (
+        (lambda place, which: qkv_grad.at[place, which], lambda ref: ref.at[:, qkv_part]),
+        (heads_of, lambda ref: ref.at[:, heads_part]),
+    )
+
+    def exchange():
+        return pltpu.make_async_remote_copy(
             src_ref=heads_block,
             dst_ref=heads_here,
             send_sem=send.at[send.shape[0] - 1],
             recv_sem=recv.at[recv.shape[0] - 1],
             device_id=swap,
             device_id_type=MESH,
-        ).wait()
-        heads_share[...] = heads_here[...]
+        )
+
+    def owned(rows_of, total):
+        share[rows_of, qkv_part] = total[:, :qkv_cols].astype(jnp.bfloat16)
+        heads_block[rows_of] = total[:, qkv_cols:].astype(jnp.bfloat16)
+
+    def done(rows_of, total):
+        back, terms = norm_back_rows(total, gain[...], tokens[rows_of].astype(jnp.float32))
+        grad_gain[...] += jnp.sum(terms, axis=0, keepdims=True)
+        out[rows_of] = (grad_middle[rows_of] + back).astype(jnp.bfloat16)
+
+    def weights():
+        yield from owners_walk(
+            weights_ring,
+            mate,
+            copies,
+            fetched(copies, core, mate, pieces, own, other, fetches),
+            own,
+            other,
+            bufs[:7],
+            rows,
+            owned,
+        )
+
+        @pl.when(apart)
+        def _():
+            exchange().start()
+
+        yield
+
+        @pl.when(apart)
+        def _():
+            exchange().wait()
+            share[:, heads_part] = heads_here[...]
+
+        @pl.when(jnp.logical_not(apart))
+        def _():
+            share[:, heads_part] = heads_block[...]
+
+    beside(
+        reduce_walk(ring, copies, part_of, bufs[7:], rows, CHUNKS, done),
+        (weights(), (0,) * 8 + (0, 1, 2, 3, 4, 4, 8, 8, 9, 10, 11, 12, 13)),
+    )
+    copies.finish()
 
 
 def back_to_tokens(partial, tokens, gain, grad_middle, qkv_grad, heads_grad, number):
     rows, width = tokens.shape
     ranks, owners = lax.axis_size("seq"), lax.axis_size("fsdp")
     places = owners // 2
-    qkv_cols, head_rows = qkv_grad.shape[1], heads_grad.shape[0] // owners
-    count = reduce_copies(CHUNKS) + 2 + 2 * (places - 1) + 1
+    qkv_cols, heads_cols = qkv_grad.shape[1], width // places
+    count = reduce_copies(CHUNKS) + OWNERS_COPIES + 2 * places + 1
     return pl.pallas_call(
         tokens_kernel,
         out_shape=[
             jax.ShapeDtypeStruct((rows, width), jnp.bfloat16),
             jax.ShapeDtypeStruct((1, width), jnp.float32),
-            jax.ShapeDtypeStruct((rows, qkv_cols), jnp.bfloat16),
-            jax.ShapeDtypeStruct((head_rows, width), jnp.bfloat16),
+            jax.ShapeDtypeStruct((rows, qkv_cols + heads_cols), jnp.bfloat16),
         ],
-        in_specs=[VMEM] * 6,
-        out_specs=[VMEM] * 4,
+        in_specs=[VMEM] * 4 + [ANYWHERE] * 2,
+        out_specs=[VMEM] * 3,
         scratch_shapes=[
-            pltpu.VMEM((places, rows, qkv_cols), jnp.bfloat16),
-            pltpu.VMEM((places, head_rows, width), jnp.bfloat16),
-            pltpu.VMEM((places, rows, qkv_cols), jnp.bfloat16),
-            pltpu.VMEM((places, head_rows, width), jnp.bfloat16),
-            pltpu.VMEM((head_rows, width), jnp.bfloat16),
-            pltpu.VMEM((head_rows, width), jnp.bfloat16),
+            pltpu.VMEM((rows, heads_cols), jnp.bfloat16),
+            pltpu.VMEM((rows, heads_cols), jnp.bfloat16),
+            pltpu.SemaphoreType.DMA((2 * places,)),
         ]
         + semaphores(count)
+        + owners_scratch(places, rows, qkv_cols + heads_cols)
         + reduce_scratch(rows, width),
         compiler_params=params(number, 40),
         name="back_to_tokens",
@@ -795,28 +939,27 @@
         gain,
         grad_middle,
         qkv_grad.reshape(places, 2, rows, qkv_cols),
-        heads_grad.reshape(2, places, head_rows, width),
+        heads_grad.reshape(2, rows, width),
     )
 
 
 def finish_kernel(
     gate_up,
     down,
-    qkv,
-    heads,
+    small,
     gain_one,
     gain_two,
     gate_up_all,
     down_all,
-    qkv_all,
-    heads_all,
+    small_all,
     gains,
     given,
     from_mate,
-    summed,
-    from_places,
+    pair,
+    from_partner,
+    by_place,
     for_partner,
-    from_partner,
+    partners,
     by_column,
     local,
     send,
@@ -825,15 +968,13 @@
     ring = seq_ring()
     me = ring.near[0]
     side = lax.axis_size("seq") // 2
-    column = lax.rem(me, side)
-    core, mate, places, others = along_fsdp()
-    greet(ring.peers + [mate] + others[1:])
+    weights_ring, core, mate = fsdp_ring()
+    greet(ring.peers + weights_ring.peers + [mate])
     copies = Copies(send, recv)
     arrays = [
         (gate_up, gate_up_all, by_rows(gate_up.shape[0], CHUNKS)),
         (down, down_all, by_rows(down.shape[0], CHUNKS)),
-        (qkv, qkv_all, by_rows(qkv.shape[0], CHUNKS)),
-        (heads, heads_all, by_columns(heads.shape[1], CHUNKS)),
+        (small, small_all, by_rows(small.shape[0], CHUNKS)),
     ]
     kept = [
         pltpu.make_async_copy(own, out.at[me], local.at[i]) for i, (own, out, _) in enumerate(arrays)
@@ -841,58 +982,60 @@
     for copy in kept:
         copy.start()
 
-    def sum_gains():
-        lanes = given.shape[3]
-        for index in range(2 * len(places)):
-            cols = pl.ds(index * lanes, lanes)
-            given[index // 2, index % 2, 0:1] = gain_one[:, cols]
-            given[index // 2, index % 2, 1:2] = gain_two[:, cols]
-            given[index // 2, index % 2, 2:8] = jnp.zeros((6, lanes), jnp.float32)
-        copy = copies.start(given.at[:, 1 - core], from_mate, mate)
-        yield
-        copy.wait_recv()
-        summed[...] = given[:, core] + from_mate[...]
-        pushed = [
-            copies.start(summed.at[places[step]], from_places.at[step], others[step])
-            for step in range(1, len(places))
-        ]
-        yield
-        for copy in pushed:
-            copy.wait_recv()
-        total = summed[places[0]]
-        for step in range(1, len(places)):
-            total += from_places[step]
-        for_partner[...] = total
-        copy = copies.start(for_partner, from_partner, ring.partner)
-        yield
-        copy.wait_recv()
-        by_column[column] = for_partner[...] + from_partner[...]
-        to_right = copies.start(by_column.at[column], by_column.at[column], ring.right)
-        to_left = copies.start(by_column.at[column], by_column.at[column], ring.left)
+    def around(table, ring_of):
+        place = lax.rem(ring_of.place, side)
+        after = lax.rem(place + 1, side)
+        mine = table.at[place]
+        to_right = copies.start(mine, mine, ring_of.right)
+        to_left = copies.start(mine, mine, ring_of.left)
         yield
         to_right.wait_recv()
         to_left.wait_recv()
-        after = lax.rem(column + 1, side)
-        copy = copies.start(by_column.at[after], by_column.at[after], ring.left)
+        copy = copies.start(table.at[after], table.at[after], ring_of.left)
         yield
         copy.wait_recv()
+
+    def sum_gains():
+        lanes = given.shape[2]
+        for index in range(given.shape[0]):
+            cols = pl.ds(index * lanes, lanes)
+            given[index, 0:1] = gain_one[:, cols]
+            given[index, 1:2] = gain_two[:, cols]
+            given[index, 2:8] = jnp.zeros((6, lanes), jnp.float32)
+        copy = copies.start(given, from_mate, mate)
+        yield
+        copy.wait_recv()
+        pair[...] = given[...] + from_mate[...]
+        copy = copies.start(pair, from_partner, weights_ring.partner)
+        yield
+        copy.wait_recv()
+        by_place[lax.rem(weights_ring.place, side)] = pair[...] + from_partner[...]
+        yield from around(by_place, weights_ring)
+        block = lax.axis_index("fsdp")
+        for_partner[...] = (by_place[0, block] + by_place[1, block]) + (
+            by_place[2, block] + by_place[3, block]
+        )
+        copy = copies.start(for_partner, partners, ring.partner)
+        yield
+        copy.wait_recv()
+        by_column[lax.rem(ring.place, side)] = for_partner[...] + partners[...]
+        yield from around(by_column, ring)
         gains[...] = (by_column[0] + by_column[1]) + (by_column[2] + by_column[3])
 
-    in_turn(
-        *(gather_walk(ring, copies, own, out, cut, CHUNKS) for own, out, cut in arrays), sum_gains()
+    beside(
+        in_step(*(gather_walk(ring, copies, own, out, cut, CHUNKS) for own, out, cut in arrays)),
+        (sum_gains(), range(1, 9)),
     )
     copies.finish()
     for copy in kept:
         copy.wait()
 
 
-def finish_grads(gate_up, down, qkv, heads, gain_one, gain_two, number):
+def finish_grads(gate_up, down, small, gain_one, gain_two, number):
     ranks, owners = lax.axis_size("seq"), lax.axis_size("fsdp")
-    blocks = (gate_up, down, qkv, heads)
-    places = owners // 2
+    blocks = (gate_up, down, small)
     lanes = gain_one.shape[1] // owners
-    size = sum(block.size for block in blocks)
-    count = len(blocks) * gather_copies(CHUNKS) + 1 + (places - 1) + 1 + 3
+    count = len(blocks) * gather_copies(CHUNKS) + 1 + 1 + 3 + 1 + 3
 
     def table(*shape):
         return pltpu.VMEM((*shape, 8, lanes), jnp.float32)
@@ -901,13 +1044,14 @@
         finish_kernel,
         out_shape=[jax.ShapeDtypeStruct((ranks, *block.shape), block.dtype) for block in blocks]
         + [jax.ShapeDtypeStruct((8, lanes), jnp.float32)],
-        in_specs=[ANYWHERE] * 4 + [VMEM] * 2,
-        out_specs=[ANYWHERE] * 4 + [VMEM],
+        in_specs=[ANYWHERE] * 3 + [VMEM] * 2,
+        out_specs=[ANYWHERE] * 3 + [VMEM],
         scratch_shapes=[
-            table(places, 2),
-            table(places),
-            table(places),
-            table(places),
+            table(owners),
+            table(owners),
+            table(owners),
+            table(owners),
+            table(ranks // 2, owners),
             table(),
             table(),
             table(ranks // 2),
@@ -928,7 +1072,22 @@
     )
 
 
-def place_kernel(gate, up, down, query, pair, heads, gate_out, up_out, down_out, query_out, key_out, value_out, heads_out):
+def place_kernel(
+    gate,
+    up,
+    down,
+    query,
+    pair,
+    heads_low,
+    heads_high,
+    gate_out,
+    up_out,
+    down_out,
+    query_out,
+    key_out,
+    value_out,
+    heads_out,
+):
     lanes = gate.shape[2]
     blocks = gate.shape[0] // 2
     for part, out in ((gate, gate_out), (up, up_out)):
@@ -943,17 +1102,18 @@
     value_out[...] = value
     down_out[...] = down[0].astype(jnp.float32)
     query_out[...] = query[0].astype(jnp.float32)
-    heads_out[...] = heads[0].astype(jnp.float32)
-
-
-def place_grads(gate_up, down, qkv, heads):
+    heads_out[:, :lanes] = heads_low[0].astype(jnp.float32)
+    heads_out[:, lanes:] = heads_high[0].astype(jnp.float32)
+
+
+def place_grads(gate_up, down, small):
     ranks, rows, both = gate_up.shape
     lanes = 128
     steps = both // 2 // lanes
     down_rows, width = down.shape[1:]
-    head_rows = heads.shape[1]
-    query_cols = qkv.shape[2] - lanes
-    assert steps == ranks and lanes == 2 * HEAD_SIZE
+    query_cols = width // ranks
+    first = query_cols // lanes
+    assert steps == ranks and lanes == 2 * HEAD_SIZE and query_cols == 2 * lanes
     real = jnp.float32
     return pl.pallas_call(
         place_kernel,
@@ -965,15 +1125,16 @@
             jax.ShapeDtypeStruct((rows, ranks * query_cols), real),
             jax.ShapeDtypeStruct((rows, ranks * HEAD_SIZE), real),
             jax.ShapeDtypeStruct((rows, ranks * HEAD_SIZE), real),
-            jax.ShapeDtypeStruct((ranks * head_rows, width), real),
+            jax.ShapeDtypeStruct((rows, width), real),
         ],
         in_specs=[
             pl.BlockSpec((ranks, rows, lanes), lambda i: (0, 0, i)),
             pl.BlockSpec((ranks, rows, lanes), lambda i: (0, 0, steps + i)),
             pl.BlockSpec((1, down_rows, width), lambda i: (i, 0, 0)),
             pl.BlockSpec((1, rows, query_cols), lambda i: (i, 0, 0)),
-            pl.BlockSpec((2, rows, lanes), lambda i: (i // 2, 0, query_cols // lanes)),
-            pl.BlockSpec((1, head_rows, width), lambda i: (i, 0, 0)),
+            pl.BlockSpec((2, rows, lanes), lambda i: (i // 2, 0, first)),
+            pl.BlockSpec((1, rows, lanes), lambda i: (i, 0, first + 1)),
+            pl.BlockSpec((1, rows, lanes), lambda i: (i, 0, first + 2)),
         ],
         out_specs=[
             pl.BlockSpec((rows, ranks * lanes), lambda i: (0, i)),
@@ -982,15 +1143,15 @@
             pl.BlockSpec((rows, query_cols), lambda i: (0, i)),
             pl.BlockSpec((rows, lanes), lambda i: (0, i // 2)),
             pl.BlockSpec((rows, lanes), lambda i: (0, i // 2)),
-            pl.BlockSpec((head_rows, width), lambda i: (i, 0)),
+            pl.BlockSpec((rows, query_cols), lambda i: (0, i)),
         ],
         compiler_params=pltpu.CompilerParams(vmem_limit_bytes=32 * 2**20),
         name="place_grads",
-    )(gate_up, gate_up, down, qkv, qkv, heads)
+    )(gate_up, gate_up, down, small, small, small, small)
 
 
 def pick_kernel(
-    query, key, value, gate, up, gain_one, gain_two, qkv_out, gate_up_out, wide, narrow, sems
+    query, key, value, gate, up, gain_one, gain_two, qkv_out, gate_out, up_out, wide, narrow, sems
 ):
     rank, ranks = lax.axis_index("seq"), lax.axis_size("seq")
     rows = query.shape[0]
@@ -1033,10 +1194,10 @@
         return jnp.where(odd == 0, low, high).astype(jnp.bfloat16)
 
     qkv_out[pl.ds(0, rows), pl.ds(query_cols, lanes)] = chosen(narrow[0], narrow[1])
-    for which in range(2):
+    for which, out in enumerate((gate_out, up_out)):
         for index in range(owners // 2):
-            cols = pl.ds((which * (owners // 2) + index) * lanes, lanes)
-            gate_up_out[:, cols] = chosen(wide[which, 2 * index], wide[which, 2 * index + 1])
+            cols = pl.ds(index * lanes, lanes)
+            out[:, cols] = chosen(wide[which, 2 * index], wide[which, 2 * index + 1])
 
 
 def pick_columns(query, key, value, gate, up, gain_one, gain_two):
@@ -1048,10 +1209,11 @@
         pick_kernel,
         out_shape=[
             jax.ShapeDtypeStruct((rows + 32, width // ranks + lanes), jnp.bfloat16),
-            jax.ShapeDtypeStruct((rows, owners * lanes), jnp.bfloat16),
+            jax.ShapeDtypeStruct((rows, owners // 2 * lanes), jnp.bfloat16),
+            jax.ShapeDtypeStruct((rows, owners // 2 * lanes), jnp.bfloat16),
         ],
         in_specs=[ANYWHERE] * 5 + [VMEM] * 2,
-        out_specs=[VMEM] * 2,
+        out_specs=[VMEM] * 3,
         scratch_shapes=[
             pltpu.VMEM((2, owners, rows, lanes), jnp.bfloat16),
             pltpu.VMEM((2, rows, lanes), jnp.bfloat16),
@@ -1128,14 +1290,14 @@
     starts,
     cotangent,
     heads,
-    down,
+    gate,
     attended,
     lse,
     queries,
     keys,
     gathered,
     heads_all,
-    down_all,
+    gate_all,
     key_rows,
     bias,
     local,
@@ -1163,7 +1325,7 @@
 
     kept = [
         pltpu.make_async_copy(cotangent, gathered.at[ring.near[0]], local.at[0]),
-        pltpu.make_async_copy(down, down_all.at[weights_ring.near[0]], local.at[1]),
+        pltpu.make_async_copy(gate, gate_all.at[weights_ring.near[0]], local.at[1]),
     ]
     for copy in kept:
         copy.start()
@@ -1178,7 +1340,6 @@
         def _():
             keep().start()
 
-        yield
         attend_tiles(qkv, cosine, sine, starts, attended, lse, queries, keys, key_rows, bias)
         yield
 
@@ -1191,32 +1352,34 @@
             keep().wait()
 
         copy = copies.start(heads_all.at[core], heads_all.at[core], mate)
-        for _ in range(2 * CHUNKS):
-            yield
+        yield
         copy.wait_recv()
 
-    in_turn(
+    beside(
         gather_walk(
             ring, copies, cotangent, gathered, by_rows(cotangent.shape[0], CHUNKS), CHUNKS
         ),
-        gather_walk(
-            weights_ring,
-            copies,
-            down,
-            down_all,
-            by_rows(down.shape[0], CHUNKS),
-            CHUNKS,
-            True,
-            mate,
+        (
+            gather_walk(
+                weights_ring,
+                copies,
+                gate,
+                gate_all,
+                by_rows(gate.shape[0], CHUNKS),
+                CHUNKS,
+                True,
+                mate,
+            ),
+            BESIDE_GATHER,
         ),
-        heads_walk(),
+        (heads_walk(), (0, 6, 10)),
     )
     copies.finish()
     for copy in kept:
         copy.wait()
 
 
-def attend(qkv, cosine, sine, starts, cotangent, heads, down, group, number):
+def attend(qkv, cosine, sine, starts, cotangent, heads, gate, group, number):
     length = qkv.shape[1]
     rows, width = cotangent.shape
     ranks = lax.axis_size("seq")
@@ -1229,7 +1392,7 @@
             jax.ShapeDtypeStruct((HEAD_SIZE, length), jnp.bfloat16),
             jax.ShapeDtypeStruct((ranks, rows, width), jnp.bfloat16),
             jax.ShapeDtypeStruct((2, *heads.shape), jnp.bfloat16),
-            jax.ShapeDtypeStruct((lax.axis_size("fsdp"), *down.shape), jnp.bfloat16),
+            jax.ShapeDtypeStruct((lax.axis_size("fsdp"), *gate.shape), jnp.bfloat16),
         ],
         in_specs=[VMEM] * 4 + [ANYWHERE] * 3,
         out_specs=[VMEM] * 4 + [ANYWHERE] * 3,
@@ -1241,7 +1404,7 @@
         + semaphores(gather_copies(CHUNKS) + gather_copies(CHUNKS, True) + 2),
         compiler_params=params(number, 40),
         name="attend",
-    )(qkv, cosine, sine, starts, cotangent, heads, down)
+    )(qkv, cosine, sine, starts, cotangent, heads, gate)
 
 
 def back_tiles(
@@ -1333,7 +1496,7 @@
         refs[9:12],
         refs[12:15],
     )
-    scratch, (send, recv), (own, other, sems) = refs[15:24], refs[24:26], refs[26:29]
+    scratch, (fetches, send, recv), (own, other) = refs[15:24], refs[24:27], refs[27:29]
     bufs = refs[29:]
     ring = seq_ring()
     weights_ring, core, mate = fsdp_ring()
@@ -1341,8 +1504,8 @@
     copies = Copies(send, recv)
 
     def compute():
-        yield
         back_tiles(*ins, out, *scratch)
+        yield
 
     def done(rows_of, total):
         layer_out[rows_of] = (middle[rows_of] + total).astype(jnp.bfloat16)
@@ -1350,22 +1513,24 @@
     def owned(rows_of, total):
         grads_share[rows_of] = total.astype(jnp.bfloat16)
 
-    in_turn(
-        owners_walk(
-            weights_ring,
-            core,
-            mate,
-            copies,
-            grads,
-            own,
-            other,
-            sems,
-            bufs[:7],
-            grads_share.shape[0],
-            owned,
+    pieces = ((lambda place, which: grads.at[place, which], lambda ref: ref),)
+    beside(
+        reduce_walk(ring, copies, part_of, bufs[7:], middle.shape[0], CHUNKS, done),
+        (
+            owners_walk(
+                weights_ring,
+                mate,
+                copies,
+                fetched(copies, core, mate, pieces, own, other, fetches),
+                own,
+                other,
+                bufs[:7],
+                grads_share.shape[0],
+                owned,
+            ),
+            (0,) * 8 + (0, 0, 1, 2, 8, 8, 8, 8, 12, 12, 14, 14),
         ),
-        reduce_walk(ring, copies, part_of, bufs[7:], middle.shape[0], CHUNKS, done),
-        compute(),
+        (compute(), (0,)),
     )
     copies.finish()
 
@@ -1391,7 +1556,7 @@
     rows, width = middle.shape
     ranks, owners = lax.axis_size("seq"), lax.axis_size("fsdp")
     places = owners // 2
-    grad_rows = down_grad.shape[0] // owners
+    grad_rows = down_grad.shape[1] // 2
     return pl.pallas_call(
         backward_kernel,
         out_shape=[
@@ -1412,7 +1577,8 @@
             pltpu.VMEM((group * HEAD_SIZE, length), jnp.float32),
             pltpu.VMEM((tiles, TILE, TILE), jnp.float32),
         ]
-        + semaphores(reduce_copies(CHUNKS) + OWNERS_COPIES)
+        + [pltpu.SemaphoreType.DMA((places,))]
+        + semaphores(reduce_copies(CHUNKS) + OWNERS_COPIES + places)
         + owners_scratch(places, grad_rows, width)
         + reduce_scratch(rows, width),
         compiler_params=params(number, 48),
@@ -1427,7 +1593,7 @@
         cosine,
         sine,
         starts,
-        partial.reshape(ranks, rows, width),
+        partial,
         middle,
         down_grad.reshape(places, 2, grad_rows, width),
     )
@@ -1472,11 +1638,10 @@
     segment_row = segment_ids[0]
     length = segment_row.shape[0]
 
-    qkv_in, gate_up_in = pick_columns(
+    qkv_in, gate_in, up_in = pick_columns(
         query_weight, key_matrix, value_matrix, gate_weight, up_weight, attention_gain, feed_gain
     )
-    whole, qkv_got, gate_up_all = gather_first(tokens[0], qkv_in, gate_up_in, 0)
-    gate_up_all = gate_up_all.reshape(width, -1)
+    whole, qkv_got = gather_first(tokens[0], qkv_in, 0)
     qkv_all = qkv_got[:, :rows].reshape(owners * rows, -1)
     gain_one = qkv_got[:, rows, :rows].reshape(1, -1).astype(jnp.float32)
     gain_two = qkv_got[:, rows + 1, :rows].reshape(1, -1).astype(jnp.float32)
@@ -1489,19 +1654,26 @@
     hidden_one = (whole * lax.rsqrt(mean_square(whole) + EPS) * gain_one).astype(jnp.bfloat16)
     qkv = jnp.einsum("tm,mc->ct", hidden_one, qkv_all, preferred_element_type=jnp.float32)
     qkv = qkv.astype(jnp.bfloat16)
-    attended, lse, queries, keys, grad_out, output_all, down_all = attend(
-        qkv, cosine, sine, starts, cotangent[0], output_weight, down_in, group, 1
-    )
-    down_all = down_all.reshape(ff_local, width)
+    attended, lse, queries, keys, grad_out, output_all, gate_all = attend(
+        qkv, cosine, sine, starts, cotangent[0], output_weight, gate_in, group, 1
+    )
+    gate_all = gate_all.reshape(width, ff_local)
     grad_out = grad_out.reshape(length, width)
     output_all = output_all.reshape(q_cols, width)
-    middle, hidden_two = add_branch(
-        contract_rows(attended, output_all).astype(jnp.bfloat16), tokens[0], gain_two, 2
-    )
+    middle, hidden_two, up_all, down_all = add_branch(
+        contract_rows(attended, output_all).astype(jnp.bfloat16),
+        tokens[0],
+        gain_two,
+        up_in,
+        down_in,
+        2,
+    )
+    up_all = up_all.reshape(width, ff_local)
+    down_all = down_all.reshape(ff_local, width)
     hidden_two = hidden_two.reshape(length, width)
 
-    gate = matmul(hidden_two, gate_up_all[:, :ff_local])
-    up_proj = matmul(hidden_two, gate_up_all[:, ff_local:])
+    gate = matmul(hidden_two, gate_all)
+    up_proj = matmul(hidden_two, up_all)
     sig_gate = jax.nn.sigmoid(gate)
     silu_gate = gate * sig_gate
     act = (silu_gate * up_proj).astype(jnp.bfloat16)
@@ -1510,16 +1682,18 @@
         jnp.bfloat16
     )
     grad_up = (grad_act * silu_gate).astype(jnp.bfloat16)
-    gate_up_grads = jnp.concatenate([grad_gate, grad_up], axis=1)
-    down_grad = contract_rows(act, grad_out).astype(jnp.bfloat16)
-    gate_up_grad = contract_rows(hidden_two, gate_up_grads).astype(jnp.bfloat16)
-    layer_partial = matmul(act, down_all).astype(jnp.bfloat16)
-    grad_middle, grad_gain_two, grad_branch, gate_up_share = back_to_middle(
-        contract_cols(gate_up_grads, gate_up_all).astype(jnp.bfloat16),
+    back_two = contract_cols(grad_gate, gate_all) + contract_cols(grad_up, up_all)
+    grad_middle, grad_gain_two, grad_branch, gate_up_share, down_grad, layer_part = back_to_middle(
+        back_two.astype(jnp.bfloat16),
         middle,
         gain_two,
         cotangent[0],
-        gate_up_grad,
+        hidden_two,
+        grad_gate,
+        grad_up,
+        act,
+        grad_out,
+        down_all,
         3,
     )
     grad_branch = grad_branch.reshape(length, width)
@@ -1537,7 +1711,7 @@
         cosine,
         sine,
         starts,
-        layer_partial,
+        layer_part,
         middle,
         down_grad,
         4,
@@ -1546,7 +1720,7 @@
     qkv_grad = jnp.einsum(
         "tm,ct->mc", hidden_one, qkv_grads, preferred_element_type=jnp.float32
     ).astype(jnp.bfloat16)
-    grad_inputs, grad_gain_one, qkv_share, heads_share = back_to_tokens(
+    grad_inputs, grad_gain_one, small_share = back_to_tokens(
         jnp.einsum("ct,mc->tm", qkv_grads, qkv_all, preferred_element_type=jnp.float32).astype(
             jnp.bfloat16
         ),
@@ -1558,7 +1732,7 @@
         5,
     )
     *gathered, gains = finish_grads(
-        gate_up_share, down_share, qkv_share, heads_share, grad_gain_one, grad_gain_two, 6
+        gate_up_share, down_share, small_share, grad_gain_one, grad_gain_two, 6
     )
     gate_grad, up_grad, down_total, query_grad, key_grad, value_grad, heads_total = place_grads(
         *gathered

time: 546 us -> 495 us (0.907)
  matrix products: 84.3 us -> 49.5 us
  Pallas kernels: 426 us -> 419 us
  local copies, waits for them, and re-layouts: 18 us -> 11 us
    dot_general x3 -> x1, matrix products: 22.5 us -> 1.31 us  [contract_rows(): jnp.einsum('ta,tb->ab', left, right, preferred_element_type=jnp.float32)]
    pallas_call x1, Pallas kernels: 55.6 us -> 39.8 us  [gather_first(): pl.pallas_call(kernel, out_shape=[jax.ShapeDtypeStruct((size, *block.shap...]
    dot_general x4 -> x3, matrix products: 30.7 us -> 16.6 us  [matmul(): return jnp.dot(left, right, preferred_element_type=jnp.float32)]
    pallas_call x1, Pallas kernels: 88.6 us -> 97 us  [back_to_middle(): pl.pallas_call(middle_kernel, out_shape=[jax.ShapeDtypeStruct((rows, widt...]
    pallas_call x1, Pallas kernels: 46.3 us -> 38.6 us  [attend_back(): pl.pallas_call(backward_kernel, out_shape=[jax.ShapeDtypeStruct(qkv.shape...]
    unnamed x52 -> x68, local copies, waits for them, and re-layouts: 17 us -> 9.97 us
    pallas_call x1, Pallas kernels: 65.9 us -> 71.7 us  [finish_grads(): pl.pallas_call(finish_kernel, out_shape=[jax.ShapeDtypeStruct((ranks, *bl...]
    dot_general x2 -> x3, matrix products: 20.7 us -> 21.2 us  [contract_cols(): jnp.einsum('ta,ba->tb', left, right, preferred_element_type=jnp.float32)]
where the time goes in v4:
time: 495 us; the launch traced here: 488 us
  Pallas kernels  419 us (85%)
  matrix products  49.5 us (10%)
  local copies, waits for them, and re-layouts  11 us (2%)
  other arithmetic  7.57 us (2%)
    pallas_call x1, Pallas kernels, back_to_middle(): pl.pallas_call(middle_kernel, out_shape=[jax.ShapeDtypeStruct((rows, widt...  97 us
    pallas_call x1, Pallas kernels, finish_grads(): pl.pallas_call(finish_kernel, out_shape=[jax.ShapeDtypeStruct((ranks, *bl...  71.7 us
    pallas_call x1, Pallas kernels, add_branch(): pl.pallas_call(branch_kernel, out_shape=[jax.ShapeDtypeStruct((rows, widt...  70 us
    pallas_call x1, Pallas kernels, attend(): pl.pallas_call(forward_kernel, out_shape=[jax.ShapeDtypeStruct((group * H...  53.4 us
    pallas_call x1, Pallas kernels, back_to_tokens(): pl.pallas_call(tokens_kernel, out_shape=[jax.ShapeDtypeStruct((rows, widt...  40.4 us
    pallas_call x1, Pallas kernels, gather_first(): pl.pallas_call(kernel, out_shape=[jax.ShapeDtypeStruct((size, *block.shap...  39.8 us
    pallas_call x1, Pallas kernels, attend_back(): pl.pallas_call(backward_kernel, out_shape=[jax.ShapeDtypeStruct(qkv.shape...  38.6 us
    dot_general x3, matrix products, contract_cols(): jnp.einsum('ta,ba->tb', left, right, preferred_element_type=jnp.float32)  21.2 us

profile of v4, /device:TPU:0, one launch (start us, length us, event | category | flops | bytes accessed | tf_op | source)
XLA Modules:
  0.0 488.4 jit_solution(15147052697943522748)
XLA Ops:
  0.7 0.9 compare_reduce_fusion
  2.3 1.2 multiply_sine_fusion
  3.5 1.6 copy-done.8
  5.1 1.6 copy-done.9
  6.7 1.0 copy-done.17
  7.8 0.9 copy-done.20
  8.7 0.9 copy-done.21
  10.9 1.1 pick_columns.1
  12.0 39.8 %gather_first.1 = (bf16[8,128,2048]{2,1,0:T(8,128)(2,1)S(1)}, bf16[16,160,384]{2,1,0:T(8,128)(2,1)S(1)}) custom-call(bf16[128,2048]{1,0:T(8,128)(2,1)S(1)} %bitcast.71, bf16[160,384]{1,0:T(8,128)(2,1)S(1)} %get-tuple-element.50.qkv), custom_call_target="tpu_custom_call" | custom-call | tf_op jit(solution)/shard_map/gather_first/pallas_call | solution.py:496
  51.9 0.9 multiply_reduce_fusion
  53.0 3.0 fusion.1
  56.1 1.0 multiply_convert_fusion
  57.1 1.8 convolution_convert_fusion.4.qkv.refs_0_
  59.0 53.4 %attend.1 = (bf16[256,1024]{1,0:T(8,128)(2,1)S(1)}, f32[4,8,1024]{2,1,0:T(8,128)S(1)}, bf16[256,1024]{1,0:T(8,128)(2,1)S(1)}, bf16[64,1024]{1,0:T(8,128)(2,1)S(1...) custom-call(bf16[384,1024]{1,0:T(8,128)(2,1)S(1)} %convolution_convert_f, ...), custom_call_target="tpu_custom_call" | custom-call | tf_op jit(solution)/shard_map/attend/pallas_call | solution.py:1386
  112.4 1.3 convolution_convert_fusion.1
  113.8 70.0 %add_branch.1 = (f32[128,2048]{1,0:T(8,128)S(1)}, bf16[8,128,2048]{2,1,0:T(8,128)(2,1)S(1)}, bf16[16,128,1024]{2,1,0:T(8,128)(2,1)S(1)}, bf16[16,64,2048]{2,1,0:T(8,128)(2,1)S(1)}) custom-call(bf16[8,128,2048]{2,1,0:T(8,128)(2,1)S(1)} %bitcast.70, bf16[128,2048]{1,0:T(8,128)(2,1)S(1)} %bitcast.72, f32[1,2048]{1,0:T(1,128)S(1)} %get-tuple-element.95.gain, ...), custom_call_target="tpu_custom_call" | custom-call | tf_op jit(solution)/shard_map/add_branch/pallas_call | solution.py:573
  183.8 6.1 %fusion.7 = f32[1024,1024]{1,0:T(8,128)} fusion(bf16[1024,2048]{1,0:T(8,128)(2,1)S(1)} %bitcast.75, bf16[1024,2048]{1,0:T(8,128)(2,1)S(1)} %bitcast.80), kind=kOutput, calls=%fused_computation.36 | convolution fusion | flops 4294967296 | bytes 12582912 | tf_op jit(solution)/shard_map/ta,ba->tb/dot_general | solution.py:1607
  190.0 6.0 %fusion.8 = f32[1024,1024]{1,0:T(8,128)} fusion(bf16[1024,2048]{1,0:T(8,128)(2,1)S(1)} %bitcast.77, bf16[2048,1024]{1,0:T(8,128)(2,1)S(1)} %bitcast.92), kind=kOutput, calls=%fused_computation.37 | convolution fusion | flops 4294967296 | bytes 12582912 | tf_op jit(solution)/shard_map/dot_general | solution.py:1611
  196.0 9.4 %multiply_convert_fusion.1 = (bf16[1024,1024]{1,0:T(8,128)(2,1)}, bf16[1024,1024]{1,0:T(8,128)(2,1)S(1)}, bf16[1024,1024]{1,0:T(8,128)(2,1)}) fusion(f32[1024,1024]{1,0:T(8,128)} %fusion.8, f32[1024,1024]{1,0:T(8,128)S(1)} %copy-done.32, bf16[1024,2048]{1,0:T(8,128)(2,1)S(1)} %bitcast.78, bf16[2048,1024]{1,0:T(8,128)(2,1)S(1)} %bitcast.94), kind=kOutput, calls=%fused_computation.6 | convolution fusion | flops 4310695936 | bytes 23068672 | tf_op jit(solution)/shard_map/dot_general | solution.py:1611
  205.3 6.8 %fusion.9 = f32[1024,2048]{1,0:T(8,128)} fusion(bf16[1024,1024]{1,0:T(8,128)(2,1)S(1)} %get-tuple-element.92.gate_grads, bf16[2048,1024]{1,0:T(8,128)(2,1)S(1)} %bitcast.93), kind=kOutput, calls=%fused_computation.38 | convolution fusion | flops 4294967296 | bytes 14680064 | tf_op jit(solution)/shard_map/ta,ba->tb/dot_general | solution.py:1607
  212.1 8.3 %add_convert_fusion = bf16[1024,2048]{1,0:T(8,128)(2,1)} fusion(f32[1024,2048]{1,0:T(8,128)} %fusion.9, bf16[1024,1024]{1,0:T(8,128)(2,1)S(1)} %copy-done.28, bf16[2048,1024]{1,0:T(8,128)(2,1)S(1)} %bitcast.95), kind=kOutput, calls=%fused_computation.3 | convolution fusion | flops 4299161600 | bytes 18874368 | tf_op jit(solution)/shard_map/ta,ba->tb/dot_general | solution.py:1607
  220.5 97.0 %back_to_middle.1 = (f32[128,2048]{1,0:T(8,128)}, f32[1,2048]{1,0:T(1,128)S(1)}, bf16[8,128,2048]{2,1,0:T(8,128)(2,1)}, bf16[128,2048]{1,0:T(8,128)(2,1)S(1)}, b...) custom-call(bf16[8,128,2048]{2,1,0:T(8,128)(2,1)} %bitcast.98, f32[128,2048]{1,0:T(8,128)} %copy-done.6, ...), custom_call_target="tpu_custom_call" | custom-call | tf_op jit(solution)/shard_map/back_to_middle/pallas_call | solution.py:776
  317.6 3.7 convolution_convert_fusion.5.refs_5_
  321.3 38.6 %attend_back.1 = (bf16[384,1024]{1,0:T(8,128)(2,1)S(1)}, bf16[128,2048]{1,0:T(8,128)(2,1)S(1)}, bf16[64,2048]{1,0:T(8,128)(2,1)S(1)}) custom-call(bf16[384,1024]{1,0:T(8,128)(2,1)S(1)} %convolution_convert_fusion.4.qkv.refs_0_, bf16[256,1024]{1,0:T(8,128)(2,1)S(1)} %copy-done.15, bf16[64,1024]{1,0:T(8,128)(2,1)S(1)} %copy-done.19, ...), custom_call_target="tpu_custom_call" | custom-call | tf_op jit(solution)/shard_map/attend_back/pallas_call | solution.py:1560
  359.9 1.3 convolution_convert_fusion.3
  361.2 0.9 copy-done.26
  362.1 2.4 convolution_convert_fusion.2
  364.6 2.4 convolution_convert_fusion
  367.0 40.4 %back_to_tokens.1 = (bf16[128,2048]{1,0:T(8,128)(2,1)S(1)}, f32[1,2048]{1,0:T(1,128)S(1)}, bf16[128,640]{1,0:T(8,128)(2,1)S(1)}) custom-call(bf16[8,128,2048]{2,1,0:T(8,128)(2,1)S(1)} %bitcast.74, bf16[128,2048]{1,0:T(8,128)(2,1)S(1)} %bitcast.73, f32[1,2048]{1,0:T(1,128)S(1)} %get-tuple-element.94.gain, f32[128,2048]{1,0:T(8,128)S(1)} %copy-done.11, ...), custom_call_target="tpu_custom_call" | custom-call | tf_op jit(solution)/shard_map/back_to_tokens/pallas_call | solution.py:917
  407.3 71.7 %finish_grads.1 = (bf16[8,128,2048]{2,1,0:T(8,128)(2,1)S(1)}, bf16[8,64,2048]{2,1,0:T(8,128)(2,1)S(1)}, bf16[8,128,640]{2,1,0:T(8,128)(2,1)S(1)}, f32[8,128]{1,0:T(8,128)S(1)}) custom-call(bf16[128,2048]{1,0:T(8,128)(2,1)S(1)} %get-tuple-element.73.gate_up, bf16[64,2048]{1,0:T(8,128)(2,1)S(1)} %get-tuple-element.74.down, ...), custom_call_target="tpu_custom_call" | custom-call | tf_op jit(solution)/shard_map/finish_grads/pallas_call | solution.py:1043
  479.6 7.1 %place_grads.1 = (f32[128,8192]{1,0:T(8,128)}, f32[128,8192]{1,0:T(8,128)}, f32[512,2048]{1,0:T(8,128)}, f32[128,2048]{1,0:T(8,128)}, f32[128,512]{1,0:T(8,128)}...) custom-call(bf16[8,128,2048]{2,1,0:T(8,128)(2,1)S(1)} %get-tuple-element.78.gate.up, ...), custom_call_target="tpu_custom_call" | custom-call | tf_op jit(solution)/shard_map/place_grads/pallas_call | solution.py:1118
  486.6 0.8 copy.26
  (73 shorter events, 3.7 us)
Async XLA Ops:
  0.6 2.8 copy-start
  0.7 11.4 %copy-start.2 = (bf16[1,128,2048]{2,1,0:T(8,128)(2,1)S(1)}, bf16[1,128,2048]{2,1,0:T(8,128)(2,1)}, u32[]{:S(2)}) copy-start(bf16[1,128,2048]{2,1,0:T(8,128)(2,1)} %param.13) | copy-start | bytes 1572868
  3.5 1.6 copy-start.8
  5.1 1.6 copy-start.9
  6.7 1.0 copy-start.17
  7.8 0.9 copy-start.20
  8.7 0.9 copy-start.21
  9.6 0.7 copy-start.22
  53.0 4.1 copy-start.29
  57.1 1.9 copy-start.10
  57.1 1.9 copy-start.16
  112.4 1.4 copy-start.12
  112.4 1.4 copy-start.14
  112.4 1.4 copy-start.18
  112.4 71.4 %copy-start.3 = (bf16[8,128,2048]{2,1,0:T(8,128)(2,1)}, bf16[8,128,2048]{2,1,0:T(8,128)(2,1)S(1)}, u32[]{:S(2)}) copy-start(bf16[8,128,2048]{2,1,0:T(8,128)(2,1)S(1)} %get-tuple-element.59) | copy-start | bytes 12582916
  183.8 6.2 %copy-start.5 = (bf16[16,64,2048]{2,1,0:T(8,128)(2,1)}, bf16[16,64,2048]{2,1,0:T(8,128)(2,1)S(1)}, u32[]{:S(2)}) copy-start(bf16[16,64,2048]{2,1,0:T(8,128)(2,1)S(1)} %get-tuple-element.61) | copy-start | bytes 12582916
  183.8 6.2 %copy-start.6 = (f32[128,2048]{1,0:T(8,128)}, f32[128,2048]{1,0:T(8,128)S(1)}, u32[]{:S(2)}) copy-start(f32[128,2048]{1,0:T(8,128)S(1)} %get-tuple-element.65.middle.refs_10_) | copy-start | bytes 3145732
  183.8 12.2 %copy-start.4 = (bf16[8,128,2048]{2,1,0:T(8,128)(2,1)}, bf16[8,128,2048]{2,1,0:T(8,128)(2,1)S(1)}, u32[]{:S(2)}) copy-start(bf16[8,128,2048]{2,1,0:T(8,128)(2,1)S(1)} %get-tuple-element.62) | copy-start | bytes 12582916
  183.8 12.2 %copy-start.24 = (bf16[16,128,1024]{2,1,0:T(8,128)(2,1)}, bf16[16,128,1024]{2,1,0:T(8,128)(2,1)S(1)}, u32[]{:S(2)}) copy-start(bf16[16,128,1024]{2,1,0:T(8,128)(2,1)S(1)} %get-tuple-element.63) | copy-start | bytes 12582916
  189.9 6.0 %copy-start.32 = (f32[1024,1024]{1,0:T(8,128)S(1)}, f32[1024,1024]{1,0:T(8,128)}, u32[]{:S(2)}) copy-start(f32[1024,1024]{1,0:T(8,128)} %fusion.7) | copy-start | bytes 12582916
  205.3 6.8 %copy-start.27 = (bf16[1024,1024]{1,0:T(8,128)(2,1)}, bf16[1024,1024]{1,0:T(8,128)(2,1)S(1)}, u32[]{:S(2)}) copy-start(bf16[1024,1024]{1,0:T(8,128)(2,1)S(1)} %get-tuple-element.92.gate_grads) | copy-start | bytes 6291460
  205.3 6.8 %copy-start.25 = (bf16[16,128,1024]{2,1,0:T(8,128)(2,1)S(1)}, bf16[16,128,1024]{2,1,0:T(8,128)(2,1)}, u32[]{:S(2)}) copy-start(bf16[16,128,1024]{2,1,0:T(8,128)(2,1)} %copy-done.24) | copy-start | bytes 12582916
  205.3 6.8 %copy-start.28 = (bf16[1024,1024]{1,0:T(8,128)(2,1)S(1)}, bf16[1024,1024]{1,0:T(8,128)(2,1)}, u32[]{:S(2)}) copy-start(bf16[1024,1024]{1,0:T(8,128)(2,1)} %get-tuple-element.93.up_grads) | copy-start | bytes 6291460
  220.5 97.1 %copy-start.13 = (bf16[2,128,2048]{2,1,0:T(8,128)(2,1)S(1)}, bf16[2,128,2048]{2,1,0:T(8,128)(2,1)}, u32[]{:S(2)}) copy-start(bf16[2,128,2048]{2,1,0:T(8,128)(2,1)} %copy-done.12) | copy-start | bytes 3145732
  317.5 3.8 copy-start.7
  317.5 3.8 copy-start.15
  317.5 3.8 copy-start.19
  321.3 38.6 %copy-start.31 = (bf16[8,128,2048]{2,1,0:T(8,128)(2,1)S(1)}, bf16[8,128,2048]{2,1,0:T(8,128)(2,1)}, u32[]{:S(2)}) copy-start(bf16[8,128,2048]{2,1,0:T(8,128)(2,1)} %get-tuple-element.66) | copy-start | bytes 12582916
  359.9 2.2 copy-start.26
  362.1 2.4 copy-start.30
  364.5 2.4 copy-start.11
  479.6 8.7 %copy-start.1 = (bf16[512,2048]{1,0:T(8,128)(2,1)S(1)}, bf16[512,2048]{1,0:T(8,128)(2,1)}, u32[]{:S(2)}) copy-start(bf16[512,2048]{1,0:T(8,128)(2,1)} %param.21) | copy-start | bytes 6291460
  (1 other events, 0.7 us)
